TPU v7x, 32 devices: a whole 2x2x4 slice. The times are simulated.
32 devices in a mesh: fsdp: 8 (over z, core), tp: 4 (over y, x).
Axes of the slice: x: 2, y: 2, z: 4, core: 2. Of those that a mesh axis runs over, the one named last changes fastest.
Arguments:
- tokens: bfloat16 [1024, 16384], P('fsdp', 'tp'), may hold values from -400 to 400
- norm_gain: bfloat16 [16384], P('tp'), may hold values from 0.5 to 1.5
- key_weight: bfloat16 [16384, 1024], P('fsdp', 'tp'), may hold values from -0.046875 to 0.046875
- value_weight: bfloat16 [16384, 1024], P('fsdp', 'tp'), may hold values from -0.046875 to 0.046875
Outputs:
- keys: bfloat16 [1024, 1024], P('fsdp', 'tp')
- values_out: bfloat16 [1024, 1024], P('fsdp', 'tp')
- hessian: float32 [16384, 16384], P('fsdp', 'tp')
All inputs are finite; a program needn't handle non-finite values.
Results may differ from a plain program's by a relative error of at most 0.0051.
Values may be sent and summed in bfloat16 or wider, within the bound.
No kernel may reach another device: no remote copies, remote signals or barrier semaphores. Data moves between devices by JAX's collectives and lax.ppermute only.
A program may use at most 192 MiB of HBM per device.

v0:
```python
import jax
import jax.numpy as jnp
from jax import lax
from jax.sharding import PartitionSpec as P

D = 16384


epsilon = 1e-05


def body(tokens, norm_gain, key_weight, value_weight):
    widened = tokens.astype(jnp.float32)
    partial_power = jnp.sum(widened * widened, axis=1)
    total_power = lax.psum(partial_power, "tp")
    inverse = lax.rsqrt(total_power / D + epsilon)
    normed = (widened * norm_gain.astype(jnp.float32)[None, :] * inverse[:, None]).astype(
        jnp.bfloat16
    )
    full_rows = lax.all_gather(normed, "tp", axis=1, tiled=True)
    key_part = jnp.dot(
        full_rows,
        lax.all_gather(key_weight, "fsdp", axis=0, tiled=True),
        preferred_element_type=jnp.float32,
    )
    value_part = jnp.dot(
        full_rows,
        lax.all_gather(value_weight, "fsdp", axis=0, tiled=True),
        preferred_element_type=jnp.float32,
    )
    keys = key_part.astype(jnp.bfloat16)
    values_out = value_part.astype(jnp.bfloat16)
    groups = lax.axis_size("fsdp")
    total_tokens = tokens.shape[0] * groups
    row_block = lax.all_to_all(full_rows, "fsdp", split_axis=1, concat_axis=0, tiled=True)
    tile = jnp.einsum(
        "tr,tc->rc",
        row_block,
        lax.all_gather(normed, "fsdp", axis=0, tiled=True),
        preferred_element_type=jnp.float32,
    )
    hessian = tile * (2.0 / total_tokens)
    return (keys, values_out, hessian)


def solution(mesh):
    placed = (P("fsdp", "tp"), P("tp"), P("fsdp", "tp"), P("fsdp", "tp"))
    return jax.shard_map(
        body,
        mesh=mesh,
        in_specs=placed,
        out_specs=(P("fsdp", "tp"), P("fsdp", "tp"), P("fsdp", "tp")),
        check_vma=False,
    )
```

profile of v0, /device:TPU:0, one launch (start us, length us, event | category | flops | bytes accessed | tf_op | source)
XLA Modules:
  0.0 430.8 jit_solution(3903034481684868536)
XLA Ops:
  7.2 0.0 all-gather.5.cloned.1.call-start
  7.2 0.7 convert_element_type.16
  7.9 1.6 copy.7
  9.5 0.6 fusion.2
  10.1 11.4 %psum.7 = f32[128]{0:T(128)S(1)} all-reduce(f32[128]{0:T(128)S(1)} %fusion.2), channel_id=1, replica_groups=mesh['fsdp'=8,'tp'=4] {'tp'}, use_global_device_ids=true, to_apply=%region_1.0 | all-reduce | flops 128 | bytes 1024 | tf_op jit(solution)/shard_map/psum | solution.py:15
  21.4 1.5 fusion.1
  22.9 0.0 all-gather.5.cloned.1.call-update
  23.0 0.0 all-gather.9.cloned.1.call-start
  23.0 0.7 all-gather.9.cloned.1.call-update
  23.7 0.0 all-gather.7.cloned.1.call-start
  23.8 0.7 all-gather.7.cloned.1.call-update
  24.4 0.0 all-gather.11.cloned.1.call-start
  24.5 0.5 all-gather.11.cloned.1.call-update
  25.0 50.2 %all-gather.5.cloned.1.call-done = bf16[128,16384]{0,1:T(8,128)(2,1)} async-done(((bf16[128,4096]{0,1:T(8,128)(2,1)}), bf16[128,16384]{0,1:T(8,128)(2,1)}) %all-gather.5.cloned.1.call-update) | async-done | bytes 4194320 | tf_op jit(solution)/shard_map/all_gather | solution.py:20
  75.2 166.1 %all_to_all.19 = bf16[128,8,2048]{0,2,1:T(8,128)(2,1)} all-to-all(bf16[128,8,2048]{0,2,1:T(8,128)(2,1)} %bitcast.9), channel_id=1, replica_groups=mesh['fsdp'=8,'tp'=4] {'fsdp'}, dimensions={1} | all-to-all | bytes 8388608 | tf_op jit(solution)/shard_map/all_to_all | solution.py:35
  241.3 6.6 %copy.8 = bf16[8,128,2048]{2,1,0:T(8,128)(2,1)} copy(bf16[8,128,2048]{1,2,0:T(8,128)(2,1)} %bitcast.10) | data formatting | bytes 8388608 | tf_op jit(solution)/shard_map/all_to_all | solution.py:35
  247.9 0.0 all-gather.9.cloned.1.call-done
  247.9 7.2 %convolution_convert_fusion = bf16[128,256]{1,0:T(8,128)(2,1)} fusion(bf16[128,16384]{0,1:T(8,128)(2,1)} %all-gather.5.cloned.1.call-done, bf16[16384,256]{1,0:T(8,128)(2,1)} %all-gather.9.cloned.1.call-done), kind=kOutput, calls=%fused_computation.6 | convolution fusion | flops 1073774592 | bytes 12648448 | tf_op jit(solution)/shard_map/dot_general | solution.py:26
  255.1 60.7 %all-gather.7.cloned.1.call-done = bf16[16384,256]{1,0:T(8,128)(2,1)} async-done(((bf16[2048,256]{1,0:T(8,128)(2,1)}), bf16[16384,256]{1,0:T(8,128)(2,1)}) %all-gather.7.cloned.1.call-update) | async-done | bytes 8388624 | tf_op jit(solution)/shard_map/all_gather | solution.py:23
  315.7 7.1 %convolution_convert_fusion.1 = bf16[128,256]{1,0:T(8,128)(2,1)} fusion(bf16[128,16384]{0,1:T(8,128)(2,1)} %all-gather.5.cloned.1.call-done, bf16[16384,256]{1,0:T(8,128)(2,1)} %all-gather.7.cloned.1.call-done), kind=kOutput, calls=%fused_computation.7 | convolution fusion | flops 1073774592 | bytes 12648448 | tf_op jit(solution)/shard_map/dot_general | solution.py:21
  322.8 76.0 %all-gather.11.cloned.1.call-done = bf16[1024,4096]{0,1:T(8,128)(2,1)} async-done(((bf16[128,4096]{0,1:T(8,128)(2,1)}), bf16[1024,4096]{0,1:T(8,128)(2,1)}) %all-gather.11.cloned.1.call-update) | async-done | bytes 8388624 | tf_op jit(solution)/shard_map/all_gather | solution.py:39
  398.8 25.4 %convolution_multiply_fusion = f32[2048,4096]{1,0:T(8,128)} fusion(bf16[1024,2048]{1,0:T(8,128)(2,1)} %bitcast.11, bf16[1024,4096]{0,1:T(8,128)(2,1)} %all-gather.11.cloned.1.call-done), kind=kOutput, calls=%fused_computation | convolution fusion | flops 17188257792 | bytes 46137344 | tf_op jit(solution)/shard_map/tr,tc->rc/dot_general | solution.py:36
  (1 shorter events, 0.0 us)
Async XLA Ops:
  7.2 68.0 %all-gather.5.cloned.1.call-start = ((), (), s32[]{:S(2)}) async-start(), calls=%async_computation.1 | async-start | bytes 5242880 | tf_op jit(solution)/shard_map/all_gather | solution.py:20
  23.0 224.9 %all-gather.9.cloned.1.call-start = ((), (), s32[]{:S(2)}) async-start(), calls=%async_computation.3 | async-start | bytes 9437184 | tf_op jit(solution)/shard_map/all_gather | solution.py:28
  23.7 292.0 %all-gather.7.cloned.1.call-start = ((), (), s32[]{:S(2)}) async-start(), calls=%async_computation.2 | async-start | bytes 9437184 | tf_op jit(solution)/shard_map/all_gather | solution.py:23
  24.4 374.4 %all-gather.11.cloned.1.call-start = ((), (), s32[]{:S(2)}) async-start(), calls=%async_computation.4 | async-start | bytes 9437184 | tf_op jit(solution)/shard_map/all_gather | solution.py:39
Sparse Core Ops, SparseCore 0:
  23.1 52.0 all-gather.4
  76.8 157.2 all-gather.8
  235.7 79.9 all-gather.6
  317.7 81.0 all-gather.10
where the time goes:
time: 431 us
  waiting for transfers between devices  189 us (44%)
  blocking collectives  177 us (41%)
  matrix products  39.7 us (9%)
  between operations  13.8 us (3%)
  local copies, waits for them, and re-layouts  8.18 us (2%)
    all_to_all x1, blocking collectives, body(): lax.all_to_all(full_rows, 'fsdp', split_axis=1, concat_axis=0, tiled=True)  166 us
    all_gather x1, waiting for transfers between devices, body(): lax.all_gather(normed, 'fsdp', axis=0, tiled=True)  76 us
    all_gather x1, waiting for transfers between devices, body(): lax.all_gather(key_weight, 'fsdp', axis=0, tiled=True)  60.7 us
    all_gather x1, waiting for transfers between devices, body(): full_rows = lax.all_gather(normed, 'tp', axis=1, tiled=True)  50.2 us
    dot_general x1, matrix products, body(): jnp.einsum('tr,tc->rc', row_block, lax.all_gather(normed, 'fsdp', axis=0,...  25.4 us
    psum x1, blocking collectives, body(): total_power = lax.psum(partial_power, 'tp')  11.4 us
  transfers between devices with their start and end apart: 4, of which 3 were waited for; matrix products, arithmetic and copies ran while one was open for 5% of the time, Pallas kernels for 0%

commit v1 on v0

v1 whole, which is shorter than its diff:
```python
import functools

import jax
import jax.numpy as jnp
from jax import lax
from jax.experimental import pallas as pl
from jax.experimental.pallas import tpu as pltpu
from jax.sharding import PartitionSpec as P

epsilon = 1e-05
BOTH = ("fsdp", "tp")

LANES = range(2)
NEAR = [(z * 2 + c, (z ^ 1) * 2 + c) for z in range(4) for c in LANES]
MIDDLE = [(z * 2 + c, (3 - z) * 2 + c) for z in (1, 2) for c in LANES]
OUTWARD = [(2 + c, c) for c in LANES] + [(4 + c, 6 + c) for c in LANES]
CORES = [(f, f ^ 1) for f in range(8)]
HOME_TWO = [(c, 4 + c) for c in LANES] + [(6 + c, 2 + c) for c in LANES]
HOME_TWO_BACK = [(2 + c, 6 + c) for c in LANES] + [(4 + c, c) for c in LANES]
HOME_THREE = [(c, 6 + c) for c in LANES] + [(6 + c, c) for c in LANES]


def plane(start, end, depths=range(4)):
    return [
        ((z * 2 + c) * 4 + (z ^ start), (z * 2 + c) * 4 + (z ^ end))
        for z in depths
        for c in LANES
    ]


def tile_kernel(scale, slots, *refs):
    rows, cols, out = refs[:slots], refs[slots : 2 * slots], refs[2 * slots]
    turned = [row[...].T for row in rows]
    width = out.shape[1]
    step = min(width, 1024)
    for left in range(0, width, step):
        total = None
        for row, col in zip(turned, cols):
            product = jnp.dot(
                row, col[:, left : left + step], preferred_element_type=jnp.float32
            )
            total = product if total is None else total + product
        out[:, left : left + step] = total * scale


def hessian_tile(rows, cols, scale):
    slots = len(rows)
    depth, height = rows[0].shape
    width = cols[0].shape[1]
    block = 256
    flops = 2 * slots * depth * height * width
    return pl.pallas_call(
        functools.partial(tile_kernel, scale, slots),
        grid=(height // block,),
        in_specs=[pl.BlockSpec((depth, block), lambda i: (0, i))] * slots
        + [pl.BlockSpec((depth, width), lambda i: (0, 0), pipeline_mode=pl.Buffered(1))] * slots,
        out_specs=pl.BlockSpec((block, width), lambda i: (i, 0)),
        out_shape=jax.ShapeDtypeStruct((height, width), jnp.float32),
        compiler_params=pltpu.CompilerParams(vmem_limit_bytes=40 << 20),
        cost_estimate=pl.CostEstimate(
            flops=flops, bytes_accessed=4 * height * width, transcendentals=0
        ),
    )(*rows, *cols)


def slice_body(tokens, norm_gain, key_weight, value_weight):
    count, width = tokens.shape
    features = width * lax.axis_size("tp")
    half = width // 2
    total_tokens = count * 8
    f, t = lax.axis_index("fsdp"), lax.axis_index("tp")
    z, core = f // 2, f % 2
    role = z ^ t
    middle = (z == 1) | (z == 2)

    def move(x, pairs, axis="fsdp"):
        return lax.ppermute(x, axis, pairs)

    near = move(tokens, NEAR)
    across = move(tokens, MIDDLE)
    own_twin = move(tokens, CORES)

    widened = tokens.astype(jnp.float32)
    partial_power = jnp.sum(widened * widened, axis=1)
    note = jnp.concatenate([partial_power, norm_gain.astype(jnp.float32)])
    notes = lax.all_gather(note, "tp")
    power = jnp.sum(notes[:, :count], axis=0)
    inverse = lax.all_gather(lax.rsqrt(power / features + epsilon), "fsdp")
    row_gain = lax.dynamic_slice(notes, (z, count + core * half), (1, half))
    col_gain = norm_gain.astype(jnp.float32)[None, :]

    outer = move(across, OUTWARD)
    beyond = move(near, MIDDLE)
    last = move(beyond, OUTWARD)
    second = jnp.where(middle, across, outer)
    third = jnp.where(middle, beyond, last)

    def my_half(block):
        return lax.dynamic_slice(block, (0, core * half), (count, half))

    def pick(at_root, at_x, at_y, at_far):
        return jnp.where(
            role == 0, at_root, jnp.where(role == 1, at_x, jnp.where(role == 2, at_y, at_far))
        )

    def spread(block, twin, direct):
        mine, other = my_half(block), my_half(twin)
        mine_x = move(mine, plane(0, 1), BOTH)
        other_y = move(other, plane(0, 2), BOTH)
        mine_far = move(mine_x, plane(1, 3), BOTH)
        other_far = move(other_y, plane(2, 3), BOTH)
        if direct:
            mine_y = move(mine, plane(0, 2), BOTH)
            other_x = move(other, plane(0, 1), BOTH)
        else:
            mine_y = move(mine_far, plane(3, 2), BOTH)
            other_x = move(other_far, plane(3, 1), BOTH)
        return pick(mine, mine_x, mine_y, mine_far), pick(other, other_x, other_y, other_far)

    def norm(block, gain, group):
        scale = lax.dynamic_slice(inverse, (group, 0), (1, count))[0]
        return (block.astype(jnp.float32) * gain * scale[:, None]).astype(jnp.bfloat16)

    sources = (
        (tokens, own_twin, z, False),
        (near, move(near, CORES), z ^ 1, False),
        (second, move(second, CORES), jnp.where(z < 2, 2, 1), True),
        (third, move(third, CORES), jnp.where(z < 2, 3, 0), True),
    )
    rows, cols = [], []
    for block, twin, group, direct in sources:
        mine, other = group * 2 + core, group * 2 + 1 - core
        cols.append(
            jnp.concatenate([norm(block, col_gain, mine), norm(twin, col_gain, other)])
        )
        row_block, row_twin = spread(block, twin, direct)
        rows.append(
            jnp.concatenate([norm(row_block, row_gain, mine), norm(row_twin, row_gain, other)])
        )

    weights = jnp.concatenate([key_weight, value_weight], axis=1)
    parts = [jnp.dot(row, weights, preferred_element_type=jnp.float32) for row in rows]
    sums = [part[:count] + move(part[count:], CORES) for part in parts]
    projected = (
        sums[0]
        + move(sums[1], NEAR)
        + move(sums[2], MIDDLE)
        + move(sums[2], HOME_TWO)
        + move(sums[3], HOME_TWO_BACK)
        + move(sums[3], HOME_THREE)
    ).astype(jnp.bfloat16)
    columns = key_weight.shape[1]
    hessian = hessian_tile(rows, cols, 2.0 / total_tokens)
    return projected[:, :columns], projected[:, columns:], hessian


def general_body(tokens, norm_gain, key_weight, value_weight):
    features = tokens.shape[1] * lax.axis_size("tp")
    total_tokens = tokens.shape[0] * lax.axis_size("fsdp")
    widened = tokens.astype(jnp.float32)
    power = lax.psum(jnp.sum(widened * widened, axis=1), "tp")
    inverse = lax.rsqrt(power / features + epsilon)
    normed = (widened * norm_gain.astype(jnp.float32)[None, :] * inverse[:, None]).astype(
        jnp.bfloat16
    )
    cols = lax.all_gather(normed, "fsdp", axis=0, tiled=True)
    full_rows = lax.all_gather(normed, "tp", axis=1, tiled=True)
    rows = lax.all_to_all(full_rows, "fsdp", split_axis=1, concat_axis=0, tiled=True)
    weights = jnp.concatenate([key_weight, value_weight], axis=1)
    part = jnp.dot(rows, weights, preferred_element_type=jnp.float32)
    projected = lax.psum_scatter(part, "fsdp", scatter_dimension=0, tiled=True).astype(jnp.bfloat16)
    columns = key_weight.shape[1]
    hessian = hessian_tile([rows], [cols], 2.0 / total_tokens)
    return projected[:, :columns], projected[:, columns:], hessian


def solution(mesh):
    small = mesh.shape["fsdp"] == 8 and mesh.shape["tp"] == 4
    placed = (P("fsdp", "tp"), P("tp"), P("fsdp", "tp"), P("fsdp", "tp"))
    return jax.shard_map(
        slice_body if small else general_body,
        mesh=mesh,
        in_specs=placed,
        out_specs=(P("fsdp", "tp"), P("fsdp", "tp"), P("fsdp", "tp")),
        check_vma=False,
    )
```

time: 431 us -> 209 us (0.48)
  blocking collectives: 177 us -> 22.4 us
  waiting for transfers between devices: 189 us -> 45.8 us
  starting transfers between devices: 0.16 us -> 90 us
  matrix products: 39.7 us -> 2.8 us
  Pallas kernels: 0 us -> 21.6 us
  between operations: 13.8 us -> 1.46 us
  other arithmetic: 2.75 us -> 13.6 us
    all_gather x4 -> x0, waiting for transfers between devices: 187 us -> none  [the longest x1 76 us: body(): lax.all_gather(normed, 'fsdp', axis=0, tiled=True)]
    all_to_all x1 -> x0, blocking collectives: 166 us -> none  [body(): lax.all_to_all(full_rows, 'fsdp', split_axis=1, concat_axis=0, tiled=True)]
    ppermute x0 -> x42, starting transfers between devices: none -> 90 us  [move(): return lax.ppermute(x, axis, pairs)]
    ppermute x0 -> x42, waiting for transfers between devices: none -> 45.8 us  [move(): return lax.ppermute(x, axis, pairs)]
    dot_general x3 -> x4, matrix products: 39.7 us -> 2.8 us  [slice_body(): jnp.dot(row, weights, preferred_element_type=jnp.float32)]
    all_gather x0 -> x2, blocking collectives: none -> 22.4 us  [the longest x1 13.9 us: slice_body(): inverse = lax.all_gather(lax.rsqrt(power / features + epsilon), 'fsdp')]
    pallas_call x0 -> x1, Pallas kernels: none -> 21.6 us  [hessian_tile(): pl.pallas_call(functools.partial(tile_kernel, scale, slots), grid=(height...]
    psum x1 -> x0, blocking collectives: 11.4 us -> none  [body(): total_power = lax.psum(partial_power, 'tp')]
  transfers between devices with their start and end apart: 4 -> 42, of which waited for: 3 -> 5; matrix products, arithmetic and copies ran while one was open for 5% -> 12% of each run, Pallas kernels for 0% -> 10%
where the time goes in v1:
time: 209 us; the launch traced here: 206 us
  starting transfers between devices  90 us (43%)
  waiting for transfers between devices  45.8 us (22%)
  blocking collectives  22.4 us (11%)
  Pallas kernels  21.6 us (10%)
  other arithmetic  13.6 us (7%)
  local copies, waits for them, and re-layouts  8.39 us (4%)
  matrix products  2.8 us (1%)
    ppermute x42, starting transfers between devices, move(): return lax.ppermute(x, axis, pairs)  90 us
    ppermute x42, waiting for transfers between devices, move(): return lax.ppermute(x, axis, pairs)  45.8 us
    pallas_call x1, Pallas kernels, hessian_tile(): pl.pallas_call(functools.partial(tile_kernel, scale, slots), grid=(height...  21.6 us
    all_gather x1, blocking collectives, slice_body(): inverse = lax.all_gather(lax.rsqrt(power / features + epsilon), 'fsdp')  13.9 us
    convert_element_type x6, other arithmetic, norm(): (block.astype(jnp.float32) * gain * scale[:, None]).astype(jnp.bfloat16)  9.84 us
    all_gather x1, blocking collectives, slice_body(): notes = lax.all_gather(note, 'tp')  8.42 us
  transfers between devices with their start and end apart: 42, of which 5 were waited for; matrix products, arithmetic and copies ran while one was open for 12% of the time, Pallas kernels for 10%

profile of v1, /device:TPU:0, one launch (start us, length us, event | category | flops | bytes accessed | tf_op | source)
XLA Modules:
  0.0 206.0 jit_solution(12629366738739770090)
XLA Ops:
  0.6 3.1 %collective-permute-start.8 = (bf16[128,4096]{1,0:T(8,128)(2,1)}, bf16[128,4096]{1,0:T(8,128)(2,1)S(1)}, u32[]{:S(2)}, u32[]{:S(2)}) collective-permute-start(bf16[128,4096]{1,0:T(8,128)(2,1)} %param.4), channel_id=1, source_target_pairs={{0,8},{4,12},{8,0},{12,4},{16,24},{20,28},{24,16},{28,20},{1,9},{5... | collective-permute-start | bytes 3145736 | tf_op jit(solution)/shard_map/ppermute | solution.py:77
  3.7 1.1 constant_dynamic-slice_fusion.16
  4.8 3.4 %collective-permute-start = (bf16[128,2048]{1,0:T(8,128)(2,1)S(1)}, bf16[128,2048]{1,0:T(8,128)(2,1)S(1)}, u32[]{:S(2)}, u32[]{:S(2)}) collective-permute-start(bf16[128,2048]{1,0:T(8,128)(2,1)S(1)} %constant_dynamic-slice_fusion.16), channel_id=1, source_target_pairs={{0,1},{4,5},{9,8},{13,12},{18,19},{22,23},{27,26},{31,30}} | collective-permute-start | bytes 1572872 | tf_op jit(solution)/shard_map/ppermute | solution.py:77
  8.3 1.7 collective-permute-start.18
  9.9 0.7 convert_element_type.106
  10.6 16.4 %collective-permute-done.8 = bf16[128,4096]{1,0:T(8,128)(2,1)S(1)} collective-permute-done((bf16[128,4096]{1,0:T(8,128)(2,1)}, bf16[128,4096]{1,0:T(8,128)(2,1)S(1)}, u32[]{:S(2)}, u32[]{:S(2)}) %collective-permute-start.8) | collective-permute-done | bytes 1048608 | tf_op jit(solution)/shard_map/ppermute | solution.py:77
  27.1 1.7 collective-permute-start.30
  28.7 1.5 fusion
  30.3 8.4 %all-gather.2 = f32[4,1,4224]{2,1,0:T(1,128)S(1)} all-gather(f32[1,1,4224]{2,1,0:T(1,128)S(1)} %reshape.35), channel_id=2, replica_groups=mesh['fsdp'=8,'tp'=4] {'tp'}, dimensions={0}, use_global_device_ids=true | all-gather | bytes 84480 | tf_op jit(solution)/shard_map/all_gather | solution.py:86
  38.8 1.5 collective-permute-start.1
  40.2 0.9 constant_dynamic-slice_fusion.14
  41.1 4.2 %collective-permute-start.4 = (bf16[128,2048]{1,0:T(8,128)(2,1)}, bf16[128,2048]{1,0:T(8,128)(2,1)}, u32[]{:S(2)}, u32[]{:S(2)}) collective-permute-start(bf16[128,2048]{1,0:T(8,128)(2,1)} %constant_dynamic-slice_fusion.14), channel_id=1, source_target_pairs={{0,2},{4,6},{9,11},{13,15},{18,16},{22,20},{27,25},{31,29}} | collective-permute-start | bytes 1572872 | tf_op jit(solution)/shard_map/ppermute | solution.py:77
  45.3 0.9 constant_dynamic-slice_fusion.12
  46.2 3.3 %collective-permute-start.9 = (bf16[128,2048]{1,0:T(8,128)(2,1)}, bf16[128,2048]{1,0:T(8,128)(2,1)}, u32[]{:S(2)}, u32[]{:S(2)}) collective-permute-start(bf16[128,2048]{1,0:T(8,128)(2,1)} %constant_dynamic-slice_fusion.12), channel_id=1, source_target_pairs={{0,1},{4,5},{9,8},{13,12},{18,19},{22,23},{27,26},{31,30}} | collective-permute-start | bytes 1572872 | tf_op jit(solution)/shard_map/ppermute | solution.py:77
  49.5 13.9 %all-gather.3 = f32[8,1,128]{2,1,0:T(1,128)S(1)} all-gather(f32[1,1,128]{2,1,0:T(1,128)S(1)} %rsqrt_bitcast_fusion), channel_id=3, replica_groups=mesh['fsdp'=8,'tp'=4] {'fsdp'}, dimensions={0}, use_global_device_ids=true | all-gather | bytes 4608 | tf_op jit(solution)/shard_map/all_gather | solution.py:88
  63.5 1.3 collective-permute-start.31
  64.8 2.3 %constant_dynamic-update-slice_fusion.1 = bf16[2048,512]{1,0:T(8,128)(2,1)} fusion(bf16[2048,256]{1,0:T(8,128)(2,1)} %param.6), kind=kLoop, calls=%fused_computation.43 | loop fusion | bytes 2097152
  67.1 1.5 collective-permute-start.5
  68.5 1.5 collective-permute-start.10
  70.0 2.3 %constant_dynamic-update-slice_fusion = bf16[2048,512]{1,0:T(8,128)(2,1)} fusion(bf16[2048,512]{1,0:T(8,128)(2,1)} %constant_dynamic-update-slice_fusion.1, bf16[2048,256]{1,0:T(8,128)(2,1)} %param.7), kind=kLoop, calls=%fused_computation.42 | loop fusion | bytes 2097152 | tf_op jit(solution)/shard_map/concatenate | solution.py:141
  73.0 1.3 collective-permute-start.19
  74.3 10.0 %collective-permute-start.13 = (bf16[128,2048]{1,0:T(8,128)(2,1)S(1)}, bf16[128,2048]{1,0:T(8,128)(2,1)S(1)}, u32[]{:S(2)}, u32[]{:S(2)}) collective-permute-start(bf16[128,2048]{1,0:T(8,128)(2,1)S(1)} %constant_dynamic-slice_fusion.10), channel_id=1, source_target_pairs={{0,2},{4,6},{9,11},{13,15},{18,16},{22,20},{27,25},{31,29}} | collective-permute-start | bytes 1572872 | tf_op jit(solution)/shard_map/ppermute | solution.py:77
  85.1 6.6 %collective-permute-done.31 = bf16[128,4096]{1,0:T(8,128)(2,1)} collective-permute-done((bf16[128,4096]{1,0:T(8,128)(2,1)}, bf16[128,4096]{1,0:T(8,128)(2,1)}, u32[]{:S(2)}, u32[]{:S(2)}) %collective-permute-start.31) | collective-permute-done | bytes 1048608 | tf_op jit(solution)/shard_map/ppermute | solution.py:77
  92.4 1.8 multiply_convert_fusion.1
  94.4 3.0 %multiply_convert_fusion.14 = (bf16[128,2048]{1,0:T(8,128)(2,1)S(1)}, bf16[128,2048]{1,0:T(8,128)(2,1)S(1)}, bf16[128,2048]{1,0:T(8,128)(2,1)S(1)}) fusion(f32[128]{0:T(128)S(1)} %get-tuple-element.24, f32[2048]{0:T(1024)S(1)} %bitcast.26, bf16[128,2048]{1,0:T(8,128)(2,1)S(1)} %copy-done.2, bf16[128,2048]{1,0:T(8,128)(2,1)S(1)} %collective-permute-done.2, ...), kind=kLoop, calls=%fused_computation.27 | loop fusion | flops 5505024 | bytes 7874055 | tf_op jit(solution)/shard_map/convert_element_type | solution.py:122
  97.4 6.8 %collective-permute-start.32 = (bf16[128,2048]{1,0:T(8,128)(2,1)S(1)}, bf16[128,2048]{1,0:T(8,128)(2,1)S(1)}, u32[]{:S(2)}, u32[]{:S(2)}) collective-permute-start(bf16[128,2048]{1,0:T(8,128)(2,1)S(1)} %constant_dynamic-slice_fusion.4), channel_id=1, source_target_pairs={{0,1},{4,5},{9,8},{13,12},{18,19},{22,23},{27,26},{31,30}} | collective-permute-start | bytes 1572872 | tf_op jit(solution)/shard_map/ppermute | solution.py:77
  104.2 0.7 fusion.20
  105.7 10.7 %collective-permute-start.33 = (bf16[128,2048]{1,0:T(8,128)(2,1)S(1)}, bf16[128,2048]{1,0:T(8,128)(2,1)S(1)}, u32[]{:S(2)}, u32[]{:S(2)}) collective-permute-start(bf16[128,2048]{1,0:T(8,128)(2,1)S(1)} %constant_dynamic-slice_fusion.4), channel_id=1, source_target_pairs={{0,2},{4,6},{9,11},{13,15},{18,16},{22,20},{27,25},{31,29}} | collective-permute-start | bytes 1572872 | tf_op jit(solution)/shard_map/ppermute | solution.py:77
  117.2 1.3 collective-permute-start.37
  118.6 2.7 %collective-permute-start.36 = (bf16[128,2048]{1,0:T(8,128)(2,1)S(1)}, bf16[128,2048]{1,0:T(8,128)(2,1)S(1)}, u32[]{:S(2)}, u32[]{:S(2)}) collective-permute-start(bf16[128,2048]{1,0:T(8,128)(2,1)S(1)} %constant_dynamic-slice_fusion.2), channel_id=1, source_target_pairs={{0,1},{4,5},{9,8},{13,12},{18,19},{22,23},{27,26},{31,30}} | collective-permute-start | bytes 1572872 | tf_op jit(solution)/shard_map/ppermute | solution.py:77
  121.2 2.4 %multiply_convert_fusion = (bf16[128,4096]{1,0:T(8,128)(2,1)S(1)}, bf16[128,4096]{1,0:T(8,128)(2,1)S(1)}, bf16[128,4096]{1,0:T(8,128)(2,1)S(1)}, bf16[128,4096]{...) fusion(bf16[128,4096]{1,0:T(8,128)(2,1)S(1)} %collective-permut, ...), kind=kLoop, calls=%fused_computation.9 | loop fusion | flops 13107200 | bytes 14699521 | tf_op jit(solution)/shard_map/convert_element_type | solution.py:122
  123.7 1.3 collective-permute-start.20
  125.0 11.6 %collective-permute-done.37 = bf16[128,2048]{1,0:T(8,128)(2,1)S(1)} collective-permute-done((bf16[128,2048]{1,0:T(8,128)(2,1)S(1)}, bf16[128,2048]{1,0:T(8,128)(2,1)S(1)}, u32[]{:S(2)}, u32[]{:S(2)}) %collective-permute-start.37) | collective-permute-done | bytes 524320 | tf_op jit(solution)/shard_map/ppermute | solution.py:77
  138.8 5.0 %collective-permute-start.21 = (bf16[128,2048]{1,0:T(8,128)(2,1)S(1)}, bf16[128,2048]{1,0:T(8,128)(2,1)S(1)}, u32[]{:S(2)}, u32[]{:S(2)}) collective-permute-start(bf16[128,2048]{1,0:T(8,128)(2,1)S(1)} %constant_dynamic-slice_fusion.8), channel_id=1, source_target_pairs={{0,2},{4,6},{9,11},{13,15},{18,16},{22,20},{27,25},{31,29}} | collective-permute-start | bytes 1572872 | tf_op jit(solution)/shard_map/ppermute | solution.py:77
  144.6 0.8 multiply_convert_fusion.8
  145.5 0.7 fusion.17
  146.9 5.6 %collective-permute-start.25 = (bf16[128,2048]{1,0:T(8,128)(2,1)S(1)}, bf16[128,2048]{1,0:T(8,128)(2,1)S(1)}, u32[]{:S(2)}, u32[]{:S(2)}) collective-permute-start(bf16[128,2048]{1,0:T(8,128)(2,1)S(1)} %constant_dynamic-slice_fusion.6), channel_id=1, source_target_pairs={{0,2},{4,6},{9,11},{13,15},{18,16},{22,20},{27,25},{31,29}} | collective-permute-start | bytes 1572872 | tf_op jit(solution)/shard_map/ppermute | solution.py:77
  152.8 1.3 collective-permute-start.24
  154.1 10.2 %collective-permute-done.25 = bf16[128,2048]{1,0:T(8,128)(2,1)S(1)} collective-permute-done((bf16[128,2048]{1,0:T(8,128)(2,1)S(1)}, bf16[128,2048]{1,0:T(8,128)(2,1)S(1)}, u32[]{:S(2)}, u32[]{:S(2)}) %collective-permute-start.25) | collective-permute-done | bytes 524320 | tf_op jit(solution)/shard_map/ppermute | solution.py:77
  165.4 1.9 collective-permute-start.41
  167.3 1.5 collective-permute-start.40
  168.8 1.5 multiply_convert_fusion.11
  170.3 0.7 fusion.19
  171.1 0.7 fusion.18
  172.6 0.9 collective-permute-done.27
  173.5 8.0 %collective-permute-start.29 = (f32[128,512]{1,0:T(8,128)S(1)}, f32[128,512]{1,0:T(8,128)S(1)}, u32[]{:S(2)}, u32[]{:S(2)}) collective-permute-start(f32[128,512]{1,0:T(8,128)S(1)} %slice_add_fusion.1), channel_id=1, source_target_pairs={{0,16},{4,20},{24,8},{28,12},{1,17},{5,21},{25,9},{29,13},{2,18},{... | collective-permute-start | bytes 786440 | tf_op jit(solution)/shard_map/ppermute | solution.py:77
  182.3 1.2 collective-permute-start.17
  183.5 21.6 %shard_map.67 = f32[2048,4096]{1,0:T(8,128)} custom-call(bf16[256,2048]{1,0:T(8,128)(2,1)S(1)} %pad_maximum_fusion.4.refs_0_, bf16[256,2048]{1,0:T(8,128)(2,1)S(1)} %get-tuple-element.34.refs_1_, bf16[256,2048]{1,0:T(8,128)(2,1)S(1)} %get-tuple-element.35.refs_2_, bf16[256,2048]{1,0:T(8,128)(2,1)S(1)} %pad_maximum_fusion.7.refs_3_, ...), custom_call_target="tpu_custom_call" | custom-call | flops 17179869184 | bytes 33554432 | tf_op jit(solution)/shard_map/pallas_call | solution.py:52
  (91 shorter events, 11.2 us)
Async XLA Ops:
  0.6 26.5 %collective-permute-start.8 = (bf16[128,4096]{1,0:T(8,128)(2,1)}, bf16[128,4096]{1,0:T(8,128)(2,1)S(1)}, u32[]{:S(2)}, u32[]{:S(2)}) collective-permute-start(bf16[128,4096]{1,0:T(8,128)(2,1)} %param.4), channel_id=1, source_target_pairs={{0,8},{4,12},{8,0},{12,4},{16,24},{20,28},{24,16},{28,20},{1,9},{5... | collective-permute-start | bytes 3145736 | tf_op jit(solution)/shard_map/ppermute | solution.py:77
  3.7 36.5 %collective-permute-start.3 = (bf16[128,4096]{1,0:T(8,128)(2,1)}, bf16[128,4096]{1,0:T(8,128)(2,1)S(1)}, u32[]{:S(2)}, u32[]{:S(2)}) collective-permute-start(bf16[128,4096]{1,0:T(8,128)(2,1)} %param.4), channel_id=1, source_target_pairs={{0,4},{4,0},{8,12},{12,8},{16,20},{20,16},{24,28},{28,24},{1,5},{5... | collective-permute-start | bytes 3145736 | tf_op jit(solution)/shard_map/ppermute | solution.py:77
  4.8 33.9 %collective-permute-start = (bf16[128,2048]{1,0:T(8,128)(2,1)S(1)}, bf16[128,2048]{1,0:T(8,128)(2,1)S(1)}, u32[]{:S(2)}, u32[]{:S(2)}) collective-permute-start(bf16[128,2048]{1,0:T(8,128)(2,1)S(1)} %constant_dynamic-slice_fusion.16), channel_id=1, source_target_pairs={{0,1},{4,5},{9,8},{13,12},{18,19},{22,23},{27,26},{31,30}} | collective-permute-start | bytes 1572872 | tf_op jit(solution)/shard_map/ppermute | solution.py:77
  8.3 64.0 %collective-permute-start.18 = (bf16[128,4096]{1,0:T(8,128)(2,1)}, bf16[128,4096]{1,0:T(8,128)(2,1)}, u32[]{:S(2)}, u32[]{:S(2)}) collective-permute-start(bf16[128,4096]{1,0:T(8,128)(2,1)} %param.4), channel_id=1, source_target_pairs={{8,16},{12,20},{16,8},{20,12},{9,17},{13,21},{17,9},{21,13},{10,18... | collective-permute-start | bytes 3145736 | tf_op jit(solution)/shard_map/ppermute | solution.py:77
  27.1 36.4 %collective-permute-start.30 = (bf16[128,4096]{1,0:T(8,128)(2,1)S(1)}, bf16[128,4096]{1,0:T(8,128)(2,1)}, u32[]{:S(2)}, u32[]{:S(2)}) collective-permute-start(bf16[128,4096]{1,0:T(8,128)(2,1)S(1)} %collective-permute-done.8), channel_id=1, source_target_pairs={{8,16},{12,20},{16,8},{20,12},{9,17},{13,21},{17,9},{21,13},{10,18... | collective-permute-start | bytes 3145736 | tf_op jit(solution)/shard_map/ppermute | solution.py:77
  38.8 10.7 %copy-start.1 = (bf16[128,2048]{1,0:T(8,128)(2,1)}, bf16[128,2048]{1,0:T(8,128)(2,1)S(1)}, u32[]{:S(2)}) copy-start(bf16[128,2048]{1,0:T(8,128)(2,1)S(1)} %collective-permute-done) | copy-start | bytes 1572868
  38.8 10.7 %collective-permute-start.1 = (bf16[128,2048]{1,0:T(8,128)(2,1)S(1)}, bf16[128,2048]{1,0:T(8,128)(2,1)}, u32[]{:S(2)}, u32[]{:S(2)}) collective-permute-start(bf16[128,2048]{1,0:T(8,128)(2,1)S(1)} %collective-permute-done), channel_id=1, source_target_pairs={{1,3},{5,7},{8,10},{12,14},{19,17},{23,21},{26,24},{30,28}} | collective-permute-start | bytes 1572872 | tf_op jit(solution)/shard_map/ppermute | solution.py:77
  41.1 25.9 %collective-permute-start.4 = (bf16[128,2048]{1,0:T(8,128)(2,1)}, bf16[128,2048]{1,0:T(8,128)(2,1)}, u32[]{:S(2)}, u32[]{:S(2)}) collective-permute-start(bf16[128,2048]{1,0:T(8,128)(2,1)} %constant_dynamic-slice_fusion.14), channel_id=1, source_target_pairs={{0,2},{4,6},{9,11},{13,15},{18,16},{22,20},{27,25},{31,29}} | collective-permute-start | bytes 1572872 | tf_op jit(solution)/shard_map/ppermute | solution.py:77
  46.2 22.4 %collective-permute-start.9 = (bf16[128,2048]{1,0:T(8,128)(2,1)}, bf16[128,2048]{1,0:T(8,128)(2,1)}, u32[]{:S(2)}, u32[]{:S(2)}) collective-permute-start(bf16[128,2048]{1,0:T(8,128)(2,1)} %constant_dynamic-slice_fusion.12), channel_id=1, source_target_pairs={{0,1},{4,5},{9,8},{13,12},{18,19},{22,23},{27,26},{31,30}} | collective-permute-start | bytes 1572872 | tf_op jit(solution)/shard_map/ppermute | solution.py:77
  49.4 23.5 %collective-permute-start.12 = (bf16[128,4096]{1,0:T(8,128)(2,1)S(1)}, bf16[128,4096]{1,0:T(8,128)(2,1)S(1)}, u32[]{:S(2)}, u32[]{:S(2)}) collective-permute-start(bf16[128,4096]{1,0:T(8,128)(2,1)S(1)} %collective-permute-done.8), channel_id=1, source_target_pairs={{0,4},{4,0},{8,12},{12,8},{16,20},{20,16},{24,28},{28,24},{1,5},{5... | collective-permute-start | bytes 3145736 | tf_op jit(solution)/shard_map/ppermute | solution.py:77
  63.5 28.2 %collective-permute-start.31 = (bf16[128,4096]{1,0:T(8,128)(2,1)}, bf16[128,4096]{1,0:T(8,128)(2,1)}, u32[]{:S(2)}, u32[]{:S(2)}) collective-permute-start(bf16[128,4096]{1,0:T(8,128)(2,1)} %collective-permute-done.30), channel_id=1, source_target_pairs={{8,0},{12,4},{16,24},{20,28},{9,1},{13,5},{17,25},{21,29},{10,2},{... | collective-permute-start | bytes 3145736 | tf_op jit(solution)/shard_map/ppermute | solution.py:77
  67.1 7.3 %collective-permute-start.5 = (bf16[128,2048]{1,0:T(8,128)(2,1)}, bf16[128,2048]{1,0:T(8,128)(2,1)}, u32[]{:S(2)}, u32[]{:S(2)}) collective-permute-start(bf16[128,2048]{1,0:T(8,128)(2,1)} %collective-permute-done.4), channel_id=1, source_target_pairs={{2,3},{6,7},{11,10},{15,14},{16,17},{20,21},{25,24},{29,28}} | collective-permute-start | bytes 1572872 | tf_op jit(solution)/shard_map/ppermute | solution.py:77
  68.5 15.9 %collective-permute-start.10 = (bf16[128,2048]{1,0:T(8,128)(2,1)}, bf16[128,2048]{1,0:T(8,128)(2,1)}, u32[]{:S(2)}, u32[]{:S(2)}) collective-permute-start(bf16[128,2048]{1,0:T(8,128)(2,1)} %collective-permute-done.9), channel_id=1, source_target_pairs={{1,3},{5,7},{8,10},{12,14},{19,17},{23,21},{26,24},{30,28}} | collective-permute-start | bytes 1572872 | tf_op jit(solution)/shard_map/ppermute | solution.py:77
  72.3 22.0 %collective-permute-start.2 = (bf16[128,2048]{1,0:T(8,128)(2,1)}, bf16[128,2048]{1,0:T(8,128)(2,1)S(1)}, u32[]{:S(2)}, u32[]{:S(2)}) collective-permute-start(bf16[128,2048]{1,0:T(8,128)(2,1)} %collective-permute-done.1), channel_id=1, source_target_pairs={{3,2},{7,6},{10,11},{14,15},{17,16},{21,20},{24,25},{28,29}} | collective-permute-start | bytes 1572872 | tf_op jit(solution)/shard_map/ppermute | solution.py:77
  73.0 45.6 %collective-permute-start.19 = (bf16[128,4096]{1,0:T(8,128)(2,1)}, bf16[128,4096]{1,0:T(8,128)(2,1)S(1)}, u32[]{:S(2)}, u32[]{:S(2)}) collective-permute-start(bf16[128,4096]{1,0:T(8,128)(2,1)} %collective-permute-done.18), channel_id=1, source_target_pairs={{8,0},{12,4},{16,24},{20,28},{9,1},{13,5},{17,25},{21,29},{10,2},{... | collective-permute-start | bytes 3145736 | tf_op jit(solution)/shard_map/ppermute | solution.py:77
  74.3 30.6 %collective-permute-start.13 = (bf16[128,2048]{1,0:T(8,128)(2,1)S(1)}, bf16[128,2048]{1,0:T(8,128)(2,1)S(1)}, u32[]{:S(2)}, u32[]{:S(2)}) collective-permute-start(bf16[128,2048]{1,0:T(8,128)(2,1)S(1)} %constant_dynamic-slice_fusion.10), channel_id=1, source_target_pairs={{0,2},{4,6},{9,11},{13,15},{18,16},{22,20},{27,25},{31,29}} | collective-permute-start | bytes 1572872 | tf_op jit(solution)/shard_map/ppermute | solution.py:77
  84.4 9.9 %collective-permute-start.6 = (bf16[128,2048]{1,0:T(8,128)(2,1)}, bf16[128,2048]{1,0:T(8,128)(2,1)S(1)}, u32[]{:S(2)}, u32[]{:S(2)}) collective-permute-start(bf16[128,2048]{1,0:T(8,128)(2,1)} %collective-permute-done.5), channel_id=1, source_target_pairs={{3,1},{7,5},{10,8},{14,12},{17,19},{21,23},{24,26},{28,30}} | collective-permute-start | bytes 1572872 | tf_op jit(solution)/shard_map/ppermute | solution.py:77
  91.7 2.7 %collective-permute-start.11 = (bf16[128,2048]{1,0:T(8,128)(2,1)}, bf16[128,2048]{1,0:T(8,128)(2,1)S(1)}, u32[]{:S(2)}, u32[]{:S(2)}) collective-permute-start(bf16[128,2048]{1,0:T(8,128)(2,1)} %collective-permute-done.10), channel_id=1, source_target_pairs={{3,2},{7,6},{10,11},{14,15},{17,16},{21,20},{24,25},{28,29}} | collective-permute-start | bytes 1572872 | tf_op jit(solution)/shard_map/ppermute | solution.py:77
  92.3 2.0 copy-start
  92.4 2.0 copy-start.2
  94.2 22.9 %collective-permute-start.35 = (bf16[128,4096]{1,0:T(8,128)(2,1)S(1)}, bf16[128,4096]{1,0:T(8,128)(2,1)S(1)}, u32[]{:S(2)}, u32[]{:S(2)}) collective-permute-start(bf16[128,4096]{1,0:T(8,128)(2,1)S(1)} %get-tuple-element.4), channel_id=1, source_target_pairs={{0,4},{4,0},{8,12},{12,8},{16,20},{20,16},{24,28},{28,24},{1,5},{5... | collective-permute-start | bytes 3145736 | tf_op jit(solution)/shard_map/ppermute | solution.py:77
  94.3 9.8 %copy-start.3 = (bf16[2048,512]{1,0:T(8,128)(2,1)S(1)}, bf16[2048,512]{1,0:T(8,128)(2,1)}, u32[]{:S(2)}) copy-start(bf16[2048,512]{1,0:T(8,128)(2,1)} %constant_dynamic-update-slice_fusion) | copy-start | bytes 6291460
  97.4 19.1 %collective-permute-start.32 = (bf16[128,2048]{1,0:T(8,128)(2,1)S(1)}, bf16[128,2048]{1,0:T(8,128)(2,1)S(1)}, u32[]{:S(2)}, u32[]{:S(2)}) collective-permute-start(bf16[128,2048]{1,0:T(8,128)(2,1)S(1)} %constant_dynamic-slice_fusion.4), channel_id=1, source_target_pairs={{0,1},{4,5},{9,8},{13,12},{18,19},{22,23},{27,26},{31,30}} | collective-permute-start | bytes 1572872 | tf_op jit(solution)/shard_map/ppermute | solution.py:77
  104.9 18.8 %collective-permute-start.14 = (bf16[128,2048]{1,0:T(8,128)(2,1)S(1)}, bf16[128,2048]{1,0:T(8,128)(2,1)S(1)}, u32[]{:S(2)}, u32[]{:S(2)}) collective-permute-start(bf16[128,2048]{1,0:T(8,128)(2,1)S(1)} %collective-permute-done.13), channel_id=1, source_target_pairs={{2,3},{6,7},{11,10},{15,14},{16,17},{20,21},{25,24},{29,28}} | collective-permute-start | bytes 1572872 | tf_op jit(solution)/shard_map/ppermute | solution.py:77
  105.7 32.3 %collective-permute-start.33 = (bf16[128,2048]{1,0:T(8,128)(2,1)S(1)}, bf16[128,2048]{1,0:T(8,128)(2,1)S(1)}, u32[]{:S(2)}, u32[]{:S(2)}) collective-permute-start(bf16[128,2048]{1,0:T(8,128)(2,1)S(1)} %constant_dynamic-slice_fusion.4), channel_id=1, source_target_pairs={{0,2},{4,6},{9,11},{13,15},{18,16},{22,20},{27,25},{31,29}} | collective-permute-start | bytes 1572872 | tf_op jit(solution)/shard_map/ppermute | solution.py:77
  116.4 22.3 %collective-permute-start.34 = (bf16[128,2048]{1,0:T(8,128)(2,1)S(1)}, bf16[128,2048]{1,0:T(8,128)(2,1)S(1)}, u32[]{:S(2)}, u32[]{:S(2)}) collective-permute-start(bf16[128,2048]{1,0:T(8,128)(2,1)S(1)} %collective-permute-done.32), channel_id=1, source_target_pairs={{1,3},{5,7},{8,10},{12,14},{19,17},{23,21},{26,24},{30,28}} | collective-permute-start | bytes 1572872 | tf_op jit(solution)/shard_map/ppermute | solution.py:77
  117.2 19.4 %collective-permute-start.37 = (bf16[128,2048]{1,0:T(8,128)(2,1)S(1)}, bf16[128,2048]{1,0:T(8,128)(2,1)S(1)}, u32[]{:S(2)}, u32[]{:S(2)}) collective-permute-start(bf16[128,2048]{1,0:T(8,128)(2,1)S(1)} %constant_dynamic-slice_fusion.2), channel_id=1, source_target_pairs={{0,2},{4,6},{9,11},{13,15},{18,16},{22,20},{27,25},{31,29}} | collective-permute-start | bytes 1572872 | tf_op jit(solution)/shard_map/ppermute | solution.py:77
  118.6 25.3 %collective-permute-start.36 = (bf16[128,2048]{1,0:T(8,128)(2,1)S(1)}, bf16[128,2048]{1,0:T(8,128)(2,1)S(1)}, u32[]{:S(2)}, u32[]{:S(2)}) collective-permute-start(bf16[128,2048]{1,0:T(8,128)(2,1)S(1)} %constant_dynamic-slice_fusion.2), channel_id=1, source_target_pairs={{0,1},{4,5},{9,8},{13,12},{18,19},{22,23},{27,26},{31,30}} | collective-permute-start | bytes 1572872 | tf_op jit(solution)/shard_map/ppermute | solution.py:77
  123.7 20.2 %collective-permute-start.20 = (bf16[128,2048]{1,0:T(8,128)(2,1)S(1)}, bf16[128,2048]{1,0:T(8,128)(2,1)S(1)}, u32[]{:S(2)}, u32[]{:S(2)}) collective-permute-start(bf16[128,2048]{1,0:T(8,128)(2,1)S(1)} %constant_dynamic-slice_fusion.8), channel_id=1, source_target_pairs={{0,1},{4,5},{9,8},{13,12},{18,19},{22,23},{27,26},{31,30}} | collective-permute-start | bytes 1572872 | tf_op jit(solution)/shard_map/ppermute | solution.py:77
  136.6 8.0 %collective-permute-start.38 = (bf16[128,2048]{1,0:T(8,128)(2,1)S(1)}, bf16[128,2048]{1,0:T(8,128)(2,1)S(1)}, u32[]{:S(2)}, u32[]{:S(2)}) collective-permute-start(bf16[128,2048]{1,0:T(8,128)(2,1)S(1)} %collective-permute-done.37), channel_id=1, source_target_pairs={{2,3},{6,7},{11,10},{15,14},{16,17},{20,21},{25,24},{29,28}} | collective-permute-start | bytes 1572872 | tf_op jit(solution)/shard_map/ppermute | solution.py:77
  138.1 27.2 %collective-permute-start.15 = (bf16[128,2048]{1,0:T(8,128)(2,1)S(1)}, bf16[128,2048]{1,0:T(8,128)(2,1)S(1)}, u32[]{:S(2)}, u32[]{:S(2)}) collective-permute-start(bf16[128,2048]{1,0:T(8,128)(2,1)S(1)} %collective-permute-done.14), channel_id=1, source_target_pairs={{3,1},{7,5},{10,8},{14,12},{17,19},{21,23},{24,26},{28,30}} | collective-permute-start | bytes 1572872 | tf_op jit(solution)/shard_map/ppermute | solution.py:77
  138.8 26.6 %collective-permute-start.21 = (bf16[128,2048]{1,0:T(8,128)(2,1)S(1)}, bf16[128,2048]{1,0:T(8,128)(2,1)S(1)}, u32[]{:S(2)}, u32[]{:S(2)}) collective-permute-start(bf16[128,2048]{1,0:T(8,128)(2,1)S(1)} %constant_dynamic-slice_fusion.8), channel_id=1, source_target_pairs={{0,2},{4,6},{9,11},{13,15},{18,16},{22,20},{27,25},{31,29}} | collective-permute-start | bytes 1572872 | tf_op jit(solution)/shard_map/ppermute | solution.py:77
  143.8 3.0 %collective-permute-start.23 = (bf16[128,4096]{1,0:T(8,128)(2,1)S(1)}, bf16[128,4096]{1,0:T(8,128)(2,1)S(1)}, u32[]{:S(2)}, u32[]{:S(2)}) collective-permute-start(bf16[128,4096]{1,0:T(8,128)(2,1)S(1)} %get-tuple-element.14), channel_id=1, source_target_pairs={{0,4},{4,0},{8,12},{12,8},{16,20},{20,16},{24,28},{28,24},{1,5},{5... | collective-permute-start | bytes 3145736 | tf_op jit(solution)/shard_map/ppermute | solution.py:77
  143.9 23.4 %collective-permute-start.22 = (bf16[128,2048]{1,0:T(8,128)(2,1)S(1)}, bf16[128,2048]{1,0:T(8,128)(2,1)S(1)}, u32[]{:S(2)}, u32[]{:S(2)}) collective-permute-start(bf16[128,2048]{1,0:T(8,128)(2,1)S(1)} %collective-permute-done.20), channel_id=1, source_target_pairs={{1,3},{5,7},{8,10},{12,14},{19,17},{23,21},{26,24},{30,28}} | collective-permute-start | bytes 1572872 | tf_op jit(solution)/shard_map/ppermute | solution.py:77
  146.2 6.6 %collective-permute-start.39 = (f32[128,512]{1,0:T(8,128)S(1)}, f32[128,512]{1,0:T(8,128)S(1)}, u32[]{:S(2)}, u32[]{:S(2)}) collective-permute-start(f32[128,512]{1,0:T(8,128)S(1)} %slice.52), channel_id=1, source_target_pairs={{0,4},{4,0},{8,12},{12,8},{16,20},{20,16},{24,28},{28,24},{1,5},{5... | collective-permute-start | bytes 786440 | tf_op jit(solution)/shard_map/ppermute | solution.py:77
  146.9 17.4 %collective-permute-start.25 = (bf16[128,2048]{1,0:T(8,128)(2,1)S(1)}, bf16[128,2048]{1,0:T(8,128)(2,1)S(1)}, u32[]{:S(2)}, u32[]{:S(2)}) collective-permute-start(bf16[128,2048]{1,0:T(8,128)(2,1)S(1)} %constant_dynamic-slice_fusion.6), channel_id=1, source_target_pairs={{0,2},{4,6},{9,11},{13,15},{18,16},{22,20},{27,25},{31,29}} | collective-permute-start | bytes 1572872 | tf_op jit(solution)/shard_map/ppermute | solution.py:77
  152.8 16.0 %collective-permute-start.24 = (bf16[128,2048]{1,0:T(8,128)(2,1)S(1)}, bf16[128,2048]{1,0:T(8,128)(2,1)S(1)}, u32[]{:S(2)}, u32[]{:S(2)}) collective-permute-start(bf16[128,2048]{1,0:T(8,128)(2,1)S(1)} %constant_dynamic-slice_fusion.6), channel_id=1, source_target_pairs={{0,1},{4,5},{9,8},{13,12},{18,19},{22,23},{27,26},{31,30}} | collective-permute-start | bytes 1572872 | tf_op jit(solution)/shard_map/ppermute | solution.py:77
  164.3 4.5 %collective-permute-start.26 = (bf16[128,2048]{1,0:T(8,128)(2,1)S(1)}, bf16[128,2048]{1,0:T(8,128)(2,1)S(1)}, u32[]{:S(2)}, u32[]{:S(2)}) collective-permute-start(bf16[128,2048]{1,0:T(8,128)(2,1)S(1)} %collective-permute-done.25), channel_id=1, source_target_pairs={{2,3},{6,7},{11,10},{15,14},{16,17},{20,21},{25,24},{29,28}} | collective-permute-start | bytes 1572872 | tf_op jit(solution)/shard_map/ppermute | solution.py:77
  165.3 17.0 %collective-permute-start.7 = (f32[128,512]{1,0:T(8,128)S(1)}, f32[128,512]{1,0:T(8,128)S(1)}, u32[]{:S(2)}, u32[]{:S(2)}) collective-permute-start(f32[128,512]{1,0:T(8,128)S(1)} %slice.46), channel_id=1, source_target_pairs={{0,4},{4,0},{8,12},{12,8},{16,20},{20,16},{24,28},{28,24},{1,5},{5... | collective-permute-start | bytes 786440 | tf_op jit(solution)/shard_map/ppermute | solution.py:77
  165.4 39.8 %collective-permute-start.41 = (f32[128,512]{1,0:T(8,128)S(1)}, f32[128,512]{1,0:T(8,128)S(1)}, u32[]{:S(2)}, u32[]{:S(2)}) collective-permute-start(f32[128,512]{1,0:T(8,128)S(1)} %slice_add_fusion), channel_id=1, source_target_pairs={{0,24},{4,28},{24,0},{28,4},{1,25},{5,29},{25,1},{29,5},{2,26},{6,... | collective-permute-start | bytes 786440 | tf_op jit(solution)/shard_map/ppermute | solution.py:77
  167.3 37.8 %collective-permute-start.40 = (f32[128,512]{1,0:T(8,128)S(1)}, f32[128,512]{1,0:T(8,128)S(1)}, u32[]{:S(2)}, u32[]{:S(2)}) collective-permute-start(f32[128,512]{1,0:T(8,128)S(1)} %slice_add_fusion), channel_id=1, source_target_pairs={{8,24},{12,28},{16,0},{20,4},{9,25},{13,29},{17,1},{21,5},{10,26},... | collective-permute-start | bytes 786440 | tf_op jit(solution)/shard_map/ppermute | solution.py:77
  171.8 1.7 collective-permute-start.27
  172.3 9.2 %collective-permute-start.16 = (f32[128,512]{1,0:T(8,128)S(1)}, f32[128,512]{1,0:T(8,128)S(1)}, u32[]{:S(2)}, u32[]{:S(2)}) collective-permute-start(f32[128,512]{1,0:T(8,128)S(1)} %slice.48), channel_id=1, source_target_pairs={{0,4},{4,0},{8,12},{12,8},{16,20},{20,16},{24,28},{28,24},{1,5},{5... | collective-permute-start | bytes 786440 | tf_op jit(solution)/shard_map/ppermute | solution.py:77
  173.5 31.6 %collective-permute-start.29 = (f32[128,512]{1,0:T(8,128)S(1)}, f32[128,512]{1,0:T(8,128)S(1)}, u32[]{:S(2)}, u32[]{:S(2)}) collective-permute-start(f32[128,512]{1,0:T(8,128)S(1)} %slice_add_fusion.1), channel_id=1, source_target_pairs={{0,16},{4,20},{24,8},{28,12},{1,17},{5,21},{25,9},{29,13},{2,18},{... | collective-permute-start | bytes 786440 | tf_op jit(solution)/shard_map/ppermute | solution.py:77
  181.6 23.6 %collective-permute-start.28 = (f32[128,512]{1,0:T(8,128)S(1)}, f32[128,512]{1,0:T(8,128)S(1)}, u32[]{:S(2)}, u32[]{:S(2)}) collective-permute-start(f32[128,512]{1,0:T(8,128)S(1)} %slice_add_fusion.1), channel_id=1, source_target_pairs={{8,16},{12,20},{16,8},{20,12},{9,17},{13,21},{17,9},{21,13},{10,18... | collective-permute-start | bytes 786440 | tf_op jit(solution)/shard_map/ppermute | solution.py:77
  182.3 22.8 %collective-permute-start.17 = (f32[128,512]{1,0:T(8,128)S(1)}, f32[128,512]{1,0:T(8,128)S(1)}, u32[]{:S(2)}, u32[]{:S(2)}) collective-permute-start(f32[128,512]{1,0:T(8,128)S(1)} %slice_add_fusion.2), channel_id=1, source_target_pairs={{0,8},{4,12},{8,0},{12,4},{16,24},{20,28},{24,16},{28,20},{1,9},{5... | collective-permute-start | bytes 786440 | tf_op jit(solution)/shard_map/ppermute | solution.py:77

commit v2 on v1

v2 whole, which is shorter than its diff:
```python
import functools

import jax
import jax.numpy as jnp
from jax import lax
from jax.experimental import pallas as pl
from jax.experimental.pallas import tpu as pltpu
from jax.sharding import PartitionSpec as P

epsilon = 1e-05

def along(chips):
    return [(start * 2 + c, end * 2 + c) for start, end in chips for c in range(2)]


NEAR = along([(z, z ^ 1) for z in range(4)])
FLIPS = {j: along([(z, z ^ j) for z in range(4)]) for j in (1, 2, 3)}
MIDDLE = along([(1, 2), (2, 1)])
OUTWARD = along([(1, 0), (2, 3)])
CORES = [(f, f ^ 1) for f in range(8)]
SIDES = {k: [(t, t ^ k) for t in range(4)] for k in (1, 2, 3)}


def tile_kernel(scale, slots, *refs):
    rows, cols, out = refs[:slots], refs[slots : 2 * slots], refs[2 * slots]
    together = 2 if slots % 2 == 0 else 1
    groups = [slice(i, i + together) for i in range(0, slots, together)]
    turned = [jnp.concatenate([row[...] for row in rows[g]]).T for g in groups]
    width = out.shape[1]
    step = min(width, 1024)
    for left in range(0, width, step):
        total = None
        for row, group in zip(turned, groups):
            col = jnp.concatenate([c[:, left : left + step] for c in cols[group]])
            product = jnp.dot(row, col, preferred_element_type=jnp.float32)
            total = product if total is None else total + product
        out[:, left : left + step] = total * scale


def hessian_tile(rows, cols, scale):
    slots = len(rows)
    depth, height = rows[0].shape
    width = cols[0].shape[1]
    block = 256
    flops = 2 * slots * depth * height * width
    return pl.pallas_call(
        functools.partial(tile_kernel, scale, slots),
        grid=(height // block,),
        in_specs=[pl.BlockSpec((depth, block), lambda i: (0, i))] * slots
        + [pl.BlockSpec((depth, width), lambda i: (0, 0), pipeline_mode=pl.Buffered(1))] * slots,
        out_specs=pl.BlockSpec((block, width), lambda i: (i, 0)),
        out_shape=jax.ShapeDtypeStruct((height, width), jnp.float32),
        compiler_params=pltpu.CompilerParams(vmem_limit_bytes=40 << 20),
        cost_estimate=pl.CostEstimate(
            flops=flops, bytes_accessed=4 * height * width, transcendentals=0
        ),
    )(*rows, *cols)


def pair_kernel(left, right, out):
    width = left.shape[1]
    out[:, :width] = left[...]
    out[:, width:] = right[...]


def side_by_side(left, right):
    depth, width = left.shape
    block = pl.BlockSpec((depth, width), lambda: (0, 0))
    return pl.pallas_call(
        pair_kernel,
        in_specs=[block, block],
        out_specs=pl.BlockSpec((depth, 2 * width), lambda: (0, 0)),
        out_shape=jax.ShapeDtypeStruct((depth, 2 * width), left.dtype),
        compiler_params=pltpu.CompilerParams(vmem_limit_bytes=16 << 20),
        cost_estimate=pl.CostEstimate(flops=0, bytes_accessed=50_000_000, transcendentals=0),
    )(left, right)


def slice_body(tokens, norm_gain, key_weight, value_weight):
    count, width = tokens.shape
    features = width * 4
    half, quarter = width // 2, count // 4
    total_tokens = count * 8
    f, t = lax.axis_index("fsdp"), lax.axis_index("tp")
    z, core = f // 2, f % 2
    role = z ^ t
    middle = (z == 1) | (z == 2)

    def move(x, pairs, axis="fsdp"):
        return lax.ppermute(x, axis, pairs)

    def reorder(x):
        return jnp.concatenate(
            [lax.dynamic_slice_in_dim(x, (t ^ k) * quarter, quarter) for k in range(4)]
        )

    turned = reorder(tokens)
    near = move(turned, NEAR)
    across = move(turned, MIDDLE)

    pieces = [turned[k * quarter : (k + 1) * quarter] for k in range(4)]
    held = [pieces[0]] + [move(pieces[k], SIDES[k], "tp") for k in (1, 2, 3)]

    widened = tokens.astype(jnp.float32)
    note = jnp.concatenate([jnp.sum(widened * widened, axis=1), norm_gain.astype(jnp.float32)])
    notes = lax.all_gather(note, "tp")
    *held, notes = lax.optimization_barrier((*held, notes))
    power = jnp.sum(notes[:, :count], axis=0)
    scale = lax.rsqrt(power / features + epsilon)
    gains = notes[:, count:]
    col_gain = norm_gain.astype(jnp.float32)[None, :]

    def norm(block, gain, scale):
        return (block.astype(jnp.float32) * gain * scale).astype(jnp.bfloat16)

    rest = lax.dynamic_slice_in_dim(scale, t * quarter, quarter)[:, None]
    quarter_scale, thirds = rest, []
    for _ in range(3):
        part = lax.reduce_precision(rest, 8, 7)
        rest = rest - part
        thirds.append(part.astype(jnp.bfloat16))
    thirds = jnp.concatenate(thirds + [jnp.zeros((quarter, 125), jnp.bfloat16)], axis=1)

    def choose(which):
        piece = jnp.where(
            which == 0,
            held[0],
            jnp.where(which == 1, held[1], jnp.where(which == 2, held[2], held[3])),
        )
        gain = lax.dynamic_slice_in_dim(gains, t ^ which, 1)
        return jnp.concatenate([norm(piece, gain, quarter_scale), thirds], axis=1)

    landed = [choose(role)] + [move(choose(role ^ j), FLIPS[j]) for j in (1, 2, 3)]

    outer = move(across, OUTWARD)
    beyond = move(near, MIDDLE)

    key_weight, value_weight, near, across = lax.optimization_barrier(
        (key_weight, value_weight, near, across)
    )
    weights = side_by_side(key_weight, value_weight)
    *landed, weights = lax.optimization_barrier((*landed, weights))
    landed = jnp.stack(landed)

    def share(which):
        features = lax.dynamic_slice_in_dim(landed, which * half, half, axis=2)
        return jnp.concatenate([features, landed[:, :, width:]], axis=2)

    mine = share(core)
    other = move(share(1 - core), CORES)
    group = jnp.stack([mine, other])
    from_x = move(group, SIDES[1], "tp")
    from_y = move(group, SIDES[2], "tp")
    last = move(beyond, OUTWARD)
    far_mine = move(from_y[0], SIDES[1], "tp")
    far_other = move(from_x[1], SIDES[2], "tp")
    from_x, from_y, turned, near, beyond = lax.optimization_barrier(
        (from_x, from_y, turned, near, beyond)
    )
    quarters = [
        [mine, from_x[0], from_y[0], far_mine],
        [other, from_x[1], from_y[1], far_other],
    ]
    blocks = [turned, near, jnp.where(middle, beyond, outer)]
    twins = [move(block, CORES) for block in blocks]

    def row_part(j, p):
        return jnp.concatenate([g[j, :, :half] for g in quarters[p]])

    sent_scales = [
        [jnp.sum(g[:, :, half:].astype(jnp.float32), axis=2) for g in quarters[p]]
        for p in range(2)
    ]
    scales = [jnp.concatenate(sent_scales[p], axis=1) for p in range(2)]

    def col_parts(j):
        return [norm((blocks, twins)[p][j], col_gain, scales[p][j][:, None]) for p in range(2)]

    rows = [[row_part(j, p) for p in range(2)] for j in range(4)]
    parts = [
        jnp.dot(jnp.concatenate(row), weights, preferred_element_type=jnp.float32) for row in rows
    ]
    own = jnp.stack([part[:count] for part in parts])
    sums = own + move(jnp.stack([part[count:] for part in parts]), CORES)
    homes = [move(sums[j], FLIPS[j]) for j in (1, 2, 3)]

    cols = [col_parts(j) for j in range(3)]
    last, cols = lax.optimization_barrier((last, cols))
    blocks.append(jnp.where(middle, across, last))
    twins.append(move(blocks[3], CORES))
    cols.append(col_parts(3))
    hessian = hessian_tile(sum(rows, []), sum(cols, []), 2.0 / total_tokens)

    hessian, homes = lax.optimization_barrier((hessian, homes))
    projected = sums[0] + homes[0] + homes[1] + homes[2]
    projected = reorder(projected.astype(jnp.bfloat16))
    columns = key_weight.shape[1]
    return projected[:, :columns], projected[:, columns:], hessian


def general_body(tokens, norm_gain, key_weight, value_weight):
    features = tokens.shape[1] * lax.axis_size("tp")
    total_tokens = tokens.shape[0] * lax.axis_size("fsdp")
    widened = tokens.astype(jnp.float32)
    power = lax.psum(jnp.sum(widened * widened, axis=1), "tp")
    inverse = lax.rsqrt(power / features + epsilon)
    normed = (widened * norm_gain.astype(jnp.float32)[None, :] * inverse[:, None]).astype(
        jnp.bfloat16
    )
    cols = lax.all_gather(normed, "fsdp", axis=0, tiled=True)
    full_rows = lax.all_gather(normed, "tp", axis=1, tiled=True)
    rows = lax.all_to_all(full_rows, "fsdp", split_axis=1, concat_axis=0, tiled=True)
    weights = jnp.concatenate([key_weight, value_weight], axis=1)
    part = jnp.dot(rows, weights, preferred_element_type=jnp.float32)
    projected = lax.psum_scatter(part, "fsdp", scatter_dimension=0, tiled=True).astype(jnp.bfloat16)
    columns = key_weight.shape[1]
    hessian = hessian_tile([rows], [cols], 2.0 / total_tokens)
    return projected[:, :columns], projected[:, columns:], hessian


def solution(mesh):
    small = mesh.shape["fsdp"] == 8 and mesh.shape["tp"] == 4
    placed = (P("fsdp", "tp"), P("tp"), P("fsdp", "tp"), P("fsdp", "tp"))
    return jax.shard_map(
        slice_body if small else general_body,
        mesh=mesh,
        in_specs=placed,
        out_specs=(P("fsdp", "tp"), P("fsdp", "tp"), P("fsdp", "tp")),
        check_vma=False,
    )
```

time: 209 us -> 150 us (0.72); the launches traced: 206 us -> 149 us
  starting transfers between devices: 90 us -> 32.3 us
  blocking collectives: 22.4 us -> 8.32 us
  waiting for transfers between devices: 45.8 us -> 57.6 us
  local copies, waits for them, and re-layouts: 8.39 us -> 13 us
    ppermute x42 -> x24, starting transfers between devices: 90 us -> 32.3 us  [move(): return lax.ppermute(x, axis, pairs)]
    all_gather x1 -> x0, blocking collectives: 13.9 us -> none  [slice_body(): inverse = lax.all_gather(lax.rsqrt(power / features + epsilon), 'fsdp')]
    ppermute x42 -> x24, waiting for transfers between devices: 45.8 us -> 57.6 us  [move(): return lax.ppermute(x, axis, pairs)]
    convert_element_type x8 -> x10, other arithmetic: 10.7 us -> 6.08 us  [the longest x6 5.89 us: norm(): return (block.astype(jnp.float32) * gain * scale).astype(jnp.bfloat16)]
    squeeze x0 -> x12, local copies, waits for them, and re-layouts: none -> 3.98 us  [the longest x7 1.41 us: row_part(): return jnp.concatenate([g[j, :, :half] for g in quarters[p]])]
    another operation x0 -> x4, other arithmetic: none -> 2.54 us  [the longest x1 1.28 us: slice_body(): landed = jnp.stack(landed)]
  transfers between devices with their start and end apart: 42 -> 24, of which waited for: 5 -> 9; matrix products, arithmetic and copies ran while one was open for 12% -> 13% of each run, Pallas kernels for 10% -> 15%
where the time goes in v2:
time: 150 us; the launch traced here: 149 us
  waiting for transfers between devices  57.6 us (38%)
  starting transfers between devices  32.3 us (22%)
  Pallas kernels  22 us (15%)
  local copies, waits for them, and re-layouts  13 us (9%)
  other arithmetic  12 us (8%)
  blocking collectives  8.32 us (6%)
  matrix products  2.8 us (2%)
    ppermute x24, waiting for transfers between devices, move(): return lax.ppermute(x, axis, pairs)  57.6 us
    ppermute x24, starting transfers between devices, move(): return lax.ppermute(x, axis, pairs)  32.3 us
    pallas_call x1, Pallas kernels, hessian_tile(): pl.pallas_call(functools.partial(tile_kernel, scale, slots), grid=(height...  21.8 us
    all_gather x1, blocking collectives, slice_body(): notes = lax.all_gather(note, 'tp')  8.32 us
    convert_element_type x6, other arithmetic, norm(): return (block.astype(jnp.float32) * gain * scale).astype(jnp.bfloat16)  5.89 us
    unnamed x27, local copies, waits for them, and re-layouts  3.03 us
  transfers between devices with their start and end apart: 24, of which 9 were waited for; matrix products, arithmetic and copies ran while one was open for 13% of the time, Pallas kernels for 15%

profile of v2, /device:TPU:0, one launch (start us, length us, event | category | flops | bytes accessed | tf_op | source)
XLA Modules:
  0.0 149.3 jit_solution(9372081888893490278)
XLA Ops:
  0.7 2.1 %constant_dynamic-slice_fusion.10 = (bf16[32,4096]{1,0:T(8,128)(2,1)}, bf16[32,4096]{1,0:T(8,128)(2,1)S(1)}, bf16[32,4096]{1,0:T(8,128)(2,1)S(1)}, bf16[32,4096]{1,0:T(8,128)(2,1)S(1)}) fusion(bf16[128,4096]{1,0:T(8,128)(2,1)} %param.4, s32[]{:T(128)S(6)} %select_n.137, s32[]{:T(128)S(6)} %select_n.136, s32[]{:T(128)S(6)} %select_n.135, s32[]{:T(128)S(6)} %select_n.134), kind=kLoop, calls=%fused_computation.138 | loop fusion | bytes 2097168 | tf_op jit(solution)/shard_map/dynamic_slice | solution.py:94
  2.7 3.9 %collective-permute-start.2 = (bf16[32,4096]{1,0:T(8,128)(2,1)}, bf16[32,4096]{1,0:T(8,128)(2,1)S(1)}, u32[]{:S(2)}, u32[]{:S(2)}) collective-permute-start(bf16[32,4096]{1,0:T(8,128)(2,1)} %get-tuple-element.95), channel_id=1, source_target_pairs={{0,3},{1,2},{2,1},{3,0},{4,7},{5,6},{6,5},{7,4},{8,11},{9,10},{10,... | collective-permute-start | bytes 786440 | tf_op jit(solution)/shard_map/ppermute | solution.py:90
  6.6 0.5 collective-permute-start.1
  7.2 1.0 pad_maximum_fusion.2
  8.2 1.7 %collective-permute-start.7 = (bf16[128,4096]{1,0:T(8,128)(2,1)S(1)}, bf16[128,4096]{1,0:T(8,128)(2,1)}, u32[]{:S(2)}, u32[]{:S(2)}) collective-permute-start(bf16[128,4096]{1,0:T(8,128)(2,1)S(1)} %pad_maximum_fusion.2), channel_id=1, source_target_pairs={{8,16},{12,20},{16,8},{20,12},{9,17},{13,21},{17,9},{21,13},{10,18... | collective-permute-start | bytes 3145736 | tf_op jit(solution)/shard_map/ppermute | solution.py:90
  9.9 4.0 %collective-permute-start.6 = (bf16[128,4096]{1,0:T(8,128)(2,1)S(1)}, bf16[128,4096]{1,0:T(8,128)(2,1)}, u32[]{:S(2)}, u32[]{:S(2)}) collective-permute-start(bf16[128,4096]{1,0:T(8,128)(2,1)S(1)} %pad_maximum_fusion.2), channel_id=1, source_target_pairs={{0,8},{4,12},{8,0},{12,4},{16,24},{20,28},{24,16},{28,20},{1,9},{5... | collective-permute-start | bytes 3145736 | tf_op jit(solution)/shard_map/ppermute | solution.py:90
  14.2 8.3 %all-gather.1 = f32[4,1,4224]{2,1,0:T(1,128)S(1)} all-gather(f32[1,1,4224]{2,1,0:T(1,128)S(1)} %reshape.25), channel_id=2, replica_groups=mesh['fsdp'=8,'tp'=4] {'tp'}, dimensions={0}, use_global_device_ids=true | all-gather | bytes 84480 | tf_op jit(solution)/shard_map/all_gather | solution.py:106
  22.8 0.5 copy-done.7
  23.3 1.3 multiply_convert_fusion.8
  24.9 0.8 concatenate.82
  25.7 0.8 concatenate.81
  26.5 0.8 concatenate.80
  27.4 1.6 %collective-permute-start.3 = (bf16[32,4224]{1,0:T(8,128)(2,1)}, bf16[32,4224]{1,0:T(8,128)(2,1)}, u32[]{:S(2)}, u32[]{:S(2)}) collective-permute-start(bf16[32,4224]{1,0:T(8,128)(2,1)} %concatenate.80), channel_id=1, source_target_pairs={{0,8},{4,12},{8,0},{12,4},{16,24},{20,28},{24,16},{28,20},{1,9},{5... | collective-permute-start | bytes 811016 | tf_op jit(solution)/shard_map/ppermute | solution.py:90
  28.9 2.6 %collective-permute-start.4 = (bf16[32,4224]{1,0:T(8,128)(2,1)}, bf16[32,4224]{1,0:T(8,128)(2,1)}, u32[]{:S(2)}, u32[]{:S(2)}) collective-permute-start(bf16[32,4224]{1,0:T(8,128)(2,1)} %concatenate.81), channel_id=1, source_target_pairs={{0,16},{4,20},{8,24},{12,28},{16,0},{20,4},{24,8},{28,12},{1,17},{... | collective-permute-start | bytes 811016 | tf_op jit(solution)/shard_map/ppermute | solution.py:90
  32.0 10.8 %collective-permute-done.6 = bf16[128,4096]{1,0:T(8,128)(2,1)} collective-permute-done((bf16[128,4096]{1,0:T(8,128)(2,1)S(1)}, bf16[128,4096]{1,0:T(8,128)(2,1)}, u32[]{:S(2)}, u32[]{:S(2)}) %collective-permute-start.6) | collective-permute-done | bytes 1048608 | tf_op jit(solution)/shard_map/ppermute | solution.py:90
  42.8 1.2 copy-done.1
  44.2 3.8 %collective-permute-done.3 = bf16[32,4224]{1,0:T(8,128)(2,1)} collective-permute-done((bf16[32,4224]{1,0:T(8,128)(2,1)}, bf16[32,4224]{1,0:T(8,128)(2,1)}, u32[]{:S(2)}, u32[]{:S(2)}) %collective-permute-start.3) | collective-permute-done | bytes 270368 | tf_op jit(solution)/shard_map/ppermute | solution.py:90
  48.0 7.2 %collective-permute-done.4 = bf16[32,4224]{1,0:T(8,128)(2,1)} collective-permute-done((bf16[32,4224]{1,0:T(8,128)(2,1)}, bf16[32,4224]{1,0:T(8,128)(2,1)}, u32[]{:S(2)}, u32[]{:S(2)}) %collective-permute-start.4) | collective-permute-done | bytes 270368 | tf_op jit(solution)/shard_map/ppermute | solution.py:90
  55.2 1.3 pad_maximum_fusion.1
  56.8 1.9 %collective-permute-done.8 = bf16[4,32,2176]{2,1,0:T(8,128)(2,1)S(1)} collective-permute-done((bf16[4,32,2176]{2,1,0:T(8,128)(2,1)S(1)}, bf16[4,32,2176]{2,1,0:T(8,128)(2,1)S(1)}, u32[]{:S(2)}, u32[]{:S(2)}) %collective-permute-start.8) | collective-permute-done | bytes 557088 | tf_op jit(solution)/shard_map/ppermute | solution.py:90
  58.8 0.8 copy-done.2
  59.6 1.1 pad_maximum_fusion
  60.7 1.5 %collective-permute-start.10 = (bf16[2,4,32,2176]{3,2,1,0:T(8,128)(2,1)}, bf16[2,4,32,2176]{3,2,1,0:T(8,128)(2,1)}, u32[]{:S(2)}, u32[]{:S(2)}) collective-permute-start(bf16[2,4,32,2176]{3,2,1,0:T(8,128)(2,1)} %pad_maximum_fusion), channel_id=1, source_target_pairs={{0,2},{1,3},{2,0},{3,1},{4,6},{5,7},{6,4},{7,5},{8,10},{9,11},{10,... | collective-permute-start | bytes 3342344 | tf_op jit(solution)/shard_map/ppermute | solution.py:90
  62.2 1.7 %collective-permute-start.11 = (bf16[128,4096]{1,0:T(8,128)(2,1)}, bf16[128,4096]{1,0:T(8,128)(2,1)}, u32[]{:S(2)}, u32[]{:S(2)}) collective-permute-start(bf16[128,4096]{1,0:T(8,128)(2,1)} %collective-permute-done.6), channel_id=1, source_target_pairs={{8,16},{12,20},{16,8},{20,12},{9,17},{13,21},{17,9},{21,13},{10,18... | collective-permute-start | bytes 3145736 | tf_op jit(solution)/shard_map/ppermute | solution.py:90
  63.9 1.4 collective-permute-start.18
  65.5 1.6 %collective-permute-start.9 = (bf16[2,4,32,2176]{3,2,1,0:T(8,128)(2,1)}, bf16[2,4,32,2176]{3,2,1,0:T(8,128)(2,1)S(1)}, u32[]{:S(2)}, u32[]{:S(2)}) collective-permute-start(bf16[2,4,32,2176]{3,2,1,0:T(8,128)(2,1)} %pad_maximum_fusion), channel_id=1, source_target_pairs={{0,1},{1,0},{2,3},{3,2},{4,5},{5,4},{6,7},{7,6},{8,9},{9,8},{10,11... | collective-permute-start | bytes 3342344 | tf_op jit(solution)/shard_map/ppermute | solution.py:90
  67.1 0.8 convert_reduce_fusion.3
  67.9 1.1 slice_bitcast_fusion.21
  69.1 1.5 collective-permute-start.15
  70.6 17.1 %collective-permute-done.10 = bf16[2,4,32,2176]{3,2,1,0:T(8,128)(2,1)} collective-permute-done((bf16[2,4,32,2176]{3,2,1,0:T(8,128)(2,1)}, bf16[2,4,32,2176]{3,2,1,0:T(8,128)(2,1)}, u32[]{:S(2)}, u32[]{:S(2)}) %collective-permute-start.10) | collective-permute-done | bytes 1114144 | tf_op jit(solution)/shard_map/ppermute | solution.py:90
  87.6 1.1 slice_bitcast_fusion.1
  88.7 1.6 %collective-permute-start.12 = (bf16[4,32,2176]{2,1,0:T(8,128)(2,1)S(1)}, bf16[4,32,2176]{2,1,0:T(8,128)(2,1)S(1)}, u32[]{:S(2)}, u32[]{:S(2)}) collective-permute-start(bf16[4,32,2176]{2,1,0:T(8,128)(2,1)S(1)} %slice_bitcast_fusion.1), channel_id=1, source_target_pairs={{0,1},{1,0},{2,3},{3,2},{4,5},{5,4},{6,7},{7,6},{8,9},{9,8},{10,11... | collective-permute-start | bytes 1671176 | tf_op jit(solution)/shard_map/ppermute | solution.py:90
  90.3 3.0 %collective-permute-done.9 = bf16[2,4,32,2176]{3,2,1,0:T(8,128)(2,1)S(1)} collective-permute-done((bf16[2,4,32,2176]{3,2,1,0:T(8,128)(2,1)}, bf16[2,4,32,2176]{3,2,1,0:T(8,128)(2,1)S(1)}, u32[]{:S(2)}, u32[]{:S(2)}) %collective-permute-start.9) | collective-permute-done | bytes 1114144 | tf_op jit(solution)/shard_map/ppermute | solution.py:90
  93.5 1.3 slice_bitcast_fusion.2
  95.4 8.7 %collective-permute-done.12 = bf16[4,32,2176]{2,1,0:T(8,128)(2,1)S(1)} collective-permute-done((bf16[4,32,2176]{2,1,0:T(8,128)(2,1)S(1)}, bf16[4,32,2176]{2,1,0:T(8,128)(2,1)S(1)}, u32[]{:S(2)}, u32[]{:S(2)}) %collective-permute-start.12) | collective-permute-done | bytes 557088 | tf_op jit(solution)/shard_map/ppermute | solution.py:90
  104.3 0.4 multiply_convert_fusion.3
  104.7 0.6 collective-permute-start.19
  105.5 4.7 %collective-permute-done.13 = bf16[4,32,2176]{2,1,0:T(8,128)(2,1)S(1)} collective-permute-done((bf16[4,32,2176]{2,1,0:T(8,128)(2,1)S(1)}, bf16[4,32,2176]{2,1,0:T(8,128)(2,1)S(1)}, u32[]{:S(2)}, u32[]{:S(2)}) %collective-permute-start.13) | collective-permute-done | bytes 557088 | tf_op jit(solution)/shard_map/ppermute | solution.py:90
  110.3 0.7 fusion.11
  111.0 0.7 fusion.14
  111.7 0.7 fusion.13
  112.4 0.7 fusion.12
  113.8 3.3 %multiply_convert_fusion.2 = (bf16[128,4096]{1,0:T(8,128)(2,1)S(1)}, bf16[128,4096]{1,0:T(8,128)(2,1)S(1)}, bf16[128,4096]{1,0:T(8,128)(2,1)S(1)}, bf16[128,4096]{1,0:T(8,128)(2,1)S(1)}, bf16[128,4096]{1,0:T(8,128)(2,1)S(1)}) fusion(bf16[128,4096]{1,0:T(8,128)(2,1)S(1)} %collective-permute-done.19, f32[128]{0:T(128)S(1)} %get-tuple-element.181, ...), kind=kLoop, calls=%fused_computation.2 | loop fusion | flops 10485760 | bytes 10504704 | tf_op jit(solution)/shard_map/convert_element_type | solution.py:114
  117.5 0.4 multiply_convert_fusion.1
  118.7 2.6 %collective-permute-start.23 = (f32[128,512]{1,0:T(8,128)S(1)}, f32[128,512]{1,0:T(8,128)S(1)}, u32[]{:S(2)}, u32[]{:S(2)}) collective-permute-start(f32[128,512]{1,0:T(8,128)S(1)} %get-tuple-element.92), channel_id=1, source_target_pairs={{0,24},{4,28},{8,16},{12,20},{16,8},{20,12},{24,0},{28,4},{1,25},{... | collective-permute-start | bytes 786440 | tf_op jit(solution)/shard_map/ppermute | solution.py:90
  121.3 5.1 %collective-permute-start.22 = (f32[128,512]{1,0:T(8,128)S(1)}, f32[128,512]{1,0:T(8,128)S(1)}, u32[]{:S(2)}, u32[]{:S(2)}) collective-permute-start(f32[128,512]{1,0:T(8,128)S(1)} %get-tuple-element.93), channel_id=1, source_target_pairs={{0,16},{4,20},{8,24},{12,28},{16,0},{20,4},{24,8},{28,12},{1,17},{... | collective-permute-start | bytes 786440 | tf_op jit(solution)/shard_map/ppermute | solution.py:90
  126.6 21.8 %shard_map.68 = f32[2048,4096]{1,0:T(8,128)} custom-call(bf16[128,2048]{1,0:T(8,128)(2,1)S(1)} %get-tuple-element.190.refs_0_, bf16[128,2048]{1,0:T(8,128)(2,1)S(1)} %get-tuple-element.194.refs_1_, bf16[128,2048]{1,0:T(8,128)(2,1)S(1)} %get-tuple-element.191.refs_2_, bf16[128,2048]{1,0:T(8,128)(2,1)S(1)} %get-tuple-element.195.refs_3_, ...), custom_call_target="tpu_custom_call" | custom-call | flops 17179869184 | bytes 33554432 | tf_op jit(solution)/shard_map/pallas_call | solution.py:46
  148.6 0.7 fusion.10
  (99 shorter events, 5.4 us)
Async XLA Ops:
  0.7 13.2 %copy-start.8 = (bf16[4096]{0:T(1024)(128)(2,1)S(1)}, bf16[4096]{0:T(1024)(128)(2,1)}, u32[]{:S(2)}) copy-start(bf16[4096]{0:T(1024)(128)(2,1)} %param.5) | copy-start | bytes 24580
  0.7 13.2 %copy-start.6 = (bf16[128,4096]{1,0:T(8,128)(2,1)S(1)}, bf16[128,4096]{1,0:T(8,128)(2,1)}, u32[]{:S(2)}) copy-start(bf16[128,4096]{1,0:T(8,128)(2,1)} %param.4) | copy-start | bytes 3145732
  2.7 19.8 %collective-permute-start.2 = (bf16[32,4096]{1,0:T(8,128)(2,1)}, bf16[32,4096]{1,0:T(8,128)(2,1)S(1)}, u32[]{:S(2)}, u32[]{:S(2)}) collective-permute-start(bf16[32,4096]{1,0:T(8,128)(2,1)} %get-tuple-element.95), channel_id=1, source_target_pairs={{0,3},{1,2},{2,1},{3,0},{4,7},{5,6},{6,5},{7,4},{8,11},{9,10},{10,... | collective-permute-start | bytes 786440 | tf_op jit(solution)/shard_map/ppermute | solution.py:90
  6.6 15.9 %collective-permute-start.1 = (bf16[32,4096]{1,0:T(8,128)(2,1)S(1)}, bf16[32,4096]{1,0:T(8,128)(2,1)S(1)}, u32[]{:S(2)}, u32[]{:S(2)}) collective-permute-start(bf16[32,4096]{1,0:T(8,128)(2,1)S(1)} %get-tuple-element.96), channel_id=1, source_target_pairs={{0,2},{1,3},{2,0},{3,1},{4,6},{5,7},{6,4},{7,5},{8,10},{9,11},{10,... | collective-permute-start | bytes 786440 | tf_op jit(solution)/shard_map/ppermute | solution.py:90
  7.1 15.4 %collective-permute-start = (bf16[32,4096]{1,0:T(8,128)(2,1)S(1)}, bf16[32,4096]{1,0:T(8,128)(2,1)}, u32[]{:S(2)}, u32[]{:S(2)}) collective-permute-start(bf16[32,4096]{1,0:T(8,128)(2,1)S(1)} %get-tuple-element.97), channel_id=1, source_target_pairs={{0,1},{1,0},{2,3},{3,2},{4,5},{5,4},{6,7},{7,6},{8,9},{9,8},{10,11... | collective-permute-start | bytes 786440 | tf_op jit(solution)/shard_map/ppermute | solution.py:90
  8.2 17.5 %copy-start.4 = (bf16[128,4096]{1,0:T(8,128)(2,1)}, bf16[128,4096]{1,0:T(8,128)(2,1)S(1)}, u32[]{:S(2)}) copy-start(bf16[128,4096]{1,0:T(8,128)(2,1)S(1)} %pad_maximum_fusion.2) | copy-start | bytes 3145732
  8.2 23.8 %collective-permute-start.7 = (bf16[128,4096]{1,0:T(8,128)(2,1)S(1)}, bf16[128,4096]{1,0:T(8,128)(2,1)}, u32[]{:S(2)}, u32[]{:S(2)}) collective-permute-start(bf16[128,4096]{1,0:T(8,128)(2,1)S(1)} %pad_maximum_fusion.2), channel_id=1, source_target_pairs={{8,16},{12,20},{16,8},{20,12},{9,17},{13,21},{17,9},{21,13},{10,18... | collective-permute-start | bytes 3145736 | tf_op jit(solution)/shard_map/ppermute | solution.py:90
  9.9 32.9 %collective-permute-start.6 = (bf16[128,4096]{1,0:T(8,128)(2,1)S(1)}, bf16[128,4096]{1,0:T(8,128)(2,1)}, u32[]{:S(2)}, u32[]{:S(2)}) collective-permute-start(bf16[128,4096]{1,0:T(8,128)(2,1)S(1)} %pad_maximum_fusion.2), channel_id=1, source_target_pairs={{0,8},{4,12},{8,0},{12,4},{16,24},{20,28},{24,16},{28,20},{1,9},{5... | collective-permute-start | bytes 3145736 | tf_op jit(solution)/shard_map/ppermute | solution.py:90
  22.6 0.7 copy-start.7
  24.6 18.2 %copy-start = (bf16[2048,256]{1,0:T(8,128)(2,1)S(1)}, bf16[2048,256]{1,0:T(8,128)(2,1)}, u32[]{:S(2)}) copy-start(bf16[2048,256]{1,0:T(8,128)(2,1)} %left) | copy-start | bytes 3145732
  27.4 20.7 %collective-permute-start.3 = (bf16[32,4224]{1,0:T(8,128)(2,1)}, bf16[32,4224]{1,0:T(8,128)(2,1)}, u32[]{:S(2)}, u32[]{:S(2)}) collective-permute-start(bf16[32,4224]{1,0:T(8,128)(2,1)} %concatenate.80), channel_id=1, source_target_pairs={{0,8},{4,12},{8,0},{12,4},{16,24},{20,28},{24,16},{28,20},{1,9},{5... | collective-permute-start | bytes 811016 | tf_op jit(solution)/shard_map/ppermute | solution.py:90
  28.9 26.3 %collective-permute-start.4 = (bf16[32,4224]{1,0:T(8,128)(2,1)}, bf16[32,4224]{1,0:T(8,128)(2,1)}, u32[]{:S(2)}, u32[]{:S(2)}) collective-permute-start(bf16[32,4224]{1,0:T(8,128)(2,1)} %concatenate.81), channel_id=1, source_target_pairs={{0,16},{4,20},{8,24},{12,28},{16,0},{20,4},{24,8},{28,12},{1,17},{... | collective-permute-start | bytes 811016 | tf_op jit(solution)/shard_map/ppermute | solution.py:90
  31.5 23.7 %collective-permute-start.5 = (bf16[32,4224]{1,0:T(8,128)(2,1)}, bf16[32,4224]{1,0:T(8,128)(2,1)}, u32[]{:S(2)}, u32[]{:S(2)}) collective-permute-start(bf16[32,4224]{1,0:T(8,128)(2,1)} %concatenate.82), channel_id=1, source_target_pairs={{0,24},{4,28},{8,16},{12,20},{16,8},{20,12},{24,0},{28,4},{1,25},{... | collective-permute-start | bytes 811016 | tf_op jit(solution)/shard_map/ppermute | solution.py:90
  42.8 1.2 copy-start.1
  56.8 2.0 %collective-permute-start.8 = (bf16[4,32,2176]{2,1,0:T(8,128)(2,1)S(1)}, bf16[4,32,2176]{2,1,0:T(8,128)(2,1)S(1)}, u32[]{:S(2)}, u32[]{:S(2)}) collective-permute-start(bf16[4,32,2176]{2,1,0:T(8,128)(2,1)S(1)} %get-tuple-element.174), channel_id=1, source_target_pairs={{0,4},{4,0},{8,12},{12,8},{16,20},{20,16},{24,28},{28,24},{1,5},{5... | collective-permute-start | bytes 1671176 | tf_op jit(solution)/shard_map/ppermute | solution.py:90
  58.8 0.8 copy-start.2
  60.7 26.9 %collective-permute-start.10 = (bf16[2,4,32,2176]{3,2,1,0:T(8,128)(2,1)}, bf16[2,4,32,2176]{3,2,1,0:T(8,128)(2,1)}, u32[]{:S(2)}, u32[]{:S(2)}) collective-permute-start(bf16[2,4,32,2176]{3,2,1,0:T(8,128)(2,1)} %pad_maximum_fusion), channel_id=1, source_target_pairs={{0,2},{1,3},{2,0},{3,1},{4,6},{5,7},{6,4},{7,5},{8,10},{9,11},{10,... | collective-permute-start | bytes 3342344 | tf_op jit(solution)/shard_map/ppermute | solution.py:90
  62.2 6.9 %collective-permute-start.11 = (bf16[128,4096]{1,0:T(8,128)(2,1)}, bf16[128,4096]{1,0:T(8,128)(2,1)}, u32[]{:S(2)}, u32[]{:S(2)}) collective-permute-start(bf16[128,4096]{1,0:T(8,128)(2,1)} %collective-permute-done.6), channel_id=1, source_target_pairs={{8,16},{12,20},{16,8},{20,12},{9,17},{13,21},{17,9},{21,13},{10,18... | collective-permute-start | bytes 3145736 | tf_op jit(solution)/shard_map/ppermute | solution.py:90
  63.9 29.4 %copy-start.5 = (bf16[128,4096]{1,0:T(8,128)(2,1)S(1)}, bf16[128,4096]{1,0:T(8,128)(2,1)}, u32[]{:S(2)}) copy-start(bf16[128,4096]{1,0:T(8,128)(2,1)} %copy-done.4) | copy-start | bytes 3145732
  63.9 40.4 %collective-permute-start.18 = (bf16[128,4096]{1,0:T(8,128)(2,1)}, bf16[128,4096]{1,0:T(8,128)(2,1)S(1)}, u32[]{:S(2)}, u32[]{:S(2)}) collective-permute-start(bf16[128,4096]{1,0:T(8,128)(2,1)} %collective-permute-done.7), channel_id=1, source_target_pairs={{8,0},{12,4},{16,24},{20,28},{9,1},{13,5},{17,25},{21,29},{10,2},{... | collective-permute-start | bytes 3145736 | tf_op jit(solution)/shard_map/ppermute | solution.py:90
  65.5 27.7 %collective-permute-start.9 = (bf16[2,4,32,2176]{3,2,1,0:T(8,128)(2,1)}, bf16[2,4,32,2176]{3,2,1,0:T(8,128)(2,1)S(1)}, u32[]{:S(2)}, u32[]{:S(2)}) collective-permute-start(bf16[2,4,32,2176]{3,2,1,0:T(8,128)(2,1)} %pad_maximum_fusion), channel_id=1, source_target_pairs={{0,1},{1,0},{2,3},{3,2},{4,5},{5,4},{6,7},{7,6},{8,9},{9,8},{10,11... | collective-permute-start | bytes 3342344 | tf_op jit(solution)/shard_map/ppermute | solution.py:90
  69.1 48.3 %collective-permute-start.15 = (bf16[128,4096]{1,0:T(8,128)(2,1)}, bf16[128,4096]{1,0:T(8,128)(2,1)S(1)}, u32[]{:S(2)}, u32[]{:S(2)}) collective-permute-start(bf16[128,4096]{1,0:T(8,128)(2,1)} %collective-permute-done.11), channel_id=1, source_target_pairs={{8,0},{12,4},{16,24},{20,28},{9,1},{13,5},{17,25},{21,29},{10,2},{... | collective-permute-start | bytes 3145736 | tf_op jit(solution)/shard_map/ppermute | solution.py:90
  88.7 15.3 %collective-permute-start.12 = (bf16[4,32,2176]{2,1,0:T(8,128)(2,1)S(1)}, bf16[4,32,2176]{2,1,0:T(8,128)(2,1)S(1)}, u32[]{:S(2)}, u32[]{:S(2)}) collective-permute-start(bf16[4,32,2176]{2,1,0:T(8,128)(2,1)S(1)} %slice_bitcast_fusion.1), channel_id=1, source_target_pairs={{0,1},{1,0},{2,3},{3,2},{4,5},{5,4},{6,7},{7,6},{8,9},{9,8},{10,11... | collective-permute-start | bytes 1671176 | tf_op jit(solution)/shard_map/ppermute | solution.py:90
  93.3 20.5 %collective-permute-start.16 = (bf16[128,4096]{1,0:T(8,128)(2,1)S(1)}, bf16[128,4096]{1,0:T(8,128)(2,1)S(1)}, u32[]{:S(2)}, u32[]{:S(2)}) collective-permute-start(bf16[128,4096]{1,0:T(8,128)(2,1)S(1)} %copy-done.5), channel_id=1, source_target_pairs={{0,4},{4,0},{8,12},{12,8},{16,20},{20,16},{24,28},{28,24},{1,5},{5... | collective-permute-start | bytes 3145736 | tf_op jit(solution)/shard_map/ppermute | solution.py:90
  95.1 15.1 %collective-permute-start.13 = (bf16[4,32,2176]{2,1,0:T(8,128)(2,1)S(1)}, bf16[4,32,2176]{2,1,0:T(8,128)(2,1)S(1)}, u32[]{:S(2)}, u32[]{:S(2)}) collective-permute-start(bf16[4,32,2176]{2,1,0:T(8,128)(2,1)S(1)} %slice_bitcast_fusion), channel_id=1, source_target_pairs={{0,2},{1,3},{2,0},{3,1},{4,6},{5,7},{6,4},{7,5},{8,10},{9,11},{10,... | collective-permute-start | bytes 1671176 | tf_op jit(solution)/shard_map/ppermute | solution.py:90
  104.1 9.7 %collective-permute-start.17 = (bf16[128,4096]{1,0:T(8,128)(2,1)}, bf16[128,4096]{1,0:T(8,128)(2,1)S(1)}, u32[]{:S(2)}, u32[]{:S(2)}) collective-permute-start(bf16[128,4096]{1,0:T(8,128)(2,1)} %collective-permute-done.6), channel_id=1, source_target_pairs={{0,4},{4,0},{8,12},{12,8},{16,20},{20,16},{24,28},{28,24},{1,5},{5... | collective-permute-start | bytes 3145736 | tf_op jit(solution)/shard_map/ppermute | solution.py:90
  104.3 1.1 copy-start.3
  104.7 9.1 %collective-permute-start.19 = (bf16[128,4096]{1,0:T(8,128)(2,1)S(1)}, bf16[128,4096]{1,0:T(8,128)(2,1)S(1)}, u32[]{:S(2)}, u32[]{:S(2)}) collective-permute-start(bf16[128,4096]{1,0:T(8,128)(2,1)S(1)} %get-tuple-element.74), channel_id=1, source_target_pairs={{0,4},{4,0},{8,12},{12,8},{16,20},{20,16},{24,28},{28,24},{1,5},{5... | collective-permute-start | bytes 3145736 | tf_op jit(solution)/shard_map/ppermute | solution.py:90
  113.3 5.1 %collective-permute-start.14 = (f32[4,128,512]{2,1,0:T(8,128)S(1)}, f32[4,128,512]{2,1,0:T(8,128)S(1)}, u32[]{:S(2)}, u32[]{:S(2)}) collective-permute-start(f32[4,128,512]{2,1,0:T(8,128)S(1)} %pad_maximum_fusion.3), channel_id=1, source_target_pairs={{0,4},{4,0},{8,12},{12,8},{16,20},{20,16},{24,28},{28,24},{1,5},{5... | collective-permute-start | bytes 3145736 | tf_op jit(solution)/shard_map/ppermute | solution.py:90
  117.9 8.5 %collective-permute-start.20 = (bf16[128,4096]{1,0:T(8,128)(2,1)S(1)}, bf16[128,4096]{1,0:T(8,128)(2,1)S(1)}, u32[]{:S(2)}, u32[]{:S(2)}) collective-permute-start(bf16[128,4096]{1,0:T(8,128)(2,1)S(1)} %get-tuple-element.72), channel_id=1, source_target_pairs={{0,4},{4,0},{8,12},{12,8},{16,20},{20,16},{24,28},{28,24},{1,5},{5... | collective-permute-start | bytes 3145736 | tf_op jit(solution)/shard_map/ppermute | solution.py:90
  118.7 29.8 %collective-permute-start.23 = (f32[128,512]{1,0:T(8,128)S(1)}, f32[128,512]{1,0:T(8,128)S(1)}, u32[]{:S(2)}, u32[]{:S(2)}) collective-permute-start(f32[128,512]{1,0:T(8,128)S(1)} %get-tuple-element.92), channel_id=1, source_target_pairs={{0,24},{4,28},{8,16},{12,20},{16,8},{20,12},{24,0},{28,4},{1,25},{... | collective-permute-start | bytes 786440 | tf_op jit(solution)/shard_map/ppermute | solution.py:90
  121.3 27.2 %collective-permute-start.22 = (f32[128,512]{1,0:T(8,128)S(1)}, f32[128,512]{1,0:T(8,128)S(1)}, u32[]{:S(2)}, u32[]{:S(2)}) collective-permute-start(f32[128,512]{1,0:T(8,128)S(1)} %get-tuple-element.93), channel_id=1, source_target_pairs={{0,16},{4,20},{8,24},{12,28},{16,0},{20,4},{24,8},{28,12},{1,17},{... | collective-permute-start | bytes 786440 | tf_op jit(solution)/shard_map/ppermute | solution.py:90
  126.4 22.1 %collective-permute-start.21 = (f32[128,512]{1,0:T(8,128)S(1)}, f32[128,512]{1,0:T(8,128)S(1)}, u32[]{:S(2)}, u32[]{:S(2)}) collective-permute-start(f32[128,512]{1,0:T(8,128)S(1)} %get-tuple-element.94), channel_id=1, source_target_pairs={{0,8},{4,12},{8,0},{12,4},{16,24},{20,28},{24,16},{28,20},{1,9},{5... | collective-permute-start | bytes 786440 | tf_op jit(solution)/shard_map/ppermute | solution.py:90

commit v3 on v2

--- a/solution.py
+++ b/solution.py
@@ -21,40 +21,44 @@
 SIDES = {k: [(t, t ^ k) for t in range(4)] for k in (1, 2, 3)}
 
 
-def tile_kernel(scale, slots, *refs):
-    rows, cols, out = refs[:slots], refs[slots : 2 * slots], refs[2 * slots]
-    together = 2 if slots % 2 == 0 else 1
-    groups = [slice(i, i + together) for i in range(0, slots, together)]
-    turned = [jnp.concatenate([row[...] for row in rows[g]]).T for g in groups]
+def tile_kernel(scale, quarters, *refs):
+    rows, cols, out = refs[:quarters], refs[quarters:-1], refs[-1]
+    slots = rows[0].shape[0]
+    each = len(cols) // slots
+    turned = [jnp.concatenate([row[j] for row in rows]).T for j in range(slots)]
     width = out.shape[1]
     step = min(width, 1024)
     for left in range(0, width, step):
         total = None
-        for row, group in zip(turned, groups):
-            col = jnp.concatenate([c[:, left : left + step] for c in cols[group]])
+        for j, row in enumerate(turned):
+            group = cols[each * j : each * (j + 1)]
+            col = jnp.concatenate([c[:, left : left + step] for c in group])
             product = jnp.dot(row, col, preferred_element_type=jnp.float32)
             total = product if total is None else total + product
         out[:, left : left + step] = total * scale
 
 
 def hessian_tile(rows, cols, scale):
-    slots = len(rows)
-    depth, height = rows[0].shape
-    width = cols[0].shape[1]
+    _, slots, depth, height = rows[0][0].shape
+    col_depth, width = cols[0].shape
     block = 256
-    flops = 2 * slots * depth * height * width
     return pl.pallas_call(
-        functools.partial(tile_kernel, scale, slots),
+        functools.partial(tile_kernel, scale, len(rows)),
         grid=(height // block,),
-        in_specs=[pl.BlockSpec((depth, block), lambda i: (0, i))] * slots
-        + [pl.BlockSpec((depth, width), lambda i: (0, 0), pipeline_mode=pl.Buffered(1))] * slots,
+        in_specs=[
+            pl.BlockSpec((None, slots, depth, block), lambda i, p=p: (p, 0, 0, i)) for _, p in rows
+        ]
+        + [pl.BlockSpec((col_depth, width), lambda i: (0, 0), pipeline_mode=pl.Buffered(1))]
+        * len(cols),
         out_specs=pl.BlockSpec((block, width), lambda i: (i, 0)),
         out_shape=jax.ShapeDtypeStruct((height, width), jnp.float32),
         compiler_params=pltpu.CompilerParams(vmem_limit_bytes=40 << 20),
         cost_estimate=pl.CostEstimate(
-            flops=flops, bytes_accessed=4 * height * width, transcendentals=0
+            flops=2 * len(cols) * col_depth * height * width,
+            bytes_accessed=4 * height * width,
+            transcendentals=0,
         ),
-    )(*rows, *cols)
+    )(*(array for array, _ in rows), *cols)
 
 
 def pair_kernel(left, right, out):
@@ -113,13 +117,14 @@
     def norm(block, gain, scale):
         return (block.astype(jnp.float32) * gain * scale).astype(jnp.bfloat16)
 
-    rest = lax.dynamic_slice_in_dim(scale, t * quarter, quarter)[:, None]
-    quarter_scale, thirds = rest, []
+    quarter_scale = lax.dynamic_slice_in_dim(scale, t * quarter, quarter)[:, None]
+    rest = reorder(scale).reshape(4, quarter).T
+    thirds = []
     for _ in range(3):
         part = lax.reduce_precision(rest, 8, 7)
         rest = rest - part
         thirds.append(part.astype(jnp.bfloat16))
-    thirds = jnp.concatenate(thirds + [jnp.zeros((quarter, 125), jnp.bfloat16)], axis=1)
+    thirds = jnp.concatenate(thirds + [jnp.zeros((quarter, 116), jnp.bfloat16)], axis=1)
 
     def choose(which):
         piece = jnp.where(
@@ -140,48 +145,43 @@
     )
     weights = side_by_side(key_weight, value_weight)
     *landed, weights = lax.optimization_barrier((*landed, weights))
-    landed = jnp.stack(landed)
-
     def share(which):
-        features = lax.dynamic_slice_in_dim(landed, which * half, half, axis=2)
-        return jnp.concatenate([features, landed[:, :, width:]], axis=2)
-
-    mine = share(core)
-    other = move(share(1 - core), CORES)
-    group = jnp.stack([mine, other])
+        return jnp.stack(
+            [lax.dynamic_slice_in_dim(block, which * half, half, axis=1) for block in landed]
+        )
+
+    group = jnp.stack([share(core), move(share(1 - core), CORES)])
     from_x = move(group, SIDES[1], "tp")
     from_y = move(group, SIDES[2], "tp")
     last = move(beyond, OUTWARD)
-    far_mine = move(from_y[0], SIDES[1], "tp")
-    far_other = move(from_x[1], SIDES[2], "tp")
     from_x, from_y, turned, near, beyond = lax.optimization_barrier(
         (from_x, from_y, turned, near, beyond)
     )
-    quarters = [
-        [mine, from_x[0], from_y[0], far_mine],
-        [other, from_x[1], from_y[1], far_other],
-    ]
+    far = [move(from_y[0], SIDES[1], "tp"), move(from_x[1], SIDES[2], "tp")]
+    sent = jnp.stack([block[:, width:].astype(jnp.float32) for block in landed])
+    lane = lax.broadcasted_iota(jnp.int32, sent.shape, 2)
+    own_scales = jnp.concatenate(
+        [jnp.sum(jnp.where((lane % 4 == k) & (lane < 12), sent, 0.0), axis=2) for k in range(4)],
+        axis=1,
+    )
+    scales = [own_scales, move(own_scales, CORES)]
     blocks = [turned, near, jnp.where(middle, beyond, outer)]
     twins = [move(block, CORES) for block in blocks]
 
-    def row_part(j, p):
-        return jnp.concatenate([g[j, :, :half] for g in quarters[p]])
-
-    sent_scales = [
-        [jnp.sum(g[:, :, half:].astype(jnp.float32), axis=2) for g in quarters[p]]
+    def col_parts(j):
+        return [norm((blocks, twins)[p][j], col_gain, scales[p][j][:, None]) for p in range(2)]
+
+    def project(block):
+        flat = block.reshape(-1, half)
+        product = jnp.dot(flat, weights, preferred_element_type=jnp.float32)
+        return product.reshape(*block.shape[:-1], -1)
+
+    parts = [project(block) for block in (group, from_x, from_y)]
+    parts = [
+        jnp.stack([part[p] for part in parts] + [project(far[p])], axis=1).reshape(4, count, -1)
         for p in range(2)
     ]
-    scales = [jnp.concatenate(sent_scales[p], axis=1) for p in range(2)]
-
-    def col_parts(j):
-        return [norm((blocks, twins)[p][j], col_gain, scales[p][j][:, None]) for p in range(2)]
-
-    rows = [[row_part(j, p) for p in range(2)] for j in range(4)]
-    parts = [
-        jnp.dot(jnp.concatenate(row), weights, preferred_element_type=jnp.float32) for row in rows
-    ]
-    own = jnp.stack([part[:count] for part in parts])
-    sums = own + move(jnp.stack([part[count:] for part in parts]), CORES)
+    sums = parts[0] + move(parts[1], CORES)
     homes = [move(sums[j], FLIPS[j]) for j in (1, 2, 3)]
 
     cols = [col_parts(j) for j in range(3)]
@@ -189,7 +189,9 @@
     blocks.append(jnp.where(middle, across, last))
     twins.append(move(blocks[3], CORES))
     cols.append(col_parts(3))
-    hessian = hessian_tile(sum(rows, []), sum(cols, []), 2.0 / total_tokens)
+    rows = [(block, p) for p in range(2) for block in (group, from_x, from_y, far[p][None])]
+    rows = [(block, min(p, block.shape[0] - 1)) for block, p in rows]
+    hessian = hessian_tile(rows, sum(cols, []), 2.0 / total_tokens)
 
     hessian, homes = lax.optimization_barrier((hessian, homes))
     projected = sums[0] + homes[0] + homes[1] + homes[2]
@@ -214,7 +216,7 @@
     part = jnp.dot(rows, weights, preferred_element_type=jnp.float32)
     projected = lax.psum_scatter(part, "fsdp", scatter_dimension=0, tiled=True).astype(jnp.bfloat16)
     columns = key_weight.shape[1]
-    hessian = hessian_tile([rows], [cols], 2.0 / total_tokens)
+    hessian = hessian_tile([(rows[None, None], 0)], [cols], 2.0 / total_tokens)
     return projected[:, :columns], projected[:, columns:], hessian
 
 

time: 150 us -> 146 us (0.973)
  starting transfers between devices: 32.3 us -> 28.5 us
  other arithmetic: 12 us -> 8.8 us
  waiting for transfers between devices: 57.6 us -> 59.6 us
    concatenate x4, local copies, waits for them, and re-layouts: 2.5 us -> 6.41 us  [choose(): return jnp.concatenate([norm(piece, gain, quarter_scale), thirds], axis=1)]
    squeeze x11 -> x2, local copies, waits for them, and re-layouts: 3.93 us -> 0.08 us  [slice_body(): far = [move(from_y[0], SIDES[1], 'tp'), move(from_x[1], SIDES[2], 'tp')]]
    ppermute x24 -> x25, starting transfers between devices: 32.3 us -> 28.5 us  [move(): return lax.ppermute(x, axis, pairs)]
    another operation x2 -> x6, local copies, waits for them, and re-layouts: 0.14 us -> 3.73 us  [the longest x2 2.15 us: share(): jnp.stack([lax.dynamic_slice_in_dim(block, which * half, half, axis=1) fo...]
    unnamed x27 -> x16, local copies, waits for them, and re-layouts: 3.03 us -> 0.46 us
    another operation x4 -> x5, other arithmetic: 2.54 us -> 0.38 us  [the longest x2 0.17 us: slice_body(): group = jnp.stack([share(core), move(share(1 - core), CORES)])]
    ppermute x24 -> x25, waiting for transfers between devices: 57.6 us -> 59.6 us  [move(): return lax.ppermute(x, axis, pairs)]
  transfers between devices with their start and end apart: 24 -> 25, of which waited for: 9 -> 11; matrix products, arithmetic and copies ran while one was open for 13% -> 13% of each run, Pallas kernels for 15% -> 15%
where the time goes in v3:
time: 146 us; the launch traced here: 145 us
  waiting for transfers between devices  59.6 us (41%)
  starting transfers between devices  28.5 us (20%)
  Pallas kernels  22.1 us (15%)
  local copies, waits for them, and re-layouts  13.2 us (9%)
  blocking collectives  8.95 us (6%)
  other arithmetic  8.8 us (6%)
  matrix products  2.98 us (2%)
    ppermute x25, waiting for transfers between devices, move(): return lax.ppermute(x, axis, pairs)  59.6 us
    ppermute x25, starting transfers between devices, move(): return lax.ppermute(x, axis, pairs)  28.5 us
    pallas_call x1, Pallas kernels, hessian_tile(): pl.pallas_call(functools.partial(tile_kernel, scale, len(rows)), grid=(he...  21.9 us
    all_gather x1, blocking collectives, slice_body(): notes = lax.all_gather(note, 'tp')  8.95 us
    convert_element_type x6, other arithmetic, norm(): return (block.astype(jnp.float32) * gain * scale).astype(jnp.bfloat16)  7.37 us
    concatenate x4, local copies, waits for them, and re-layouts, choose(): return jnp.concatenate([norm(piece, gain, quarter_scale), thirds], axis=1)  6.41 us
    dot_general x5, matrix products, project(): product = jnp.dot(flat, weights, preferred_element_type=jnp.float32)  2.98 us
  transfers between devices with their start and end apart: 25, of which 11 were waited for; matrix products, arithmetic and copies ran while one was open for 13% of the time, Pallas kernels for 15%

profile of v3, /device:TPU:0, one launch (start us, length us, event | category | flops | bytes accessed | tf_op | source)
XLA Modules:
  0.0 145.4 jit_solution(7689528383359769516)
XLA Ops:
  0.7 1.4 constant_dynamic-slice_fusion.8
  2.0 4.0 %collective-permute-start.2 = (bf16[32,4096]{1,0:T(8,128)(2,1)S(1)}, bf16[32,4096]{1,0:T(8,128)(2,1)S(1)}, u32[]{:S(2)}, u32[]{:S(2)}) collective-permute-start(bf16[32,4096]{1,0:T(8,128)(2,1)S(1)} %get-tuple-element.77), channel_id=1, source_target_pairs={{0,3},{1,2},{2,1},{3,0},{4,7},{5,6},{6,5},{7,4},{8,11},{9,10},{10,... | collective-permute-start | bytes 786440 | tf_op jit(solution)/shard_map/ppermute | solution.py:94
  6.0 0.5 collective-permute-start.1
  6.7 1.6 %collective-permute-start.7 = (bf16[128,4096]{1,0:T(8,128)(2,1)S(1)}, bf16[128,4096]{1,0:T(8,128)(2,1)}, u32[]{:S(2)}, u32[]{:S(2)}) collective-permute-start(bf16[128,4096]{1,0:T(8,128)(2,1)S(1)} %pad_maximum_fusion), channel_id=1, source_target_pairs={{8,16},{12,20},{16,8},{20,12},{9,17},{13,21},{17,9},{21,13},{10,18... | collective-permute-start | bytes 3145736 | tf_op jit(solution)/shard_map/ppermute | solution.py:94
  8.4 3.9 %collective-permute-start.6 = (bf16[128,4096]{1,0:T(8,128)(2,1)S(1)}, bf16[128,4096]{1,0:T(8,128)(2,1)}, u32[]{:S(2)}, u32[]{:S(2)}) collective-permute-start(bf16[128,4096]{1,0:T(8,128)(2,1)S(1)} %pad_maximum_fusion), channel_id=1, source_target_pairs={{0,8},{4,12},{8,0},{12,4},{16,24},{20,28},{24,16},{28,20},{1,9},{5... | collective-permute-start | bytes 3145736 | tf_op jit(solution)/shard_map/ppermute | solution.py:94
  12.7 9.0 %all-gather.1 = f32[4,1,4224]{2,1,0:T(1,128)S(1)} all-gather(f32[1,1,4224]{2,1,0:T(1,128)S(1)} %reshape.68), channel_id=2, replica_groups=mesh['fsdp'=8,'tp'=4] {'tp'}, dimensions={0}, use_global_device_ids=true | all-gather | bytes 84480 | tf_op jit(solution)/shard_map/all_gather | solution.py:110
  22.6 1.2 multiply_convert_fusion.8
  23.9 1.9 %concatenate.37 = bf16[32,4224]{1,0:T(8,128)(2,1)} concatenate(bf16[32,4096]{1,0:T(8,128)(2,1)} %get-tuple-element.71, bf16[32,4]{1,0:T(8,128)(2,1)S(1)} %get-tuple-element.112, bf16[32,4]{1,0:T(8,128)(2,1)S(1)} %get-tuple-element.111, bf16[32,4]{1,0:T(8,128)(2,1)S(1)} %get-tuple-element.110, bf16[32,116]{1,0:T(8,128)(2,1)S(1)} %broadcast_in_dim.18), dimensions={1} | concatenate | bytes 540672 | tf_op jit(solution)/shard_map/concatenate | solution.py:136
  25.8 1.7 %concatenate.36 = bf16[32,4224]{1,0:T(8,128)(2,1)} concatenate(bf16[32,4096]{1,0:T(8,128)(2,1)} %get-tuple-element.72, bf16[32,4]{1,0:T(8,128)(2,1)S(1)} %get-tuple-element.112, bf16[32,4]{1,0:T(8,128)(2,1)S(1)} %get-tuple-element.111, bf16[32,4]{1,0:T(8,128)(2,1)S(1)} %get-tuple-element.110, bf16[32,116]{1,0:T(8,128)(2,1)S(1)} %broadcast_in_dim.18), dimensions={1} | concatenate | bytes 540672 | tf_op jit(solution)/shard_map/concatenate | solution.py:136
  27.5 1.7 %concatenate.35 = bf16[32,4224]{1,0:T(8,128)(2,1)} concatenate(bf16[32,4096]{1,0:T(8,128)(2,1)} %get-tuple-element.73, bf16[32,4]{1,0:T(8,128)(2,1)S(1)} %get-tuple-element.112, bf16[32,4]{1,0:T(8,128)(2,1)S(1)} %get-tuple-element.111, bf16[32,4]{1,0:T(8,128)(2,1)S(1)} %get-tuple-element.110, bf16[32,116]{1,0:T(8,128)(2,1)S(1)} %broadcast_in_dim.18), dimensions={1} | concatenate | bytes 540672 | tf_op jit(solution)/shard_map/concatenate | solution.py:136
  29.2 1.6 %collective-permute-start.3 = (bf16[32,4224]{1,0:T(8,128)(2,1)}, bf16[32,4224]{1,0:T(8,128)(2,1)}, u32[]{:S(2)}, u32[]{:S(2)}) collective-permute-start(bf16[32,4224]{1,0:T(8,128)(2,1)} %concatenate.35), channel_id=1, source_target_pairs={{0,8},{4,12},{8,0},{12,4},{16,24},{20,28},{24,16},{28,20},{1,9},{5... | collective-permute-start | bytes 811016 | tf_op jit(solution)/shard_map/ppermute | solution.py:94
  30.8 2.6 %collective-permute-start.4 = (bf16[32,4224]{1,0:T(8,128)(2,1)}, bf16[32,4224]{1,0:T(8,128)(2,1)}, u32[]{:S(2)}, u32[]{:S(2)}) collective-permute-start(bf16[32,4224]{1,0:T(8,128)(2,1)} %concatenate.36), channel_id=1, source_target_pairs={{0,16},{4,20},{8,24},{12,28},{16,0},{20,4},{24,8},{28,12},{1,17},{... | collective-permute-start | bytes 811016 | tf_op jit(solution)/shard_map/ppermute | solution.py:94
  33.6 1.8 %multiply_convert_fusion.11 = bf16[32,4096]{1,0:T(8,128)(2,1)} fusion(f32[32]{0:T(128)S(1)} %get-tuple-element.124, f32[4096]{0:T(1024)S(1)} %bitcast.130, bf16[32,4096]{1,0:T(8,128)(2,1)S(1)} %get-tuple-element.33, bf16[32,4096]{1,0:T(8,128)(2,1)} %copy-done.5, bf16[32,4096]{1,0:T(8,128)(2,1)} %copy-done.4, bf16[32,4096]{1,0:T(8,128)(2,1)} %copy-done.3, ...), kind=kLoop, calls=%fused_computation.29 | loop fusion | flops 917504 | bytes 1327235 | tf_op jit(solution)/shard_map/convert_element_type | solution.py:118
  35.5 1.0 concatenate.34
  36.5 5.4 %collective-permute-done.6 = bf16[128,4096]{1,0:T(8,128)(2,1)} collective-permute-done((bf16[128,4096]{1,0:T(8,128)(2,1)S(1)}, bf16[128,4096]{1,0:T(8,128)(2,1)}, u32[]{:S(2)}, u32[]{:S(2)}) %collective-permute-start.6) | collective-permute-done | bytes 1048608 | tf_op jit(solution)/shard_map/ppermute | solution.py:94
  42.1 4.4 %collective-permute-done.3 = bf16[32,4224]{1,0:T(8,128)(2,1)} collective-permute-done((bf16[32,4224]{1,0:T(8,128)(2,1)}, bf16[32,4224]{1,0:T(8,128)(2,1)}, u32[]{:S(2)}, u32[]{:S(2)}) %collective-permute-start.3) | collective-permute-done | bytes 270368 | tf_op jit(solution)/shard_map/ppermute | solution.py:94
  46.4 6.6 %collective-permute-done.4 = bf16[32,4224]{1,0:T(8,128)(2,1)} collective-permute-done((bf16[32,4224]{1,0:T(8,128)(2,1)}, bf16[32,4224]{1,0:T(8,128)(2,1)}, u32[]{:S(2)}, u32[]{:S(2)}) %collective-permute-start.4) | collective-permute-done | bytes 270368 | tf_op jit(solution)/shard_map/ppermute | solution.py:94
  53.0 0.7 slice_bitcast_fusion.8
  53.7 1.0 dynamic-slice_bitcast_fusion.6
  54.8 1.1 dynamic-slice_bitcast_fusion.4
  56.1 0.7 collective-permute-start.11
  56.8 0.7 slice_bitcast_fusion.6
  58.1 1.5 %collective-permute-start.10 = (bf16[2,4,32,2048]{3,2,1,0:T(8,128)(2,1)S(1)}, bf16[2,4,32,2048]{3,2,1,0:T(8,128)(2,1)S(1)}, u32[]{:S(2)}, u32[]{:S(2)}) collective-permute-start(bf16[2,4,32,2048]{3,2,1,0:T(8,128)(2,1)S(1)} %pad_maximum_fusion.1.refs_0_.refs_4_), channel_id=1, source_target_pairs={{0,2},{1,3},{2,0},{3,1},{4,6},{5,7},{6,4},{7,5},{8,10},{9,11},{10,... | collective-permute-start | bytes 3145736 | tf_op jit(solution)/shard_map/ppermute | solution.py:94
  59.6 1.5 %collective-permute-start.9 = (bf16[2,4,32,2048]{3,2,1,0:T(8,128)(2,1)S(1)}, bf16[2,4,32,2048]{3,2,1,0:T(8,128)(2,1)S(1)}, u32[]{:S(2)}, u32[]{:S(2)}) collective-permute-start(bf16[2,4,32,2048]{3,2,1,0:T(8,128)(2,1)S(1)} %pad_maximum_fusion.1.refs_0_.refs_4_), channel_id=1, source_target_pairs={{0,1},{1,0},{2,3},{3,2},{4,5},{5,4},{6,7},{7,6},{8,9},{9,8},{10,11... | collective-permute-start | bytes 3145736 | tf_op jit(solution)/shard_map/ppermute | solution.py:94
  61.2 1.3 collective-permute-start.19
  62.5 0.7 fusion.29
  63.2 1.5 %collective-permute-start.15 = (bf16[128,4096]{1,0:T(8,128)(2,1)S(1)}, bf16[128,4096]{1,0:T(8,128)(2,1)S(1)}, u32[]{:S(2)}, u32[]{:S(2)}) collective-permute-start(bf16[128,4096]{1,0:T(8,128)(2,1)S(1)} %collective-permute-done.11), channel_id=1, source_target_pairs={{8,0},{12,4},{16,24},{20,28},{9,1},{13,5},{17,25},{21,29},{10,2},{... | collective-permute-start | bytes 3145736 | tf_op jit(solution)/shard_map/ppermute | solution.py:94
  64.7 18.8 %collective-permute-done.10.refs_2_.refs_6_ = bf16[2,4,32,2048]{3,2,1,0:T(8,128)(2,1)S(1)} collective-permute-done((bf16[2,4,32,2048]{3,2,1,0:T(8,128)(2,1)S(1)}, bf16[2,4,32,2048]{3,2,1,0:T(8,128)(2,1)S(1)}, u32[]{:S(2)}, u32[]{:S(2)}) %collective-permute-start.10) | collective-permute-done | bytes 1048608 | tf_op jit(solution)/shard_map/ppermute | solution.py:94
  83.5 1.2 collective-permute-done.9.refs_1_.refs_5_
  84.7 0.7 collective-permute-start.13
  85.3 0.7 fusion.31
  86.1 0.7 fusion.30
  86.8 7.4 %collective-permute-done.19 = bf16[128,4096]{1,0:T(8,128)(2,1)S(1)} collective-permute-done((bf16[128,4096]{1,0:T(8,128)(2,1)}, bf16[128,4096]{1,0:T(8,128)(2,1)S(1)}, u32[]{:S(2)}, u32[]{:S(2)}) %collective-permute-start.19) | collective-permute-done | bytes 1048608 | tf_op jit(solution)/shard_map/ppermute | solution.py:94
  94.2 0.4 multiply_convert_fusion.3
  94.8 0.5 collective-permute-start.16
  95.4 2.3 %collective-permute-done.13 = bf16[4,32,2048]{2,1,0:T(8,128)(2,1)S(1)} collective-permute-done((bf16[4,32,2048]{2,1,0:T(8,128)(2,1)S(1)}, bf16[4,32,2048]{2,1,0:T(8,128)(2,1)S(1)}, u32[]{:S(2)}, u32[]{:S(2)}) %collective-permute-start.13) | collective-permute-done | bytes 524320 | tf_op jit(solution)/shard_map/ppermute | solution.py:94
  97.7 1.5 %collective-permute-start.12 = (bf16[4,32,2048]{2,1,0:T(8,128)(2,1)S(1)}, bf16[4,32,2048]{2,1,0:T(8,128)(2,1)S(1)}, u32[]{:S(2)}, u32[]{:S(2)}) collective-permute-start(bf16[4,32,2048]{2,1,0:T(8,128)(2,1)S(1)} %slice_bitcast_fusion.1), channel_id=1, source_target_pairs={{0,1},{1,0},{2,3},{3,2},{4,5},{5,4},{6,7},{7,6},{8,9},{9,8},{10,11... | collective-permute-start | bytes 1572872 | tf_op jit(solution)/shard_map/ppermute | solution.py:94
  99.2 0.4 fusion.7
  99.9 0.5 collective-permute-done.16
  100.6 3.2 %multiply_convert_fusion.2 = (bf16[128,4096]{1,0:T(8,128)(2,1)S(1)}, bf16[128,4096]{1,0:T(8,128)(2,1)S(1)}, bf16[128,4096]{1,0:T(8,128)(2,1)S(1)}, bf16[128,4096]{1,0:T(8,128)(2,1)S(1)}, bf16[128,4096]{1,0:T(8,128)(2,1)S(1)}) fusion(bf16[128,4096]{1,0:T(8,128)(2,1)S(1)} %collective-permute-done.20, f32[128]{0:T(128)S(1)} %get-tuple-element.114, ...), kind=kLoop, calls=%fused_computation.6 | loop fusion | flops 10485760 | bytes 10504704 | tf_op jit(solution)/shard_map/convert_element_type | solution.py:118
  103.8 12.7 %collective-permute-done.15 = bf16[128,4096]{1,0:T(8,128)(2,1)S(1)} collective-permute-done((bf16[128,4096]{1,0:T(8,128)(2,1)S(1)}, bf16[128,4096]{1,0:T(8,128)(2,1)S(1)}, u32[]{:S(2)}, u32[]{:S(2)}) %collective-permute-start.15) | collective-permute-done | bytes 1048608 | tf_op jit(solution)/shard_map/ppermute | solution.py:94
  116.5 0.4 multiply_convert_fusion.1
  117.0 0.4 fusion.4
  118.0 1.4 collective-permute-start.24
  119.4 0.9 collective-permute-start.23
  120.3 2.2 %collective-permute-start.22 = (f32[128,512]{1,0:T(8,128)S(1)}, f32[128,512]{1,0:T(8,128)S(1)}, u32[]{:S(2)}, u32[]{:S(2)}) collective-permute-start(f32[128,512]{1,0:T(8,128)S(1)} %get-tuple-element.76), channel_id=1, source_target_pairs={{0,8},{4,12},{8,0},{12,4},{16,24},{20,28},{24,16},{28,20},{1,9},{5... | collective-permute-start | bytes 786440 | tf_op jit(solution)/shard_map/ppermute | solution.py:94
  122.7 21.9 %shard_map.68 = f32[2048,4096]{1,0:T(8,128)} custom-call(bf16[2,4,32,2048]{3,2,1,0:T(8,128)(2,1)S(1)} %pad_maximum_fusion.1.refs_0_.refs_4_, bf16[2,4,32,2048]{3,2,1,0:T(8,128)(2,1)S(1)} %collective-permute-done.9.refs_1_.refs_5_, bf16[2,4,32,2048]{3,2,1,0:T(8,128)(2,1)S(1)} %collective-permute-done.10.refs_2_.refs_6_, ...), custom_call_target="tpu_custom_call" | custom-call | flops 17179869184 | bytes 33554432 | tf_op jit(solution)/shard_map/pallas_call | solution.py:45
  144.8 0.7 fusion.27
  (79 shorter events, 4.3 us)
Async XLA Ops:
  0.7 11.6 %copy-start.2 = (bf16[128,4096]{1,0:T(8,128)(2,1)S(1)}, bf16[128,4096]{1,0:T(8,128)(2,1)}, u32[]{:S(2)}) copy-start(bf16[128,4096]{1,0:T(8,128)(2,1)} %param.4) | copy-start | bytes 3145732
  2.0 10.5 %copy-start.6 = (bf16[4096]{0:T(1024)(128)(2,1)S(1)}, bf16[4096]{0:T(1024)(128)(2,1)}, u32[]{:S(2)}) copy-start(bf16[4096]{0:T(1024)(128)(2,1)} %param.5) | copy-start | bytes 24580
  2.0 19.7 %collective-permute-start.2 = (bf16[32,4096]{1,0:T(8,128)(2,1)S(1)}, bf16[32,4096]{1,0:T(8,128)(2,1)S(1)}, u32[]{:S(2)}, u32[]{:S(2)}) collective-permute-start(bf16[32,4096]{1,0:T(8,128)(2,1)S(1)} %get-tuple-element.77), channel_id=1, source_target_pairs={{0,3},{1,2},{2,1},{3,0},{4,7},{5,6},{6,5},{7,4},{8,11},{9,10},{10,... | collective-permute-start | bytes 786440 | tf_op jit(solution)/shard_map/ppermute | solution.py:94
  6.0 15.8 %collective-permute-start.1 = (bf16[32,4096]{1,0:T(8,128)(2,1)S(1)}, bf16[32,4096]{1,0:T(8,128)(2,1)S(1)}, u32[]{:S(2)}, u32[]{:S(2)}) collective-permute-start(bf16[32,4096]{1,0:T(8,128)(2,1)S(1)} %get-tuple-element.78), channel_id=1, source_target_pairs={{0,2},{1,3},{2,0},{3,1},{4,6},{5,7},{6,4},{7,5},{8,10},{9,11},{10,... | collective-permute-start | bytes 786440 | tf_op jit(solution)/shard_map/ppermute | solution.py:94
  6.5 15.3 %collective-permute-start = (bf16[32,4096]{1,0:T(8,128)(2,1)S(1)}, bf16[32,4096]{1,0:T(8,128)(2,1)S(1)}, u32[]{:S(2)}, u32[]{:S(2)}) collective-permute-start(bf16[32,4096]{1,0:T(8,128)(2,1)S(1)} %get-tuple-element.79), channel_id=1, source_target_pairs={{0,1},{1,0},{2,3},{3,2},{4,5},{5,4},{6,7},{7,6},{8,9},{9,8},{10,11... | collective-permute-start | bytes 786440 | tf_op jit(solution)/shard_map/ppermute | solution.py:94
  6.7 29.8 %collective-permute-start.7 = (bf16[128,4096]{1,0:T(8,128)(2,1)S(1)}, bf16[128,4096]{1,0:T(8,128)(2,1)}, u32[]{:S(2)}, u32[]{:S(2)}) collective-permute-start(bf16[128,4096]{1,0:T(8,128)(2,1)S(1)} %pad_maximum_fusion), channel_id=1, source_target_pairs={{8,16},{12,20},{16,8},{20,12},{9,17},{13,21},{17,9},{21,13},{10,18... | collective-permute-start | bytes 3145736 | tf_op jit(solution)/shard_map/ppermute | solution.py:94
  8.4 33.5 %collective-permute-start.6 = (bf16[128,4096]{1,0:T(8,128)(2,1)S(1)}, bf16[128,4096]{1,0:T(8,128)(2,1)}, u32[]{:S(2)}, u32[]{:S(2)}) collective-permute-start(bf16[128,4096]{1,0:T(8,128)(2,1)S(1)} %pad_maximum_fusion), channel_id=1, source_target_pairs={{0,8},{4,12},{8,0},{12,4},{16,24},{20,28},{24,16},{28,20},{1,9},{5... | collective-permute-start | bytes 3145736 | tf_op jit(solution)/shard_map/ppermute | solution.py:94
  21.7 0.7 copy-start.3
  21.8 0.8 copy-start.4
  21.8 0.9 copy-start.5
  23.8 18.0 %copy-start = (bf16[2048,256]{1,0:T(8,128)(2,1)S(1)}, bf16[2048,256]{1,0:T(8,128)(2,1)}, u32[]{:S(2)}) copy-start(bf16[2048,256]{1,0:T(8,128)(2,1)} %left) | copy-start | bytes 3145732
  23.8 18.0 %copy-start.1 = (bf16[2048,256]{1,0:T(8,128)(2,1)S(1)}, bf16[2048,256]{1,0:T(8,128)(2,1)}, u32[]{:S(2)}) copy-start(bf16[2048,256]{1,0:T(8,128)(2,1)} %right) | copy-start | bytes 3145732
  29.2 17.2 %collective-permute-start.3 = (bf16[32,4224]{1,0:T(8,128)(2,1)}, bf16[32,4224]{1,0:T(8,128)(2,1)}, u32[]{:S(2)}, u32[]{:S(2)}) collective-permute-start(bf16[32,4224]{1,0:T(8,128)(2,1)} %concatenate.35), channel_id=1, source_target_pairs={{0,8},{4,12},{8,0},{12,4},{16,24},{20,28},{24,16},{28,20},{1,9},{5... | collective-permute-start | bytes 811016 | tf_op jit(solution)/shard_map/ppermute | solution.py:94
  30.8 22.2 %collective-permute-start.4 = (bf16[32,4224]{1,0:T(8,128)(2,1)}, bf16[32,4224]{1,0:T(8,128)(2,1)}, u32[]{:S(2)}, u32[]{:S(2)}) collective-permute-start(bf16[32,4224]{1,0:T(8,128)(2,1)} %concatenate.36), channel_id=1, source_target_pairs={{0,16},{4,20},{8,24},{12,28},{16,0},{20,4},{24,8},{28,12},{1,17},{... | collective-permute-start | bytes 811016 | tf_op jit(solution)/shard_map/ppermute | solution.py:94
  33.4 19.6 %collective-permute-start.5 = (bf16[32,4224]{1,0:T(8,128)(2,1)}, bf16[32,4224]{1,0:T(8,128)(2,1)}, u32[]{:S(2)}, u32[]{:S(2)}) collective-permute-start(bf16[32,4224]{1,0:T(8,128)(2,1)} %concatenate.37), channel_id=1, source_target_pairs={{0,24},{4,28},{8,16},{12,20},{16,8},{20,12},{24,0},{28,4},{1,25},{... | collective-permute-start | bytes 811016 | tf_op jit(solution)/shard_map/ppermute | solution.py:94
  56.0 2.0 %collective-permute-start.8 = (bf16[4,32,2048]{2,1,0:T(8,128)(2,1)S(1)}, bf16[4,32,2048]{2,1,0:T(8,128)(2,1)S(1)}, u32[]{:S(2)}, u32[]{:S(2)}) collective-permute-start(bf16[4,32,2048]{2,1,0:T(8,128)(2,1)S(1)} %pad_maximum_fusion.4), channel_id=1, source_target_pairs={{0,4},{4,0},{8,12},{12,8},{16,20},{20,16},{24,28},{28,24},{1,5},{5... | collective-permute-start | bytes 1572872 | tf_op jit(solution)/shard_map/ppermute | solution.py:94
  56.1 7.2 %collective-permute-start.11 = (bf16[128,4096]{1,0:T(8,128)(2,1)}, bf16[128,4096]{1,0:T(8,128)(2,1)S(1)}, u32[]{:S(2)}, u32[]{:S(2)}) collective-permute-start(bf16[128,4096]{1,0:T(8,128)(2,1)} %collective-permute-done.6), channel_id=1, source_target_pairs={{8,16},{12,20},{16,8},{20,12},{9,17},{13,21},{17,9},{21,13},{10,18... | collective-permute-start | bytes 3145736 | tf_op jit(solution)/shard_map/ppermute | solution.py:94
  58.1 25.4 %collective-permute-start.10 = (bf16[2,4,32,2048]{3,2,1,0:T(8,128)(2,1)S(1)}, bf16[2,4,32,2048]{3,2,1,0:T(8,128)(2,1)S(1)}, u32[]{:S(2)}, u32[]{:S(2)}) collective-permute-start(bf16[2,4,32,2048]{3,2,1,0:T(8,128)(2,1)S(1)} %pad_maximum_fusion.1.refs_0_.refs_4_), channel_id=1, source_target_pairs={{0,2},{1,3},{2,0},{3,1},{4,6},{5,7},{6,4},{7,5},{8,10},{9,11},{10,... | collective-permute-start | bytes 3145736 | tf_op jit(solution)/shard_map/ppermute | solution.py:94
  59.6 25.1 %collective-permute-start.9 = (bf16[2,4,32,2048]{3,2,1,0:T(8,128)(2,1)S(1)}, bf16[2,4,32,2048]{3,2,1,0:T(8,128)(2,1)S(1)}, u32[]{:S(2)}, u32[]{:S(2)}) collective-permute-start(bf16[2,4,32,2048]{3,2,1,0:T(8,128)(2,1)S(1)} %pad_maximum_fusion.1.refs_0_.refs_4_), channel_id=1, source_target_pairs={{0,1},{1,0},{2,3},{3,2},{4,5},{5,4},{6,7},{7,6},{8,9},{9,8},{10,11... | collective-permute-start | bytes 3145736 | tf_op jit(solution)/shard_map/ppermute | solution.py:94
  61.1 1.3 collective-permute-start.17
  61.2 33.1 %collective-permute-start.19 = (bf16[128,4096]{1,0:T(8,128)(2,1)}, bf16[128,4096]{1,0:T(8,128)(2,1)S(1)}, u32[]{:S(2)}, u32[]{:S(2)}) collective-permute-start(bf16[128,4096]{1,0:T(8,128)(2,1)} %collective-permute-done.7), channel_id=1, source_target_pairs={{8,0},{12,4},{16,24},{20,28},{9,1},{13,5},{17,25},{21,29},{10,2},{... | collective-permute-start | bytes 3145736 | tf_op jit(solution)/shard_map/ppermute | solution.py:94
  63.2 53.3 %collective-permute-start.15 = (bf16[128,4096]{1,0:T(8,128)(2,1)S(1)}, bf16[128,4096]{1,0:T(8,128)(2,1)S(1)}, u32[]{:S(2)}, u32[]{:S(2)}) collective-permute-start(bf16[128,4096]{1,0:T(8,128)(2,1)S(1)} %collective-permute-done.11), channel_id=1, source_target_pairs={{8,0},{12,4},{16,24},{20,28},{9,1},{13,5},{17,25},{21,29},{10,2},{... | collective-permute-start | bytes 3145736 | tf_op jit(solution)/shard_map/ppermute | solution.py:94
  84.7 13.1 %collective-permute-start.13 = (bf16[4,32,2048]{2,1,0:T(8,128)(2,1)S(1)}, bf16[4,32,2048]{2,1,0:T(8,128)(2,1)S(1)}, u32[]{:S(2)}, u32[]{:S(2)}) collective-permute-start(bf16[4,32,2048]{2,1,0:T(8,128)(2,1)S(1)} %slice_bitcast_fusion), channel_id=1, source_target_pairs={{0,2},{1,3},{2,0},{3,1},{4,6},{5,7},{6,4},{7,5},{8,10},{9,11},{10,... | collective-permute-start | bytes 1572872 | tf_op jit(solution)/shard_map/ppermute | solution.py:94
  94.7 5.1 %collective-permute-start.20 = (bf16[128,4096]{1,0:T(8,128)(2,1)S(1)}, bf16[128,4096]{1,0:T(8,128)(2,1)S(1)}, u32[]{:S(2)}, u32[]{:S(2)}) collective-permute-start(bf16[128,4096]{1,0:T(8,128)(2,1)S(1)} %get-tuple-element.70), channel_id=1, source_target_pairs={{0,4},{4,0},{8,12},{12,8},{16,20},{20,16},{24,28},{28,24},{1,5},{5... | collective-permute-start | bytes 3145736 | tf_op jit(solution)/shard_map/ppermute | solution.py:94
  94.8 5.6 %collective-permute-start.16 = (bf16[128,4096]{1,0:T(8,128)(2,1)S(1)}, bf16[128,4096]{1,0:T(8,128)(2,1)S(1)}, u32[]{:S(2)}, u32[]{:S(2)}) collective-permute-start(bf16[128,4096]{1,0:T(8,128)(2,1)S(1)} %pad_maximum_fusion), channel_id=1, source_target_pairs={{0,4},{4,0},{8,12},{12,8},{16,20},{20,16},{24,28},{28,24},{1,5},{5... | collective-permute-start | bytes 3145736 | tf_op jit(solution)/shard_map/ppermute | solution.py:94
  95.3 5.4 %collective-permute-start.18 = (bf16[128,4096]{1,0:T(8,128)(2,1)}, bf16[128,4096]{1,0:T(8,128)(2,1)S(1)}, u32[]{:S(2)}, u32[]{:S(2)}) collective-permute-start(bf16[128,4096]{1,0:T(8,128)(2,1)} %collective-permute-done.6), channel_id=1, source_target_pairs={{0,4},{4,0},{8,12},{12,8},{16,20},{20,16},{24,28},{28,24},{1,5},{5... | collective-permute-start | bytes 3145736 | tf_op jit(solution)/shard_map/ppermute | solution.py:94
  97.7 19.3 %collective-permute-start.12 = (bf16[4,32,2048]{2,1,0:T(8,128)(2,1)S(1)}, bf16[4,32,2048]{2,1,0:T(8,128)(2,1)S(1)}, u32[]{:S(2)}, u32[]{:S(2)}) collective-permute-start(bf16[4,32,2048]{2,1,0:T(8,128)(2,1)S(1)} %slice_bitcast_fusion.1), channel_id=1, source_target_pairs={{0,1},{1,0},{2,3},{3,2},{4,5},{5,4},{6,7},{7,6},{8,9},{9,8},{10,11... | collective-permute-start | bytes 1572872 | tf_op jit(solution)/shard_map/ppermute | solution.py:94
  99.8 17.8 %collective-permute-start.14 = (f32[4,128,512]{2,1,0:T(8,128)S(1)}, f32[4,128,512]{2,1,0:T(8,128)S(1)}, u32[]{:S(2)}, u32[]{:S(2)}) collective-permute-start(f32[4,128,512]{2,1,0:T(8,128)S(1)} %bitcast.117), channel_id=1, source_target_pairs={{0,4},{4,0},{8,12},{12,8},{16,20},{20,16},{24,28},{28,24},{1,5},{5... | collective-permute-start | bytes 3145736 | tf_op jit(solution)/shard_map/ppermute | solution.py:94
  116.9 5.5 %collective-permute-start.21 = (bf16[128,4096]{1,0:T(8,128)(2,1)S(1)}, bf16[128,4096]{1,0:T(8,128)(2,1)S(1)}, u32[]{:S(2)}, u32[]{:S(2)}) collective-permute-start(bf16[128,4096]{1,0:T(8,128)(2,1)S(1)} %get-tuple-element.68), channel_id=1, source_target_pairs={{0,4},{4,0},{8,12},{12,8},{16,20},{20,16},{24,28},{28,24},{1,5},{5... | collective-permute-start | bytes 3145736 | tf_op jit(solution)/shard_map/ppermute | solution.py:94
  118.0 26.6 %collective-permute-start.24 = (f32[128,512]{1,0:T(8,128)S(1)}, f32[128,512]{1,0:T(8,128)S(1)}, u32[]{:S(2)}, u32[]{:S(2)}) collective-permute-start(f32[128,512]{1,0:T(8,128)S(1)} %get-tuple-element.74), channel_id=1, source_target_pairs={{0,24},{4,28},{8,16},{12,20},{16,8},{20,12},{24,0},{28,4},{1,25},{... | collective-permute-start | bytes 786440 | tf_op jit(solution)/shard_map/ppermute | solution.py:94
  119.4 25.2 %collective-permute-start.23 = (f32[128,512]{1,0:T(8,128)S(1)}, f32[128,512]{1,0:T(8,128)S(1)}, u32[]{:S(2)}, u32[]{:S(2)}) collective-permute-start(f32[128,512]{1,0:T(8,128)S(1)} %get-tuple-element.75), channel_id=1, source_target_pairs={{0,16},{4,20},{8,24},{12,28},{16,0},{20,4},{24,8},{28,12},{1,17},{... | collective-permute-start | bytes 786440 | tf_op jit(solution)/shard_map/ppermute | solution.py:94
  120.3 24.4 %collective-permute-start.22 = (f32[128,512]{1,0:T(8,128)S(1)}, f32[128,512]{1,0:T(8,128)S(1)}, u32[]{:S(2)}, u32[]{:S(2)}) collective-permute-start(f32[128,512]{1,0:T(8,128)S(1)} %get-tuple-element.76), channel_id=1, source_target_pairs={{0,8},{4,12},{8,0},{12,4},{16,24},{20,28},{24,16},{28,20},{1,9},{5... | collective-permute-start | bytes 786440 | tf_op jit(solution)/shard_map/ppermute | solution.py:94

commit v4 on v3

--- a/solution.py
+++ b/solution.py
@@ -80,6 +80,45 @@
     )(left, right)
 
 
+def pieces_kernel(places, *refs):
+    held, (notes, scale, thirds) = refs[:4], refs[4:7]
+    outs, kept = refs[7:11], refs[11]
+    role, t = places[0], places[1]
+    width = held[0].shape[1]
+    first = notes.shape[1] - width
+    for k in range(4):
+        gain = notes[pl.ds(t ^ k, 1), :][:, first:]
+        kept[k] = (held[k][...].astype(jnp.float32) * gain * scale[...]).astype(kept.dtype)
+    for j in range(4):
+        outs[j][:, :width] = kept[role ^ j]
+        outs[j][:, width:] = thirds[...]
+
+
+def row_pieces(places, held, notes, scale, thirds):
+    quarter, width = held[0].shape
+
+    def whole(*shape):
+        return pl.BlockSpec(shape, lambda: (0,) * len(shape))
+
+    out = whole(quarter, width + thirds.shape[1])
+    shape = jax.ShapeDtypeStruct((quarter, width + thirds.shape[1]), thirds.dtype)
+    return list(
+        pl.pallas_call(
+            pieces_kernel,
+            in_specs=[pl.BlockSpec(memory_space=pltpu.SMEM)]
+            + [whole(quarter, width)] * 4
+            + [whole(*notes.shape), whole(*scale.shape), whole(*thirds.shape)],
+            out_specs=[out] * 4,
+            out_shape=[shape] * 4,
+            scratch_shapes=[pltpu.VMEM((4, quarter, width), thirds.dtype)],
+            compiler_params=pltpu.CompilerParams(vmem_limit_bytes=16 << 20),
+            cost_estimate=pl.CostEstimate(
+                flops=0, bytes_accessed=16 * quarter * width, transcendentals=0
+            ),
+        )(places, *held, notes, scale, thirds)
+    )
+
+
 def slice_body(tokens, norm_gain, key_weight, value_weight):
     count, width = tokens.shape
     features = width * 4
@@ -99,8 +138,8 @@
         )
 
     turned = reorder(tokens)
-    near = move(turned, NEAR)
-    across = move(turned, MIDDLE)
+    near = move(tokens, NEAR)
+    across = move(tokens, MIDDLE)
 
     pieces = [turned[k * quarter : (k + 1) * quarter] for k in range(4)]
     held = [pieces[0]] + [move(pieces[k], SIDES[k], "tp") for k in (1, 2, 3)]
@@ -111,7 +150,6 @@
     *held, notes = lax.optimization_barrier((*held, notes))
     power = jnp.sum(notes[:, :count], axis=0)
     scale = lax.rsqrt(power / features + epsilon)
-    gains = notes[:, count:]
     col_gain = norm_gain.astype(jnp.float32)[None, :]
 
     def norm(block, gain, scale):
@@ -126,16 +164,8 @@
         thirds.append(part.astype(jnp.bfloat16))
     thirds = jnp.concatenate(thirds + [jnp.zeros((quarter, 116), jnp.bfloat16)], axis=1)
 
-    def choose(which):
-        piece = jnp.where(
-            which == 0,
-            held[0],
-            jnp.where(which == 1, held[1], jnp.where(which == 2, held[2], held[3])),
-        )
-        gain = lax.dynamic_slice_in_dim(gains, t ^ which, 1)
-        return jnp.concatenate([norm(piece, gain, quarter_scale), thirds], axis=1)
-
-    landed = [choose(role)] + [move(choose(role ^ j), FLIPS[j]) for j in (1, 2, 3)]
+    leaving = row_pieces(jnp.stack([role, t]), held, notes, quarter_scale, thirds)
+    landed = leaving[:1] + [move(leaving[j], FLIPS[j]) for j in (1, 2, 3)]
 
     outer = move(across, OUTWARD)
     beyond = move(near, MIDDLE)
@@ -154,8 +184,8 @@
     from_x = move(group, SIDES[1], "tp")
     from_y = move(group, SIDES[2], "tp")
     last = move(beyond, OUTWARD)
-    from_x, from_y, turned, near, beyond = lax.optimization_barrier(
-        (from_x, from_y, turned, near, beyond)
+    from_x, from_y, tokens, near, beyond = lax.optimization_barrier(
+        (from_x, from_y, tokens, near, beyond)
     )
     far = [move(from_y[0], SIDES[1], "tp"), move(from_x[1], SIDES[2], "tp")]
     sent = jnp.stack([block[:, width:].astype(jnp.float32) for block in landed])
@@ -165,11 +195,13 @@
         axis=1,
     )
     scales = [own_scales, move(own_scales, CORES)]
-    blocks = [turned, near, jnp.where(middle, beyond, outer)]
+    blocks = [tokens, near, jnp.where(middle, beyond, outer)]
     twins = [move(block, CORES) for block in blocks]
 
     def col_parts(j):
-        return [norm((blocks, twins)[p][j], col_gain, scales[p][j][:, None]) for p in range(2)]
+        return [
+            norm(reorder((blocks, twins)[p][j]), col_gain, scales[p][j][:, None]) for p in range(2)
+        ]
 
     def project(block):
         flat = block.reshape(-1, half)

time: 146 us -> 142 us (0.973)
  local copies, waits for them, and re-layouts: 13.2 us -> 7.48 us
  waiting for transfers between devices: 59.6 us -> 55.5 us
  blocking collectives: 8.95 us -> 13 us
  Pallas kernels: 22.1 us -> 23.9 us
    concatenate x4 -> x1, local copies, waits for them, and re-layouts: 6.41 us -> 0.08 us  [slice_body(): jnp.concatenate(thirds + [jnp.zeros((quarter, 116), jnp.bfloat16)], axis=1)]
    ppermute x25, waiting for transfers between devices: 59.6 us -> 55.5 us  [move(): return lax.ppermute(x, axis, pairs)]
    all_gather x1, blocking collectives: 8.95 us -> 13 us  [slice_body(): notes = lax.all_gather(note, 'tp')]
    dynamic_slice x3 -> x11, local copies, waits for them, and re-layouts: 1.46 us -> 4.27 us  [reorder(): lax.dynamic_slice_in_dim(x, (t ^ k) * quarter, quarter)]
    pallas_call x0 -> x1, Pallas kernels: none -> 1.86 us  [row_pieces(): pl.pallas_call(pieces_kernel, in_specs=[pl.BlockSpec(memory_space=pltpu.S...]
    convert_element_type x6 -> x3, other arithmetic: 7.37 us -> 6.12 us  [norm(): return (block.astype(jnp.float32) * gain * scale).astype(jnp.bfloat16)]
  transfers between devices with their start and end apart: 25 -> 25, of which waited for: 11 -> 8; matrix products, arithmetic and copies ran while one was open for 13% -> 12% of each run, Pallas kernels for 15% -> 17%
where the time goes in v4:
time: 142 us; the launch traced here: 141 us
  waiting for transfers between devices  55.5 us (39%)
  starting transfers between devices  28.1 us (20%)
  Pallas kernels  23.9 us (17%)
  blocking collectives  13 us (9%)
  other arithmetic  9.14 us (6%)
  local copies, waits for them, and re-layouts  7.48 us (5%)
  matrix products  3.12 us (2%)
    ppermute x25, waiting for transfers between devices, move(): return lax.ppermute(x, axis, pairs)  55.5 us
    ppermute x25, starting transfers between devices, move(): return lax.ppermute(x, axis, pairs)  28.1 us
    pallas_call x1, Pallas kernels, hessian_tile(): pl.pallas_call(functools.partial(tile_kernel, scale, len(rows)), grid=(he...  21.9 us
    all_gather x1, blocking collectives, slice_body(): notes = lax.all_gather(note, 'tp')  13 us
    convert_element_type x3, other arithmetic, norm(): return (block.astype(jnp.float32) * gain * scale).astype(jnp.bfloat16)  6.12 us
    dynamic_slice x11, local copies, waits for them, and re-layouts, reorder(): lax.dynamic_slice_in_dim(x, (t ^ k) * quarter, quarter)  4.27 us
    dot_general x5, matrix products, project(): product = jnp.dot(flat, weights, preferred_element_type=jnp.float32)  3.12 us
  transfers between devices with their start and end apart: 25, of which 8 were waited for; matrix products, arithmetic and copies ran while one was open for 12% of the time, Pallas kernels for 17%

profile of v4, /device:TPU:0, one launch (start us, length us, event | category | flops | bytes accessed | tf_op | source)
XLA Modules:
  0.0 141.4 jit_solution(4690920458806433495)
XLA Ops:
  0.6 3.1 %collective-permute-start.6 = (bf16[128,4096]{1,0:T(8,128)(2,1)}, bf16[128,4096]{1,0:T(8,128)(2,1)}, u32[]{:S(2)}, u32[]{:S(2)}) collective-permute-start(bf16[128,4096]{1,0:T(8,128)(2,1)} %param.4), channel_id=1, source_target_pairs={{0,8},{4,12},{8,0},{12,4},{16,24},{20,28},{24,16},{28,20},{1,9},{5... | collective-permute-start | bytes 3145736 | tf_op jit(solution)/shard_map/ppermute | solution.py:133
  3.7 1.6 %collective-permute-start.7 = (bf16[128,4096]{1,0:T(8,128)(2,1)}, bf16[128,4096]{1,0:T(8,128)(2,1)}, u32[]{:S(2)}, u32[]{:S(2)}) collective-permute-start(bf16[128,4096]{1,0:T(8,128)(2,1)} %param.4), channel_id=1, source_target_pairs={{8,16},{12,20},{16,8},{20,12},{9,17},{13,21},{17,9},{21,13},{10,18... | collective-permute-start | bytes 3145736 | tf_op jit(solution)/shard_map/ppermute | solution.py:133
  5.4 2.2 %constant_dynamic-slice_fusion.36 = (bf16[32,4096]{1,0:T(8,128)(2,1)}, bf16[32,4096]{1,0:T(8,128)(2,1)}, bf16[32,4096]{1,0:T(8,128)(2,1)}, bf16[32,4096]{1,0:T(8,128)(2,1)S(1)}) fusion(bf16[128,4096]{1,0:T(8,128)(2,1)} %param.4, s32[]{:T(128)S(6)} %select_n.123, s32[]{:T(128)S(6)} %select_n.122, s32[]{:T(128)S(6)} %select_n.121, s32[]{:T(128)S(6)} %select_n.120), kind=kLoop, calls=%fused_computation.103 | loop fusion | bytes 2097168 | tf_op jit(solution)/shard_map/dynamic_slice | solution.py:137
  7.6 2.4 %collective-permute-start.2 = (bf16[32,4096]{1,0:T(8,128)(2,1)}, bf16[32,4096]{1,0:T(8,128)(2,1)S(1)}, u32[]{:S(2)}, u32[]{:S(2)}) collective-permute-start(bf16[32,4096]{1,0:T(8,128)(2,1)} %get-tuple-element.110), channel_id=1, source_target_pairs={{0,3},{1,2},{2,1},{3,0},{4,7},{5,6},{6,5},{7,4},{8,11},{9,10},{10,... | collective-permute-start | bytes 786440 | tf_op jit(solution)/shard_map/ppermute | solution.py:133
  10.0 0.5 collective-permute-start.1
  10.6 0.5 collective-permute-start
  11.1 1.5 %multiply_reduce_fusion = f32[128]{0:T(128)S(1)} fusion(bf16[128,4096]{1,0:T(8,128)(2,1)} %param.4), kind=kLoop, calls=%fused_computation.12 | loop fusion | flops 1572736 | bytes 1049088 | tf_op jit(solution)/shard_map/reduce_sum | solution.py:148
  12.7 13.0 %all-gather.1 = f32[4,1,4224]{2,1,0:T(1,128)S(1)} all-gather(f32[1,1,4224]{2,1,0:T(1,128)S(1)} %reshape.67), channel_id=2, replica_groups=mesh['fsdp'=8,'tp'=4] {'tp'}, dimensions={0}, use_global_device_ids=true | all-gather | bytes 84480 | tf_op jit(solution)/shard_map/all_gather | solution.py:149
  26.4 1.9 %shard_map.67 = (bf16[32,4224]{1,0:T(8,128)(2,1)S(1)}, bf16[32,4224]{1,0:T(8,128)(2,1)}, bf16[32,4224]{1,0:T(8,128)(2,1)}, bf16[32,4224]{1,0:T(8,128)(2,1)}) custom-call(s32[2]{0:T(128)S(1)} %pad_add_fusion.places, bf16[32,4096]{1,0:T(8,128)(2,1)S(1)} %get-tuple-element.37.refs_0_, bf16[32,4096]{1,0:T(8,128)(2,1)S(1)} %collective-permute-done.refs_1_, ...), custom_call_target="tpu_custom_call" | custom-call | bytes 2097152 | tf_op jit(solution)/shard_map/pallas_call | solution.py:106
  28.2 3.2 %collective-permute-start.3 = (bf16[32,4224]{1,0:T(8,128)(2,1)}, bf16[32,4224]{1,0:T(8,128)(2,1)}, u32[]{:S(2)}, u32[]{:S(2)}) collective-permute-start(bf16[32,4224]{1,0:T(8,128)(2,1)} %get-tuple-element.43), channel_id=1, source_target_pairs={{0,8},{4,12},{8,0},{12,4},{16,24},{20,28},{24,16},{28,20},{1,9},{5... | collective-permute-start | bytes 811016 | tf_op jit(solution)/shard_map/ppermute | solution.py:133
  31.4 2.4 %collective-permute-start.5 = (bf16[32,4224]{1,0:T(8,128)(2,1)}, bf16[32,4224]{1,0:T(8,128)(2,1)S(1)}, u32[]{:S(2)}, u32[]{:S(2)}) collective-permute-start(bf16[32,4224]{1,0:T(8,128)(2,1)} %get-tuple-element.45), channel_id=1, source_target_pairs={{0,24},{4,28},{8,16},{12,20},{16,8},{20,12},{24,0},{28,4},{1,25},{... | collective-permute-start | bytes 811016 | tf_op jit(solution)/shard_map/ppermute | solution.py:133
  33.9 0.2 shard_map.68
  34.0 8.2 %collective-permute-done.3 = bf16[32,4224]{1,0:T(8,128)(2,1)} collective-permute-done((bf16[32,4224]{1,0:T(8,128)(2,1)}, bf16[32,4224]{1,0:T(8,128)(2,1)}, u32[]{:S(2)}, u32[]{:S(2)}) %collective-permute-start.3) | collective-permute-done | bytes 270368 | tf_op jit(solution)/shard_map/ppermute | solution.py:133
  42.2 11.4 %collective-permute-done.4 = bf16[32,4224]{1,0:T(8,128)(2,1)S(1)} collective-permute-done((bf16[32,4224]{1,0:T(8,128)(2,1)}, bf16[32,4224]{1,0:T(8,128)(2,1)S(1)}, u32[]{:S(2)}, u32[]{:S(2)}) %collective-permute-start.4) | collective-permute-done | bytes 270368 | tf_op jit(solution)/shard_map/ppermute | solution.py:133
  53.6 0.7 slice_bitcast_fusion.8
  54.3 1.0 dynamic-slice_bitcast_fusion.6
  55.5 0.7 collective-permute-start.11
  56.2 1.3 collective-permute-start.19
  57.5 0.2 fusion.14
  57.9 0.8 collective-permute-start.10
  58.7 1.3 collective-permute-start.9
  60.1 1.1 collective-permute-done.17
  61.2 0.7 fusion.29
  62.0 1.6 %collective-permute-start.15 = (bf16[128,4096]{1,0:T(8,128)(2,1)S(1)}, bf16[128,4096]{1,0:T(8,128)(2,1)S(1)}, u32[]{:S(2)}, u32[]{:S(2)}) collective-permute-start(bf16[128,4096]{1,0:T(8,128)(2,1)S(1)} %collective-permute-done.11), channel_id=1, source_target_pairs={{8,0},{12,4},{16,24},{20,28},{9,1},{13,5},{17,25},{21,29},{10,2},{... | collective-permute-start | bytes 3145736 | tf_op jit(solution)/shard_map/ppermute | solution.py:133
  63.6 19.9 %collective-permute-done.10.refs_2_.refs_6_ = bf16[2,4,32,2048]{3,2,1,0:T(8,128)(2,1)S(1)} collective-permute-done((bf16[2,4,32,2048]{3,2,1,0:T(8,128)(2,1)S(1)}, bf16[2,4,32,2048]{3,2,1,0:T(8,128)(2,1)S(1)}, u32[]{:S(2)}, u32[]{:S(2)}) %collective-permute-start.10) | collective-permute-done | bytes 1048608 | tf_op jit(solution)/shard_map/ppermute | solution.py:133
  83.5 0.5 collective-permute-done.9.refs_1_.refs_5_
  84.0 3.4 %collective-permute-done.19 = bf16[128,4096]{1,0:T(8,128)(2,1)S(1)} collective-permute-done((bf16[128,4096]{1,0:T(8,128)(2,1)}, bf16[128,4096]{1,0:T(8,128)(2,1)S(1)}, u32[]{:S(2)}, u32[]{:S(2)}) %collective-permute-start.19) | collective-permute-done | bytes 1048608 | tf_op jit(solution)/shard_map/ppermute | solution.py:133
  87.8 0.5 collective-permute-start.16
  88.4 0.7 fusion.30
  89.2 0.6 collective-permute-start.12
  89.7 1.5 %collective-permute-start.13 = (bf16[4,32,2048]{2,1,0:T(8,128)(2,1)S(1)}, bf16[4,32,2048]{2,1,0:T(8,128)(2,1)S(1)}, u32[]{:S(2)}, u32[]{:S(2)}) collective-permute-start(bf16[4,32,2048]{2,1,0:T(8,128)(2,1)S(1)} %slice_bitcast_fusion), channel_id=1, source_target_pairs={{0,2},{1,3},{2,0},{3,1},{4,6},{5,7},{6,4},{7,5},{8,10},{9,11},{10,... | collective-permute-start | bytes 1572872 | tf_op jit(solution)/shard_map/ppermute | solution.py:133
  91.3 1.3 constant_dynamic-slice_fusion.27
  92.5 0.7 fusion.31
  93.4 10.0 %collective-permute-done.13 = bf16[4,32,2048]{2,1,0:T(8,128)(2,1)S(1)} collective-permute-done((bf16[4,32,2048]{2,1,0:T(8,128)(2,1)S(1)}, bf16[4,32,2048]{2,1,0:T(8,128)(2,1)S(1)}, u32[]{:S(2)}, u32[]{:S(2)}) %collective-permute-start.13) | collective-permute-done | bytes 524320 | tf_op jit(solution)/shard_map/ppermute | solution.py:133
  103.3 0.5 fusion.7
  104.0 0.6 collective-permute-start.14
  104.5 0.5 fusion.4
  105.2 2.8 %multiply_convert_fusion.2 = (bf16[128,4096]{1,0:T(8,128)(2,1)S(1)}, bf16[128,4096]{1,0:T(8,128)(2,1)S(1)}, bf16[128,4096]{1,0:T(8,128)(2,1)S(1)}) fusion(bf16[32,4096]{1,0:T(8,128)(2,1)S(1)} %get-tuple-element.87, bf16[32,4096]{1,0:T(8,128)(2,1)S(1)} %get-tuple-element.88, bf16[32,4096]{1,0:T(8,128)(2,1)S(1)} %get-tuple-element.89, ...), kind=kLoop, calls=%fused_computation.6 | loop fusion | flops 17301504 | bytes 6309376 | tf_op jit(solution)/shard_map/convert_element_type | solution.py:156
  108.1 2.8 %multiply_convert_fusion.3 = (bf16[128,4096]{1,0:T(8,128)(2,1)S(1)}, bf16[128,4096]{1,0:T(8,128)(2,1)S(1)}, bf16[128,4096]{1,0:T(8,128)(2,1)S(1)}) fusion(bf16[32,4096]{1,0:T(8,128)(2,1)S(1)} %get-tuple-element.91, bf16[32,4096]{1,0:T(8,128)(2,1)S(1)} %get-tuple-element.92, bf16[32,4096]{1,0:T(8,128)(2,1)S(1)} %get-tuple-element.93, ...), kind=kLoop, calls=%fused_computation.7 | loop fusion | flops 17301504 | bytes 6309376 | tf_op jit(solution)/shard_map/convert_element_type | solution.py:156
  110.9 1.1 collective-permute-done.15
  112.1 0.1 broadcast_select_fusion
  112.6 0.2 bitcast_add_fusion
  112.8 1.6 %collective-permute-start.24 = (f32[128,512]{1,0:T(8,128)S(1)}, f32[128,512]{1,0:T(8,128)S(1)}, u32[]{:S(2)}, u32[]{:S(2)}) collective-permute-start(f32[128,512]{1,0:T(8,128)S(1)} %get-tuple-element.75), channel_id=1, source_target_pairs={{0,24},{4,28},{8,16},{12,20},{16,8},{20,12},{24,0},{28,4},{1,25},{... | collective-permute-start | bytes 786440 | tf_op jit(solution)/shard_map/ppermute | solution.py:133
  114.4 3.3 %collective-permute-start.23 = (f32[128,512]{1,0:T(8,128)S(1)}, f32[128,512]{1,0:T(8,128)S(1)}, u32[]{:S(2)}, u32[]{:S(2)}) collective-permute-start(f32[128,512]{1,0:T(8,128)S(1)} %get-tuple-element.76), channel_id=1, source_target_pairs={{0,16},{4,20},{8,24},{12,28},{16,0},{20,4},{24,8},{28,12},{1,17},{... | collective-permute-start | bytes 786440 | tf_op jit(solution)/shard_map/ppermute | solution.py:133
  117.8 0.3 collective-permute-start.22
  118.1 0.6 multiply_convert_fusion
  118.7 21.9 %shard_map.69 = f32[2048,4096]{1,0:T(8,128)} custom-call(bf16[2,4,32,2048]{3,2,1,0:T(8,128)(2,1)S(1)} %pad_maximum_fusion.refs_0_.refs_4_, bf16[2,4,32,2048]{3,2,1,0:T(8,128)(2,1)S(1)} %collective-permute-done.9.refs_1_.refs_5_, bf16[2,4,32,2048]{3,2,1,0:T(8,128)(2,1)S(1)} %collective-permute-done.10.refs_2_.refs_6_, bf16[1,4,32,2048]{3,2,1,0:T(8,128)(2,1)S(1)} %bitcast.112, ...), custom_call_target="tpu_custom_call" | custom-call | flops 17179869184 | bytes 33554432 | tf_op jit(solution)/shard_map/pallas_call | solution.py:45
  140.8 0.7 fusion.27
  (78 shorter events, 2.9 us)
Async XLA Ops:
  0.6 12.0 %copy-start.3 = (bf16[4096]{0:T(1024)(128)(2,1)S(1)}, bf16[4096]{0:T(1024)(128)(2,1)}, u32[]{:S(2)}) copy-start(bf16[4096]{0:T(1024)(128)(2,1)} %param.5) | copy-start | bytes 24580
  0.6 33.2 %collective-permute-start.6 = (bf16[128,4096]{1,0:T(8,128)(2,1)}, bf16[128,4096]{1,0:T(8,128)(2,1)}, u32[]{:S(2)}, u32[]{:S(2)}) collective-permute-start(bf16[128,4096]{1,0:T(8,128)(2,1)} %param.4), channel_id=1, source_target_pairs={{0,8},{4,12},{8,0},{12,4},{16,24},{20,28},{24,16},{28,20},{1,9},{5... | collective-permute-start | bytes 3145736 | tf_op jit(solution)/shard_map/ppermute | solution.py:133
  3.7 30.1 %collective-permute-start.7 = (bf16[128,4096]{1,0:T(8,128)(2,1)}, bf16[128,4096]{1,0:T(8,128)(2,1)}, u32[]{:S(2)}, u32[]{:S(2)}) collective-permute-start(bf16[128,4096]{1,0:T(8,128)(2,1)} %param.4), channel_id=1, source_target_pairs={{8,16},{12,20},{16,8},{20,12},{9,17},{13,21},{17,9},{21,13},{10,18... | collective-permute-start | bytes 3145736 | tf_op jit(solution)/shard_map/ppermute | solution.py:133
  5.4 28.5 %copy-start = (bf16[2048,256]{1,0:T(8,128)(2,1)S(1)}, bf16[2048,256]{1,0:T(8,128)(2,1)}, u32[]{:S(2)}) copy-start(bf16[2048,256]{1,0:T(8,128)(2,1)} %left) | copy-start | bytes 3145732
  5.4 28.5 %copy-start.1 = (bf16[2048,256]{1,0:T(8,128)(2,1)S(1)}, bf16[2048,256]{1,0:T(8,128)(2,1)}, u32[]{:S(2)}) copy-start(bf16[2048,256]{1,0:T(8,128)(2,1)} %right) | copy-start | bytes 3145732
  7.6 18.2 %collective-permute-start.2 = (bf16[32,4096]{1,0:T(8,128)(2,1)}, bf16[32,4096]{1,0:T(8,128)(2,1)S(1)}, u32[]{:S(2)}, u32[]{:S(2)}) collective-permute-start(bf16[32,4096]{1,0:T(8,128)(2,1)} %get-tuple-element.110), channel_id=1, source_target_pairs={{0,3},{1,2},{2,1},{3,0},{4,7},{5,6},{6,5},{7,4},{8,11},{9,10},{10,... | collective-permute-start | bytes 786440 | tf_op jit(solution)/shard_map/ppermute | solution.py:133
  10.0 15.8 %collective-permute-start.1 = (bf16[32,4096]{1,0:T(8,128)(2,1)}, bf16[32,4096]{1,0:T(8,128)(2,1)S(1)}, u32[]{:S(2)}, u32[]{:S(2)}) collective-permute-start(bf16[32,4096]{1,0:T(8,128)(2,1)} %get-tuple-element.111), channel_id=1, source_target_pairs={{0,2},{1,3},{2,0},{3,1},{4,6},{5,7},{6,4},{7,5},{8,10},{9,11},{10,... | collective-permute-start | bytes 786440 | tf_op jit(solution)/shard_map/ppermute | solution.py:133
  10.6 15.3 %collective-permute-start = (bf16[32,4096]{1,0:T(8,128)(2,1)}, bf16[32,4096]{1,0:T(8,128)(2,1)S(1)}, u32[]{:S(2)}, u32[]{:S(2)}) collective-permute-start(bf16[32,4096]{1,0:T(8,128)(2,1)} %get-tuple-element.112), channel_id=1, source_target_pairs={{0,1},{1,0},{2,3},{3,2},{4,5},{5,4},{6,7},{7,6},{8,9},{9,8},{10,11... | collective-permute-start | bytes 786440 | tf_op jit(solution)/shard_map/ppermute | solution.py:133
  28.2 13.9 %collective-permute-start.3 = (bf16[32,4224]{1,0:T(8,128)(2,1)}, bf16[32,4224]{1,0:T(8,128)(2,1)}, u32[]{:S(2)}, u32[]{:S(2)}) collective-permute-start(bf16[32,4224]{1,0:T(8,128)(2,1)} %get-tuple-element.43), channel_id=1, source_target_pairs={{0,8},{4,12},{8,0},{12,4},{16,24},{20,28},{24,16},{28,20},{1,9},{5... | collective-permute-start | bytes 811016 | tf_op jit(solution)/shard_map/ppermute | solution.py:133
  31.4 22.1 %collective-permute-start.4 = (bf16[32,4224]{1,0:T(8,128)(2,1)}, bf16[32,4224]{1,0:T(8,128)(2,1)S(1)}, u32[]{:S(2)}, u32[]{:S(2)}) collective-permute-start(bf16[32,4224]{1,0:T(8,128)(2,1)} %get-tuple-element.44), channel_id=1, source_target_pairs={{0,16},{4,20},{8,24},{12,28},{16,0},{20,4},{24,8},{28,12},{1,17},{... | collective-permute-start | bytes 811016 | tf_op jit(solution)/shard_map/ppermute | solution.py:133
  31.4 22.1 %collective-permute-start.5 = (bf16[32,4224]{1,0:T(8,128)(2,1)}, bf16[32,4224]{1,0:T(8,128)(2,1)S(1)}, u32[]{:S(2)}, u32[]{:S(2)}) collective-permute-start(bf16[32,4224]{1,0:T(8,128)(2,1)} %get-tuple-element.45), channel_id=1, source_target_pairs={{0,24},{4,28},{8,16},{12,20},{16,8},{20,12},{24,0},{28,4},{1,25},{... | collective-permute-start | bytes 811016 | tf_op jit(solution)/shard_map/ppermute | solution.py:133
  55.4 2.4 %collective-permute-start.8 = (bf16[4,32,2048]{2,1,0:T(8,128)(2,1)S(1)}, bf16[4,32,2048]{2,1,0:T(8,128)(2,1)S(1)}, u32[]{:S(2)}, u32[]{:S(2)}) collective-permute-start(bf16[4,32,2048]{2,1,0:T(8,128)(2,1)S(1)} %pad_maximum_fusion.3), channel_id=1, source_target_pairs={{0,4},{4,0},{8,12},{12,8},{16,20},{20,16},{24,28},{28,24},{1,5},{5... | collective-permute-start | bytes 1572872 | tf_op jit(solution)/shard_map/ppermute | solution.py:133
  55.5 6.5 %collective-permute-start.11 = (bf16[128,4096]{1,0:T(8,128)(2,1)}, bf16[128,4096]{1,0:T(8,128)(2,1)S(1)}, u32[]{:S(2)}, u32[]{:S(2)}) collective-permute-start(bf16[128,4096]{1,0:T(8,128)(2,1)} %collective-permute-done.6), channel_id=1, source_target_pairs={{8,16},{12,20},{16,8},{20,12},{9,17},{13,21},{17,9},{21,13},{10,18... | collective-permute-start | bytes 3145736 | tf_op jit(solution)/shard_map/ppermute | solution.py:133
  56.2 31.1 %collective-permute-start.19 = (bf16[128,4096]{1,0:T(8,128)(2,1)}, bf16[128,4096]{1,0:T(8,128)(2,1)S(1)}, u32[]{:S(2)}, u32[]{:S(2)}) collective-permute-start(bf16[128,4096]{1,0:T(8,128)(2,1)} %collective-permute-done.7), channel_id=1, source_target_pairs={{8,0},{12,4},{16,24},{20,28},{9,1},{13,5},{17,25},{21,29},{10,2},{... | collective-permute-start | bytes 3145736 | tf_op jit(solution)/shard_map/ppermute | solution.py:133
  57.9 25.6 %collective-permute-start.10 = (bf16[2,4,32,2048]{3,2,1,0:T(8,128)(2,1)S(1)}, bf16[2,4,32,2048]{3,2,1,0:T(8,128)(2,1)S(1)}, u32[]{:S(2)}, u32[]{:S(2)}) collective-permute-start(bf16[2,4,32,2048]{3,2,1,0:T(8,128)(2,1)S(1)} %pad_maximum_fusion.refs_0_.refs_4_), channel_id=1, source_target_pairs={{0,2},{1,3},{2,0},{3,1},{4,6},{5,7},{6,4},{7,5},{8,10},{9,11},{10,... | collective-permute-start | bytes 3145736 | tf_op jit(solution)/shard_map/ppermute | solution.py:133
  58.7 25.3 %collective-permute-start.9 = (bf16[2,4,32,2048]{3,2,1,0:T(8,128)(2,1)S(1)}, bf16[2,4,32,2048]{3,2,1,0:T(8,128)(2,1)S(1)}, u32[]{:S(2)}, u32[]{:S(2)}) collective-permute-start(bf16[2,4,32,2048]{3,2,1,0:T(8,128)(2,1)S(1)} %pad_maximum_fusion.refs_0_.refs_4_), channel_id=1, source_target_pairs={{0,1},{1,0},{2,3},{3,2},{4,5},{5,4},{6,7},{7,6},{8,9},{9,8},{10,11... | collective-permute-start | bytes 3145736 | tf_op jit(solution)/shard_map/ppermute | solution.py:133
  60.0 1.2 collective-permute-start.17
  62.0 25.7 %copy-start.2 = (bf16[128,4096]{1,0:T(8,128)(2,1)S(1)}, bf16[128,4096]{1,0:T(8,128)(2,1)}, u32[]{:S(2)}) copy-start(bf16[128,4096]{1,0:T(8,128)(2,1)} %param.4) | copy-start | bytes 3145732
  62.0 50.1 %collective-permute-start.15 = (bf16[128,4096]{1,0:T(8,128)(2,1)S(1)}, bf16[128,4096]{1,0:T(8,128)(2,1)S(1)}, u32[]{:S(2)}, u32[]{:S(2)}) collective-permute-start(bf16[128,4096]{1,0:T(8,128)(2,1)S(1)} %collective-permute-done.11), channel_id=1, source_target_pairs={{8,0},{12,4},{16,24},{20,28},{9,1},{13,5},{17,25},{21,29},{10,2},{... | collective-permute-start | bytes 3145736 | tf_op jit(solution)/shard_map/ppermute | solution.py:133
  87.6 17.4 %collective-permute-start.20 = (bf16[128,4096]{1,0:T(8,128)(2,1)S(1)}, bf16[128,4096]{1,0:T(8,128)(2,1)S(1)}, u32[]{:S(2)}, u32[]{:S(2)}) collective-permute-start(bf16[128,4096]{1,0:T(8,128)(2,1)S(1)} %broadcast_select_fusion.1), channel_id=1, source_target_pairs={{0,4},{4,0},{8,12},{12,8},{16,20},{20,16},{24,28},{28,24},{1,5},{5... | collective-permute-start | bytes 3145736 | tf_op jit(solution)/shard_map/ppermute | solution.py:133
  87.8 17.3 %collective-permute-start.16 = (bf16[128,4096]{1,0:T(8,128)(2,1)S(1)}, bf16[128,4096]{1,0:T(8,128)(2,1)S(1)}, u32[]{:S(2)}, u32[]{:S(2)}) collective-permute-start(bf16[128,4096]{1,0:T(8,128)(2,1)S(1)} %copy-done.2), channel_id=1, source_target_pairs={{0,4},{4,0},{8,12},{12,8},{16,20},{20,16},{24,28},{28,24},{1,5},{5... | collective-permute-start | bytes 3145736 | tf_op jit(solution)/shard_map/ppermute | solution.py:133
  89.2 14.8 %collective-permute-start.12 = (bf16[4,32,2048]{2,1,0:T(8,128)(2,1)S(1)}, bf16[4,32,2048]{2,1,0:T(8,128)(2,1)S(1)}, u32[]{:S(2)}, u32[]{:S(2)}) collective-permute-start(bf16[4,32,2048]{2,1,0:T(8,128)(2,1)S(1)} %slice_bitcast_fusion.1), channel_id=1, source_target_pairs={{0,1},{1,0},{2,3},{3,2},{4,5},{5,4},{6,7},{7,6},{8,9},{9,8},{10,11... | collective-permute-start | bytes 1572872 | tf_op jit(solution)/shard_map/ppermute | solution.py:133
  89.7 13.6 %collective-permute-start.13 = (bf16[4,32,2048]{2,1,0:T(8,128)(2,1)S(1)}, bf16[4,32,2048]{2,1,0:T(8,128)(2,1)S(1)}, u32[]{:S(2)}, u32[]{:S(2)}) collective-permute-start(bf16[4,32,2048]{2,1,0:T(8,128)(2,1)S(1)} %slice_bitcast_fusion), channel_id=1, source_target_pairs={{0,2},{1,3},{2,0},{3,1},{4,6},{5,7},{6,4},{7,5},{8,10},{9,11},{10,... | collective-permute-start | bytes 1572872 | tf_op jit(solution)/shard_map/ppermute | solution.py:133
  103.3 4.7 %collective-permute-start.18 = (bf16[128,4096]{1,0:T(8,128)(2,1)}, bf16[128,4096]{1,0:T(8,128)(2,1)S(1)}, u32[]{:S(2)}, u32[]{:S(2)}) collective-permute-start(bf16[128,4096]{1,0:T(8,128)(2,1)} %collective-permute-done.6), channel_id=1, source_target_pairs={{0,4},{4,0},{8,12},{12,8},{16,20},{20,16},{24,28},{28,24},{1,5},{5... | collective-permute-start | bytes 3145736 | tf_op jit(solution)/shard_map/ppermute | solution.py:133
  104.0 8.6 %collective-permute-start.14 = (f32[4,128,512]{2,1,0:T(8,128)S(1)}, f32[4,128,512]{2,1,0:T(8,128)S(1)}, u32[]{:S(2)}, u32[]{:S(2)}) collective-permute-start(f32[4,128,512]{2,1,0:T(8,128)S(1)} %bitcast.118), channel_id=1, source_target_pairs={{0,4},{4,0},{8,12},{12,8},{16,20},{20,16},{24,28},{28,24},{1,5},{5... | collective-permute-start | bytes 3145736 | tf_op jit(solution)/shard_map/ppermute | solution.py:133
  112.2 5.9 %collective-permute-start.21 = (bf16[128,4096]{1,0:T(8,128)(2,1)S(1)}, bf16[128,4096]{1,0:T(8,128)(2,1)S(1)}, u32[]{:S(2)}, u32[]{:S(2)}) collective-permute-start(bf16[128,4096]{1,0:T(8,128)(2,1)S(1)} %broadcast_select_fusion), channel_id=1, source_target_pairs={{0,4},{4,0},{8,12},{12,8},{16,20},{20,16},{24,28},{28,24},{1,5},{5... | collective-permute-start | bytes 3145736 | tf_op jit(solution)/shard_map/ppermute | solution.py:133
  112.8 27.8 %collective-permute-start.24 = (f32[128,512]{1,0:T(8,128)S(1)}, f32[128,512]{1,0:T(8,128)S(1)}, u32[]{:S(2)}, u32[]{:S(2)}) collective-permute-start(f32[128,512]{1,0:T(8,128)S(1)} %get-tuple-element.75), channel_id=1, source_target_pairs={{0,24},{4,28},{8,16},{12,20},{16,8},{20,12},{24,0},{28,4},{1,25},{... | collective-permute-start | bytes 786440 | tf_op jit(solution)/shard_map/ppermute | solution.py:133
  114.4 26.2 %collective-permute-start.23 = (f32[128,512]{1,0:T(8,128)S(1)}, f32[128,512]{1,0:T(8,128)S(1)}, u32[]{:S(2)}, u32[]{:S(2)}) collective-permute-start(f32[128,512]{1,0:T(8,128)S(1)} %get-tuple-element.76), channel_id=1, source_target_pairs={{0,16},{4,20},{8,24},{12,28},{16,0},{20,4},{24,8},{28,12},{1,17},{... | collective-permute-start | bytes 786440 | tf_op jit(solution)/shard_map/ppermute | solution.py:133
  117.8 22.9 %collective-permute-start.22 = (f32[128,512]{1,0:T(8,128)S(1)}, f32[128,512]{1,0:T(8,128)S(1)}, u32[]{:S(2)}, u32[]{:S(2)}) collective-permute-start(f32[128,512]{1,0:T(8,128)S(1)} %get-tuple-element.77), channel_id=1, source_target_pairs={{0,8},{4,12},{8,0},{12,4},{16,24},{20,28},{24,16},{28,20},{1,9},{5... | collective-permute-start | bytes 786440 | tf_op jit(solution)/shard_map/ppermute | solution.py:133

commit v5 on v4

--- a/solution.py
+++ b/solution.py
@@ -184,10 +184,6 @@
     from_x = move(group, SIDES[1], "tp")
     from_y = move(group, SIDES[2], "tp")
     last = move(beyond, OUTWARD)
-    from_x, from_y, tokens, near, beyond = lax.optimization_barrier(
-        (from_x, from_y, tokens, near, beyond)
-    )
-    far = [move(from_y[0], SIDES[1], "tp"), move(from_x[1], SIDES[2], "tp")]
     sent = jnp.stack([block[:, width:].astype(jnp.float32) for block in landed])
     lane = lax.broadcasted_iota(jnp.int32, sent.shape, 2)
     own_scales = jnp.concatenate(
@@ -195,13 +191,20 @@
         axis=1,
     )
     scales = [own_scales, move(own_scales, CORES)]
-    blocks = [tokens, near, jnp.where(middle, beyond, outer)]
+    blocks = [tokens, near]
     twins = [move(block, CORES) for block in blocks]
 
     def col_parts(j):
         return [
             norm(reorder((blocks, twins)[p][j]), col_gain, scales[p][j][:, None]) for p in range(2)
         ]
+
+    cols = [col_parts(j) for j in range(2)]
+    from_x, from_y, beyond, cols = lax.optimization_barrier((from_x, from_y, beyond, cols))
+    far = [move(from_y[0], SIDES[1], "tp"), move(from_x[1], SIDES[2], "tp")]
+    blocks.append(jnp.where(middle, beyond, outer))
+    twins.append(move(blocks[2], CORES))
+    cols.append(col_parts(2))
 
     def project(block):
         flat = block.reshape(-1, half)
@@ -216,7 +219,6 @@
     sums = parts[0] + move(parts[1], CORES)
     homes = [move(sums[j], FLIPS[j]) for j in (1, 2, 3)]
 
-    cols = [col_parts(j) for j in range(3)]
     last, cols = lax.optimization_barrier((last, cols))
     blocks.append(jnp.where(middle, across, last))
     twins.append(move(blocks[3], CORES))

time: 142 us -> 139 us (0.979)
    dynamic_slice x11 -> x10, local copies, waits for them, and re-layouts: 4.27 us -> 5.32 us  [reorder(): lax.dynamic_slice_in_dim(x, (t ^ k) * quarter, quarter)]
    convert_element_type x3 -> x4, other arithmetic: 6.12 us -> 5.23 us  [norm(): return (block.astype(jnp.float32) * gain * scale).astype(jnp.bfloat16)]
  transfers between devices with their start and end apart: 25 -> 25, of which waited for: 8 -> 8; matrix products, arithmetic and copies ran while one was open for 12% -> 13% of each run, Pallas kernels for 17% -> 17%
where the time goes in v5:
time: 139 us
  waiting for transfers between devices  56.6 us (41%)
  starting transfers between devices  26.9 us (19%)
  Pallas kernels  23.1 us (17%)
  blocking collectives  12.6 us (9%)
  other arithmetic  8.24 us (6%)
  local copies, waits for them, and re-layouts  6.89 us (5%)
  matrix products  2.98 us (2%)
    ppermute x25, waiting for transfers between devices, move(): return lax.ppermute(x, axis, pairs)  56.6 us
    ppermute x25, starting transfers between devices, move(): return lax.ppermute(x, axis, pairs)  26.9 us
    pallas_call x1, Pallas kernels, hessian_tile(): pl.pallas_call(functools.partial(tile_kernel, scale, len(rows)), grid=(he...  21.9 us
    all_gather x1, blocking collectives, slice_body(): notes = lax.all_gather(note, 'tp')  12.6 us
    dynamic_slice x10, local copies, waits for them, and re-layouts, reorder(): lax.dynamic_slice_in_dim(x, (t ^ k) * quarter, quarter)  5.32 us
    convert_element_type x4, other arithmetic, norm(): return (block.astype(jnp.float32) * gain * scale).astype(jnp.bfloat16)  5.23 us
    dot_general x5, matrix products, project(): product = jnp.dot(flat, weights, preferred_element_type=jnp.float32)  2.98 us
  transfers between devices with their start and end apart: 25, of which 8 were waited for; matrix products, arithmetic and copies ran while one was open for 13% of the time, Pallas kernels for 17%

profile of v5, /device:TPU:0, one launch (start us, length us, event | category | flops | bytes accessed | tf_op | source)
XLA Modules:
  0.0 138.5 jit_solution(1964873915703841489)
XLA Ops:
  0.6 3.1 %collective-permute-start.6 = (bf16[128,4096]{1,0:T(8,128)(2,1)}, bf16[128,4096]{1,0:T(8,128)(2,1)}, u32[]{:S(2)}, u32[]{:S(2)}) collective-permute-start(bf16[128,4096]{1,0:T(8,128)(2,1)} %param.4), channel_id=1, source_target_pairs={{0,8},{4,12},{8,0},{12,4},{16,24},{20,28},{24,16},{28,20},{1,9},{5... | collective-permute-start | bytes 3145736 | tf_op jit(solution)/shard_map/ppermute | solution.py:133
  3.7 1.6 %collective-permute-start.7 = (bf16[128,4096]{1,0:T(8,128)(2,1)}, bf16[128,4096]{1,0:T(8,128)(2,1)}, u32[]{:S(2)}, u32[]{:S(2)}) collective-permute-start(bf16[128,4096]{1,0:T(8,128)(2,1)} %param.4), channel_id=1, source_target_pairs={{8,16},{12,20},{16,8},{20,12},{9,17},{13,21},{17,9},{21,13},{10,18... | collective-permute-start | bytes 3145736 | tf_op jit(solution)/shard_map/ppermute | solution.py:133
  5.4 2.2 %constant_dynamic-slice_fusion.32 = (bf16[32,4096]{1,0:T(8,128)(2,1)S(1)}, bf16[32,4096]{1,0:T(8,128)(2,1)}, bf16[32,4096]{1,0:T(8,128)(2,1)}, bf16[32,4096]{1,0:T(8,128)(2,1)S(1)}) fusion(bf16[128,4096]{1,0:T(8,128)(2,1)} %param.4, s32[]{:T(128)S(6)} %select_n.123, s32[]{:T(128)S(6)} %select_n.122, s32[]{:T(128)S(6)} %select_n.121, s32[]{:T(128)S(6)} %select_n.120), kind=kLoop, calls=%fused_computation.99 | loop fusion | bytes 2097168 | tf_op jit(solution)/shard_map/dynamic_slice | solution.py:137
  7.6 2.4 %collective-permute-start.2 = (bf16[32,4096]{1,0:T(8,128)(2,1)S(1)}, bf16[32,4096]{1,0:T(8,128)(2,1)S(1)}, u32[]{:S(2)}, u32[]{:S(2)}) collective-permute-start(bf16[32,4096]{1,0:T(8,128)(2,1)S(1)} %get-tuple-element.110), channel_id=1, source_target_pairs={{0,3},{1,2},{2,1},{3,0},{4,7},{5,6},{6,5},{7,4},{8,11},{9,10},{10,... | collective-permute-start | bytes 786440 | tf_op jit(solution)/shard_map/ppermute | solution.py:133
  10.0 0.5 collective-permute-start.1
  10.5 0.5 collective-permute-start
  11.0 1.5 %multiply_reduce_fusion = f32[128]{0:T(128)S(1)} fusion(bf16[128,4096]{1,0:T(8,128)(2,1)} %param.4), kind=kLoop, calls=%fused_computation.12 | loop fusion | flops 1572736 | bytes 1049088 | tf_op jit(solution)/shard_map/reduce_sum | solution.py:148
  12.7 12.6 %all-gather.1 = f32[4,1,4224]{2,1,0:T(1,128)S(1)} all-gather(f32[1,1,4224]{2,1,0:T(1,128)S(1)} %reshape.67), channel_id=2, replica_groups=mesh['fsdp'=8,'tp'=4] {'tp'}, dimensions={0}, use_global_device_ids=true | all-gather | bytes 84480 | tf_op jit(solution)/shard_map/all_gather | solution.py:149
  26.1 1.0 shard_map.67
  27.1 3.3 %collective-permute-start.3 = (bf16[32,4224]{1,0:T(8,128)(2,1)S(1)}, bf16[32,4224]{1,0:T(8,128)(2,1)S(1)}, u32[]{:S(2)}, u32[]{:S(2)}) collective-permute-start(bf16[32,4224]{1,0:T(8,128)(2,1)S(1)} %get-tuple-element.45), channel_id=1, source_target_pairs={{0,8},{4,12},{8,0},{12,4},{16,24},{20,28},{24,16},{28,20},{1,9},{5... | collective-permute-start | bytes 811016 | tf_op jit(solution)/shard_map/ppermute | solution.py:133
  30.4 2.4 %collective-permute-start.5 = (bf16[32,4224]{1,0:T(8,128)(2,1)S(1)}, bf16[32,4224]{1,0:T(8,128)(2,1)S(1)}, u32[]{:S(2)}, u32[]{:S(2)}) collective-permute-start(bf16[32,4224]{1,0:T(8,128)(2,1)S(1)} %get-tuple-element.47), channel_id=1, source_target_pairs={{0,24},{4,28},{8,16},{12,20},{16,8},{20,12},{24,0},{28,4},{1,25},{... | collective-permute-start | bytes 811016 | tf_op jit(solution)/shard_map/ppermute | solution.py:133
  32.9 0.2 shard_map.68
  33.0 1.3 constant_dynamic-slice_fusion.27
  34.3 7.6 %collective-permute-done.3 = bf16[32,4224]{1,0:T(8,128)(2,1)S(1)} collective-permute-done((bf16[32,4224]{1,0:T(8,128)(2,1)S(1)}, bf16[32,4224]{1,0:T(8,128)(2,1)S(1)}, u32[]{:S(2)}, u32[]{:S(2)}) %collective-permute-start.3) | collective-permute-done | bytes 270368 | tf_op jit(solution)/shard_map/ppermute | solution.py:133
  41.9 10.3 %collective-permute-done.4 = bf16[32,4224]{1,0:T(8,128)(2,1)S(1)} collective-permute-done((bf16[32,4224]{1,0:T(8,128)(2,1)S(1)}, bf16[32,4224]{1,0:T(8,128)(2,1)S(1)}, u32[]{:S(2)}, u32[]{:S(2)}) %collective-permute-start.4) | collective-permute-done | bytes 270368 | tf_op jit(solution)/shard_map/ppermute | solution.py:133
  52.4 0.2 fusion.14
  52.7 0.6 collective-permute-start.8
  53.3 0.7 collective-permute-start.11
  54.0 1.3 multiply_convert_fusion.7.refs_8_
  55.3 1.3 collective-permute-start.19
  56.6 1.3 constant_dynamic-slice_fusion.31
  58.2 1.0 collective-permute-start.10
  59.2 1.1 collective-permute-start.9
  60.2 0.7 fusion.29
  61.0 1.5 %collective-permute-start.18 = (bf16[128,4096]{1,0:T(8,128)(2,1)S(1)}, bf16[128,4096]{1,0:T(8,128)(2,1)S(1)}, u32[]{:S(2)}, u32[]{:S(2)}) collective-permute-start(bf16[128,4096]{1,0:T(8,128)(2,1)S(1)} %collective-permute-done.11), channel_id=1, source_target_pairs={{8,0},{12,4},{16,24},{20,28},{9,1},{13,5},{17,25},{21,29},{10,2},{... | collective-permute-start | bytes 3145736 | tf_op jit(solution)/shard_map/ppermute | solution.py:133
  62.5 0.1 constant_dynamic-slice_fusion.23
  62.6 2.8 %multiply_convert_fusion.4 = (bf16[128,4096]{1,0:T(8,128)(2,1)S(1)}, bf16[128,4096]{1,0:T(8,128)(2,1)S(1)}, bf16[128,4096]{1,0:T(8,128)(2,1)S(1)}) fusion(bf16[32,4096]{1,0:T(8,128)(2,1)S(1)} %get-tuple-element.99, bf16[32,4096]{1,0:T(8,128)(2,1)S(1)} %get-tuple-element.100, bf16[32,4096]{1,0:T(8,128)(2,1)S(1)} %get-tuple-element.101, ...), kind=kLoop, calls=%fused_computation.8 | loop fusion | flops 17301504 | bytes 6309376 | tf_op jit(solution)/shard_map/convert_element_type | solution.py:156
  65.4 17.9 %collective-permute-done.10.refs_2_.refs_6_ = bf16[2,4,32,2048]{3,2,1,0:T(8,128)(2,1)S(1)} collective-permute-done((bf16[2,4,32,2048]{3,2,1,0:T(8,128)(2,1)S(1)}, bf16[2,4,32,2048]{3,2,1,0:T(8,128)(2,1)S(1)}, u32[]{:S(2)}, u32[]{:S(2)}) %collective-permute-start.10) | collective-permute-done | bytes 1048608 | tf_op jit(solution)/shard_map/ppermute | solution.py:133
  83.3 0.7 collective-permute-done.9.refs_1_.refs_5_
  84.0 3.0 %collective-permute-done.19 = bf16[128,4096]{1,0:T(8,128)(2,1)S(1)} collective-permute-done((bf16[128,4096]{1,0:T(8,128)(2,1)}, bf16[128,4096]{1,0:T(8,128)(2,1)S(1)}, u32[]{:S(2)}, u32[]{:S(2)}) %collective-permute-start.19) | collective-permute-done | bytes 1048608 | tf_op jit(solution)/shard_map/ppermute | solution.py:133
  87.0 0.1 broadcast_select_fusion.1
  87.3 0.7 fusion.31
  88.1 1.0 collective-permute-start.16
  89.1 0.7 fusion.30
  89.8 1.1 collective-permute-start.15
  91.0 11.5 %collective-permute-done.16 = bf16[4,32,2048]{2,1,0:T(8,128)(2,1)S(1)} collective-permute-done((bf16[4,32,2048]{2,1,0:T(8,128)(2,1)S(1)}, bf16[4,32,2048]{2,1,0:T(8,128)(2,1)S(1)}, u32[]{:S(2)}, u32[]{:S(2)}) %collective-permute-start.16) | collective-permute-done | bytes 524320 | tf_op jit(solution)/shard_map/ppermute | solution.py:133
  102.5 0.4 fusion.7
  103.2 0.7 collective-permute-done.15
  103.9 0.4 fusion.4
  104.4 0.6 multiply_convert_fusion.2
  105.0 4.8 %collective-permute-done.18 = bf16[128,4096]{1,0:T(8,128)(2,1)S(1)} collective-permute-done((bf16[128,4096]{1,0:T(8,128)(2,1)S(1)}, bf16[128,4096]{1,0:T(8,128)(2,1)S(1)}, u32[]{:S(2)}, u32[]{:S(2)}) %collective-permute-start.18) | collective-permute-done | bytes 1048608 | tf_op jit(solution)/shard_map/ppermute | solution.py:133
  109.8 0.1 broadcast_select_fusion
  110.3 0.2 bitcast_add_fusion
  110.6 2.3 %collective-permute-start.24 = (f32[128,512]{1,0:T(8,128)S(1)}, f32[128,512]{1,0:T(8,128)S(1)}, u32[]{:S(2)}, u32[]{:S(2)}) collective-permute-start(f32[128,512]{1,0:T(8,128)S(1)} %get-tuple-element.79), channel_id=1, source_target_pairs={{0,24},{4,28},{8,16},{12,20},{16,8},{20,12},{24,0},{28,4},{1,25},{... | collective-permute-start | bytes 786440 | tf_op jit(solution)/shard_map/ppermute | solution.py:133
  113.0 2.1 %collective-permute-start.22 = (f32[128,512]{1,0:T(8,128)S(1)}, f32[128,512]{1,0:T(8,128)S(1)}, u32[]{:S(2)}, u32[]{:S(2)}) collective-permute-start(f32[128,512]{1,0:T(8,128)S(1)} %get-tuple-element.81), channel_id=1, source_target_pairs={{0,8},{4,12},{8,0},{12,4},{16,24},{20,28},{24,16},{28,20},{1,9},{5... | collective-permute-start | bytes 786440 | tf_op jit(solution)/shard_map/ppermute | solution.py:133
  115.2 0.6 multiply_convert_fusion
  115.8 21.9 %shard_map.69 = f32[2048,4096]{1,0:T(8,128)} custom-call(bf16[2,4,32,2048]{3,2,1,0:T(8,128)(2,1)S(1)} %pad_maximum_fusion.refs_0_.refs_4_, bf16[2,4,32,2048]{3,2,1,0:T(8,128)(2,1)S(1)} %collective-permute-done.9.refs_1_.refs_5_, bf16[2,4,32,2048]{3,2,1,0:T(8,128)(2,1)S(1)} %collective-permute-done.10.refs_2_.refs_6_, bf16[1,4,32,2048]{3,2,1,0:T(8,128)(2,1)S(1)} %bitcast.113, ...), custom_call_target="tpu_custom_call" | custom-call | flops 17179869184 | bytes 33554432 | tf_op jit(solution)/shard_map/pallas_call | solution.py:45
  137.8 0.7 fusion.27
  (76 shorter events, 2.6 us)
Async XLA Ops:
  0.6 12.0 %copy-start.2 = (bf16[4096]{0:T(1024)(128)(2,1)S(1)}, bf16[4096]{0:T(1024)(128)(2,1)}, u32[]{:S(2)}) copy-start(bf16[4096]{0:T(1024)(128)(2,1)} %param.5) | copy-start | bytes 24580
  0.6 29.8 %collective-permute-start.6 = (bf16[128,4096]{1,0:T(8,128)(2,1)}, bf16[128,4096]{1,0:T(8,128)(2,1)}, u32[]{:S(2)}, u32[]{:S(2)}) collective-permute-start(bf16[128,4096]{1,0:T(8,128)(2,1)} %param.4), channel_id=1, source_target_pairs={{0,8},{4,12},{8,0},{12,4},{16,24},{20,28},{24,16},{28,20},{1,9},{5... | collective-permute-start | bytes 3145736 | tf_op jit(solution)/shard_map/ppermute | solution.py:133
  3.7 29.1 %collective-permute-start.7 = (bf16[128,4096]{1,0:T(8,128)(2,1)}, bf16[128,4096]{1,0:T(8,128)(2,1)}, u32[]{:S(2)}, u32[]{:S(2)}) collective-permute-start(bf16[128,4096]{1,0:T(8,128)(2,1)} %param.4), channel_id=1, source_target_pairs={{8,16},{12,20},{16,8},{20,12},{9,17},{13,21},{17,9},{21,13},{10,18... | collective-permute-start | bytes 3145736 | tf_op jit(solution)/shard_map/ppermute | solution.py:133
  5.4 27.5 %copy-start = (bf16[2048,256]{1,0:T(8,128)(2,1)S(1)}, bf16[2048,256]{1,0:T(8,128)(2,1)}, u32[]{:S(2)}) copy-start(bf16[2048,256]{1,0:T(8,128)(2,1)} %left) | copy-start | bytes 3145732
  5.4 27.5 %copy-start.1 = (bf16[2048,256]{1,0:T(8,128)(2,1)S(1)}, bf16[2048,256]{1,0:T(8,128)(2,1)}, u32[]{:S(2)}) copy-start(bf16[2048,256]{1,0:T(8,128)(2,1)} %right) | copy-start | bytes 3145732
  7.6 17.9 %collective-permute-start.2 = (bf16[32,4096]{1,0:T(8,128)(2,1)S(1)}, bf16[32,4096]{1,0:T(8,128)(2,1)S(1)}, u32[]{:S(2)}, u32[]{:S(2)}) collective-permute-start(bf16[32,4096]{1,0:T(8,128)(2,1)S(1)} %get-tuple-element.110), channel_id=1, source_target_pairs={{0,3},{1,2},{2,1},{3,0},{4,7},{5,6},{6,5},{7,4},{8,11},{9,10},{10,... | collective-permute-start | bytes 786440 | tf_op jit(solution)/shard_map/ppermute | solution.py:133
  10.0 15.5 %collective-permute-start.1 = (bf16[32,4096]{1,0:T(8,128)(2,1)}, bf16[32,4096]{1,0:T(8,128)(2,1)S(1)}, u32[]{:S(2)}, u32[]{:S(2)}) collective-permute-start(bf16[32,4096]{1,0:T(8,128)(2,1)} %get-tuple-element.111), channel_id=1, source_target_pairs={{0,2},{1,3},{2,0},{3,1},{4,6},{5,7},{6,4},{7,5},{8,10},{9,11},{10,... | collective-permute-start | bytes 786440 | tf_op jit(solution)/shard_map/ppermute | solution.py:133
  10.5 15.0 %collective-permute-start = (bf16[32,4096]{1,0:T(8,128)(2,1)}, bf16[32,4096]{1,0:T(8,128)(2,1)S(1)}, u32[]{:S(2)}, u32[]{:S(2)}) collective-permute-start(bf16[32,4096]{1,0:T(8,128)(2,1)} %get-tuple-element.112), channel_id=1, source_target_pairs={{0,1},{1,0},{2,3},{3,2},{4,5},{5,4},{6,7},{7,6},{8,9},{9,8},{10,11... | collective-permute-start | bytes 786440 | tf_op jit(solution)/shard_map/ppermute | solution.py:133
  25.5 29.8 %collective-permute-start.12 = (bf16[128,4096]{1,0:T(8,128)(2,1)}, bf16[128,4096]{1,0:T(8,128)(2,1)}, u32[]{:S(2)}, u32[]{:S(2)}) collective-permute-start(bf16[128,4096]{1,0:T(8,128)(2,1)} %param.4), channel_id=1, source_target_pairs={{0,4},{4,0},{8,12},{12,8},{16,20},{20,16},{24,28},{28,24},{1,5},{5... | collective-permute-start | bytes 3145736 | tf_op jit(solution)/shard_map/ppermute | solution.py:133
  27.1 14.8 %collective-permute-start.3 = (bf16[32,4224]{1,0:T(8,128)(2,1)S(1)}, bf16[32,4224]{1,0:T(8,128)(2,1)S(1)}, u32[]{:S(2)}, u32[]{:S(2)}) collective-permute-start(bf16[32,4224]{1,0:T(8,128)(2,1)S(1)} %get-tuple-element.45), channel_id=1, source_target_pairs={{0,8},{4,12},{8,0},{12,4},{16,24},{20,28},{24,16},{28,20},{1,9},{5... | collective-permute-start | bytes 811016 | tf_op jit(solution)/shard_map/ppermute | solution.py:133
  30.4 21.9 %collective-permute-start.4 = (bf16[32,4224]{1,0:T(8,128)(2,1)S(1)}, bf16[32,4224]{1,0:T(8,128)(2,1)S(1)}, u32[]{:S(2)}, u32[]{:S(2)}) collective-permute-start(bf16[32,4224]{1,0:T(8,128)(2,1)S(1)} %get-tuple-element.46), channel_id=1, source_target_pairs={{0,16},{4,20},{8,24},{12,28},{16,0},{20,4},{24,8},{28,12},{1,17},{... | collective-permute-start | bytes 811016 | tf_op jit(solution)/shard_map/ppermute | solution.py:133
  30.4 21.9 %collective-permute-start.5 = (bf16[32,4224]{1,0:T(8,128)(2,1)S(1)}, bf16[32,4224]{1,0:T(8,128)(2,1)S(1)}, u32[]{:S(2)}, u32[]{:S(2)}) collective-permute-start(bf16[32,4224]{1,0:T(8,128)(2,1)S(1)} %get-tuple-element.47), channel_id=1, source_target_pairs={{0,24},{4,28},{8,16},{12,20},{16,8},{20,12},{24,0},{28,4},{1,25},{... | collective-permute-start | bytes 811016 | tf_op jit(solution)/shard_map/ppermute | solution.py:133
  32.8 29.6 %collective-permute-start.14 = (bf16[128,4096]{1,0:T(8,128)(2,1)}, bf16[128,4096]{1,0:T(8,128)(2,1)S(1)}, u32[]{:S(2)}, u32[]{:S(2)}) collective-permute-start(bf16[128,4096]{1,0:T(8,128)(2,1)} %collective-permute-done.6), channel_id=1, source_target_pairs={{0,4},{4,0},{8,12},{12,8},{16,20},{20,16},{24,28},{28,24},{1,5},{5... | collective-permute-start | bytes 3145736 | tf_op jit(solution)/shard_map/ppermute | solution.py:133
  52.6 5.4 %collective-permute-start.13 = (f32[4,128]{1,0:T(4,128)S(1)}, f32[4,128]{1,0:T(4,128)S(1)}, u32[]{:S(2)}, u32[]{:S(2)}) collective-permute-start(f32[4,128]{1,0:T(4,128)S(1)} %pad_maximum_fusion.7), channel_id=1, source_target_pairs={{0,4},{4,0},{8,12},{12,8},{16,20},{20,16},{24,28},{28,24},{1,5},{5... | collective-permute-start | bytes 6152 | tf_op jit(solution)/shard_map/ppermute | solution.py:133
  52.7 5.3 %collective-permute-start.8 = (bf16[4,32,2048]{2,1,0:T(8,128)(2,1)S(1)}, bf16[4,32,2048]{2,1,0:T(8,128)(2,1)S(1)}, u32[]{:S(2)}, u32[]{:S(2)}) collective-permute-start(bf16[4,32,2048]{2,1,0:T(8,128)(2,1)S(1)} %pad_maximum_fusion.3), channel_id=1, source_target_pairs={{0,4},{4,0},{8,12},{12,8},{16,20},{20,16},{24,28},{28,24},{1,5},{5... | collective-permute-start | bytes 1572872 | tf_op jit(solution)/shard_map/ppermute | solution.py:133
  53.3 7.7 %collective-permute-start.11 = (bf16[128,4096]{1,0:T(8,128)(2,1)}, bf16[128,4096]{1,0:T(8,128)(2,1)S(1)}, u32[]{:S(2)}, u32[]{:S(2)}) collective-permute-start(bf16[128,4096]{1,0:T(8,128)(2,1)} %collective-permute-done.6), channel_id=1, source_target_pairs={{8,16},{12,20},{16,8},{20,12},{9,17},{13,21},{17,9},{21,13},{10,18... | collective-permute-start | bytes 3145736 | tf_op jit(solution)/shard_map/ppermute | solution.py:133
  55.3 31.6 %collective-permute-start.19 = (bf16[128,4096]{1,0:T(8,128)(2,1)}, bf16[128,4096]{1,0:T(8,128)(2,1)S(1)}, u32[]{:S(2)}, u32[]{:S(2)}) collective-permute-start(bf16[128,4096]{1,0:T(8,128)(2,1)} %collective-permute-done.7), channel_id=1, source_target_pairs={{8,0},{12,4},{16,24},{20,28},{9,1},{13,5},{17,25},{21,29},{10,2},{... | collective-permute-start | bytes 3145736 | tf_op jit(solution)/shard_map/ppermute | solution.py:133
  58.2 25.2 %collective-permute-start.10 = (bf16[2,4,32,2048]{3,2,1,0:T(8,128)(2,1)S(1)}, bf16[2,4,32,2048]{3,2,1,0:T(8,128)(2,1)S(1)}, u32[]{:S(2)}, u32[]{:S(2)}) collective-permute-start(bf16[2,4,32,2048]{3,2,1,0:T(8,128)(2,1)S(1)} %pad_maximum_fusion.refs_0_.refs_4_), channel_id=1, source_target_pairs={{0,2},{1,3},{2,0},{3,1},{4,6},{5,7},{6,4},{7,5},{8,10},{9,11},{10,... | collective-permute-start | bytes 3145736 | tf_op jit(solution)/shard_map/ppermute | solution.py:133
  59.2 24.8 %collective-permute-start.9 = (bf16[2,4,32,2048]{3,2,1,0:T(8,128)(2,1)S(1)}, bf16[2,4,32,2048]{3,2,1,0:T(8,128)(2,1)S(1)}, u32[]{:S(2)}, u32[]{:S(2)}) collective-permute-start(bf16[2,4,32,2048]{3,2,1,0:T(8,128)(2,1)S(1)} %pad_maximum_fusion.refs_0_.refs_4_), channel_id=1, source_target_pairs={{0,1},{1,0},{2,3},{3,2},{4,5},{5,4},{6,7},{7,6},{8,9},{9,8},{10,11... | collective-permute-start | bytes 3145736 | tf_op jit(solution)/shard_map/ppermute | solution.py:133
  61.0 48.8 %collective-permute-start.18 = (bf16[128,4096]{1,0:T(8,128)(2,1)S(1)}, bf16[128,4096]{1,0:T(8,128)(2,1)S(1)}, u32[]{:S(2)}, u32[]{:S(2)}) collective-permute-start(bf16[128,4096]{1,0:T(8,128)(2,1)S(1)} %collective-permute-done.11), channel_id=1, source_target_pairs={{8,0},{12,4},{16,24},{20,28},{9,1},{13,5},{17,25},{21,29},{10,2},{... | collective-permute-start | bytes 3145736 | tf_op jit(solution)/shard_map/ppermute | solution.py:133
  87.2 17.1 %collective-permute-start.20 = (bf16[128,4096]{1,0:T(8,128)(2,1)S(1)}, bf16[128,4096]{1,0:T(8,128)(2,1)S(1)}, u32[]{:S(2)}, u32[]{:S(2)}) collective-permute-start(bf16[128,4096]{1,0:T(8,128)(2,1)S(1)} %broadcast_select_fusion.1), channel_id=1, source_target_pairs={{0,4},{4,0},{8,12},{12,8},{16,20},{20,16},{24,28},{28,24},{1,5},{5... | collective-permute-start | bytes 3145736 | tf_op jit(solution)/shard_map/ppermute | solution.py:133
  88.1 14.4 %collective-permute-start.16 = (bf16[4,32,2048]{2,1,0:T(8,128)(2,1)S(1)}, bf16[4,32,2048]{2,1,0:T(8,128)(2,1)S(1)}, u32[]{:S(2)}, u32[]{:S(2)}) collective-permute-start(bf16[4,32,2048]{2,1,0:T(8,128)(2,1)S(1)} %slice_bitcast_fusion), channel_id=1, source_target_pairs={{0,2},{1,3},{2,0},{3,1},{4,6},{5,7},{6,4},{7,5},{8,10},{9,11},{10,... | collective-permute-start | bytes 1572872 | tf_op jit(solution)/shard_map/ppermute | solution.py:133
  89.8 14.1 %collective-permute-start.15 = (bf16[4,32,2048]{2,1,0:T(8,128)(2,1)S(1)}, bf16[4,32,2048]{2,1,0:T(8,128)(2,1)S(1)}, u32[]{:S(2)}, u32[]{:S(2)}) collective-permute-start(bf16[4,32,2048]{2,1,0:T(8,128)(2,1)S(1)} %slice_bitcast_fusion.1), channel_id=1, source_target_pairs={{0,1},{1,0},{2,3},{3,2},{4,5},{5,4},{6,7},{7,6},{8,9},{9,8},{10,11... | collective-permute-start | bytes 1572872 | tf_op jit(solution)/shard_map/ppermute | solution.py:133
  103.1 7.2 %collective-permute-start.17 = (f32[4,128,512]{2,1,0:T(8,128)S(1)}, f32[4,128,512]{2,1,0:T(8,128)S(1)}, u32[]{:S(2)}, u32[]{:S(2)}) collective-permute-start(f32[4,128,512]{2,1,0:T(8,128)S(1)} %bitcast.118), channel_id=1, source_target_pairs={{0,4},{4,0},{8,12},{12,8},{16,20},{20,16},{24,28},{28,24},{1,5},{5... | collective-permute-start | bytes 3145736 | tf_op jit(solution)/shard_map/ppermute | solution.py:133
  110.0 5.1 %collective-permute-start.21 = (bf16[128,4096]{1,0:T(8,128)(2,1)S(1)}, bf16[128,4096]{1,0:T(8,128)(2,1)S(1)}, u32[]{:S(2)}, u32[]{:S(2)}) collective-permute-start(bf16[128,4096]{1,0:T(8,128)(2,1)S(1)} %broadcast_select_fusion), channel_id=1, source_target_pairs={{0,4},{4,0},{8,12},{12,8},{16,20},{20,16},{24,28},{28,24},{1,5},{5... | collective-permute-start | bytes 3145736 | tf_op jit(solution)/shard_map/ppermute | solution.py:133
  110.6 27.0 %collective-permute-start.24 = (f32[128,512]{1,0:T(8,128)S(1)}, f32[128,512]{1,0:T(8,128)S(1)}, u32[]{:S(2)}, u32[]{:S(2)}) collective-permute-start(f32[128,512]{1,0:T(8,128)S(1)} %get-tuple-element.79), channel_id=1, source_target_pairs={{0,24},{4,28},{8,16},{12,20},{16,8},{20,12},{24,0},{28,4},{1,25},{... | collective-permute-start | bytes 786440 | tf_op jit(solution)/shard_map/ppermute | solution.py:133
  113.0 24.7 %collective-permute-start.23 = (f32[128,512]{1,0:T(8,128)S(1)}, f32[128,512]{1,0:T(8,128)S(1)}, u32[]{:S(2)}, u32[]{:S(2)}) collective-permute-start(f32[128,512]{1,0:T(8,128)S(1)} %get-tuple-element.80), channel_id=1, source_target_pairs={{0,16},{4,20},{8,24},{12,28},{16,0},{20,4},{24,8},{28,12},{1,17},{... | collective-permute-start | bytes 786440 | tf_op jit(solution)/shard_map/ppermute | solution.py:133
  113.0 24.7 %collective-permute-start.22 = (f32[128,512]{1,0:T(8,128)S(1)}, f32[128,512]{1,0:T(8,128)S(1)}, u32[]{:S(2)}, u32[]{:S(2)}) collective-permute-start(f32[128,512]{1,0:T(8,128)S(1)} %get-tuple-element.81), channel_id=1, source_target_pairs={{0,8},{4,12},{8,0},{12,4},{16,24},{20,28},{24,16},{28,20},{1,9},{5... | collective-permute-start | bytes 786440 | tf_op jit(solution)/shard_map/ppermute | solution.py:133

commit v6 on v5

--- a/solution.py
+++ b/solution.py
@@ -119,6 +119,30 @@
     )
 
 
+def halves_kernel(core, *refs):
+    blocks, mine, leaving = refs[:4], refs[4], refs[5]
+    half = mine.shape[2]
+    kept = pl.multiple_of(core[0] * half, 128)
+    given = pl.multiple_of((1 - core[0]) * half, 128)
+    for j, block in enumerate(blocks):
+        mine[j] = block[:, pl.ds(kept, half)]
+        leaving[j] = block[:, pl.ds(given, half)]
+
+
+def halves_apart(core, blocks, half):
+    block = pl.BlockSpec(blocks[0].shape, lambda: (0, 0))
+    shape = (len(blocks), blocks[0].shape[0], half)
+    out = pl.BlockSpec(shape, lambda: (0, 0, 0))
+    return pl.pallas_call(
+        halves_kernel,
+        in_specs=[pl.BlockSpec(memory_space=pltpu.SMEM)] + [block] * len(blocks),
+        out_specs=[out] * 2,
+        out_shape=[jax.ShapeDtypeStruct(shape, blocks[0].dtype)] * 2,
+        compiler_params=pltpu.CompilerParams(vmem_limit_bytes=16 << 20),
+        cost_estimate=pl.CostEstimate(flops=0, bytes_accessed=2_000_000, transcendentals=0),
+    )(core, *blocks)
+
+
 def slice_body(tokens, norm_gain, key_weight, value_weight):
     count, width = tokens.shape
     features = width * 4
@@ -175,12 +199,8 @@
     )
     weights = side_by_side(key_weight, value_weight)
     *landed, weights = lax.optimization_barrier((*landed, weights))
-    def share(which):
-        return jnp.stack(
-            [lax.dynamic_slice_in_dim(block, which * half, half, axis=1) for block in landed]
-        )
-
-    group = jnp.stack([share(core), move(share(1 - core), CORES)])
+    mine, leaving = halves_apart(core[None], landed, half)
+    group = jnp.stack([mine, move(leaving, CORES)])
     from_x = move(group, SIDES[1], "tp")
     from_y = move(group, SIDES[2], "tp")
     last = move(beyond, OUTWARD)

time: 139 us -> 139 us (level)
  transfers between devices with their start and end apart: 25 -> 25, of which waited for: 8 -> 8; matrix products, arithmetic and copies ran while one was open for 13% -> 12% of each run, Pallas kernels for 17% -> 17%
where the time goes in v6:
time: 139 us; the launch traced here: 138 us
  waiting for transfers between devices  56.8 us (41%)
  starting transfers between devices  26.8 us (19%)
  Pallas kernels  23.2 us (17%)
  blocking collectives  12.6 us (9%)
  other arithmetic  8.1 us (6%)
  local copies, waits for them, and re-layouts  6.8 us (5%)
  matrix products  2.98 us (2%)
    ppermute x25, waiting for transfers between devices, move(): return lax.ppermute(x, axis, pairs)  56.8 us
    ppermute x25, starting transfers between devices, move(): return lax.ppermute(x, axis, pairs)  26.8 us
    pallas_call x1, Pallas kernels, hessian_tile(): pl.pallas_call(functools.partial(tile_kernel, scale, len(rows)), grid=(he...  21.9 us
    all_gather x1, blocking collectives, slice_body(): notes = lax.all_gather(note, 'tp')  12.6 us
    dynamic_slice x10, local copies, waits for them, and re-layouts, reorder(): lax.dynamic_slice_in_dim(x, (t ^ k) * quarter, quarter)  5.33 us
    convert_element_type x4, other arithmetic, norm(): return (block.astype(jnp.float32) * gain * scale).astype(jnp.bfloat16)  5.23 us
    dot_general x5, matrix products, project(): product = jnp.dot(flat, weights, preferred_element_type=jnp.float32)  2.98 us
  transfers between devices with their start and end apart: 25, of which 8 were waited for; matrix products, arithmetic and copies ran while one was open for 12% of the time, Pallas kernels for 17%

profile of v6, /device:TPU:0, one launch (start us, length us, event | category | flops | bytes accessed | tf_op | source)
XLA Modules:
  0.0 138.4 jit_solution(1541829407737347269)
XLA Ops:
  0.6 3.1 %collective-permute-start.6 = (bf16[128,4096]{1,0:T(8,128)(2,1)}, bf16[128,4096]{1,0:T(8,128)(2,1)}, u32[]{:S(2)}, u32[]{:S(2)}) collective-permute-start(bf16[128,4096]{1,0:T(8,128)(2,1)} %param.4), channel_id=1, source_target_pairs={{0,8},{4,12},{8,0},{12,4},{16,24},{20,28},{24,16},{28,20},{1,9},{5... | collective-permute-start | bytes 3145736 | tf_op jit(solution)/shard_map/ppermute | solution.py:157
  3.7 1.6 %collective-permute-start.7 = (bf16[128,4096]{1,0:T(8,128)(2,1)}, bf16[128,4096]{1,0:T(8,128)(2,1)}, u32[]{:S(2)}, u32[]{:S(2)}) collective-permute-start(bf16[128,4096]{1,0:T(8,128)(2,1)} %param.4), channel_id=1, source_target_pairs={{8,16},{12,20},{16,8},{20,12},{9,17},{13,21},{17,9},{21,13},{10,18... | collective-permute-start | bytes 3145736 | tf_op jit(solution)/shard_map/ppermute | solution.py:157
  5.4 2.2 %constant_dynamic-slice_fusion.32 = (bf16[32,4096]{1,0:T(8,128)(2,1)S(1)}, bf16[32,4096]{1,0:T(8,128)(2,1)}, bf16[32,4096]{1,0:T(8,128)(2,1)}, bf16[32,4096]{1,0:T(8,128)(2,1)S(1)}) fusion(bf16[128,4096]{1,0:T(8,128)(2,1)} %param.4, s32[]{:T(128)S(6)} %select_n.112, s32[]{:T(128)S(6)} %select_n.111, s32[]{:T(128)S(6)} %select_n.110, s32[]{:T(128)S(6)} %select_n.109), kind=kLoop, calls=%fused_computation.89 | loop fusion | bytes 2097168 | tf_op jit(solution)/shard_map/dynamic_slice | solution.py:161
  7.6 2.4 %collective-permute-start.2 = (bf16[32,4096]{1,0:T(8,128)(2,1)S(1)}, bf16[32,4096]{1,0:T(8,128)(2,1)S(1)}, u32[]{:S(2)}, u32[]{:S(2)}) collective-permute-start(bf16[32,4096]{1,0:T(8,128)(2,1)S(1)} %get-tuple-element.114), channel_id=1, source_target_pairs={{0,3},{1,2},{2,1},{3,0},{4,7},{5,6},{6,5},{7,4},{8,11},{9,10},{10,... | collective-permute-start | bytes 786440 | tf_op jit(solution)/shard_map/ppermute | solution.py:157
  10.0 0.5 collective-permute-start.1
  10.5 0.5 collective-permute-start
  11.1 1.5 %multiply_reduce_fusion = f32[128]{0:T(128)S(1)} fusion(bf16[128,4096]{1,0:T(8,128)(2,1)} %param.4), kind=kLoop, calls=%fused_computation.12 | loop fusion | flops 1572736 | bytes 1049088 | tf_op jit(solution)/shard_map/reduce_sum | solution.py:172
  12.7 12.6 %all-gather.1 = f32[4,1,4224]{2,1,0:T(1,128)S(1)} all-gather(f32[1,1,4224]{2,1,0:T(1,128)S(1)} %reshape.67), channel_id=2, replica_groups=mesh['fsdp'=8,'tp'=4] {'tp'}, dimensions={0}, use_global_device_ids=true | all-gather | bytes 84480 | tf_op jit(solution)/shard_map/all_gather | solution.py:173
  26.1 1.0 shard_map.67
  27.1 3.3 %collective-permute-start.3 = (bf16[32,4224]{1,0:T(8,128)(2,1)S(1)}, bf16[32,4224]{1,0:T(8,128)(2,1)S(1)}, u32[]{:S(2)}, u32[]{:S(2)}) collective-permute-start(bf16[32,4224]{1,0:T(8,128)(2,1)S(1)} %get-tuple-element.47), channel_id=1, source_target_pairs={{0,8},{4,12},{8,0},{12,4},{16,24},{20,28},{24,16},{28,20},{1,9},{5... | collective-permute-start | bytes 811016 | tf_op jit(solution)/shard_map/ppermute | solution.py:157
  30.4 2.4 %collective-permute-start.5 = (bf16[32,4224]{1,0:T(8,128)(2,1)S(1)}, bf16[32,4224]{1,0:T(8,128)(2,1)S(1)}, u32[]{:S(2)}, u32[]{:S(2)}) collective-permute-start(bf16[32,4224]{1,0:T(8,128)(2,1)S(1)} %get-tuple-element.49), channel_id=1, source_target_pairs={{0,24},{4,28},{8,16},{12,20},{16,8},{20,12},{24,0},{28,4},{1,25},{... | collective-permute-start | bytes 811016 | tf_op jit(solution)/shard_map/ppermute | solution.py:157
  32.9 0.2 shard_map.68
  33.0 1.3 constant_dynamic-slice_fusion.27
  34.3 7.6 %collective-permute-done.3.refs_1_ = bf16[32,4224]{1,0:T(8,128)(2,1)S(1)} collective-permute-done((bf16[32,4224]{1,0:T(8,128)(2,1)S(1)}, bf16[32,4224]{1,0:T(8,128)(2,1)S(1)}, u32[]{:S(2)}, u32[]{:S(2)}) %collective-permute-start.3) | collective-permute-done | bytes 270368 | tf_op jit(solution)/shard_map/ppermute | solution.py:157
  41.9 10.3 %collective-permute-done.4.refs_2_ = bf16[32,4224]{1,0:T(8,128)(2,1)S(1)} collective-permute-done((bf16[32,4224]{1,0:T(8,128)(2,1)S(1)}, bf16[32,4224]{1,0:T(8,128)(2,1)S(1)}, u32[]{:S(2)}, u32[]{:S(2)}) %collective-permute-start.4) | collective-permute-done | bytes 270368 | tf_op jit(solution)/shard_map/ppermute | solution.py:157
  52.4 0.2 fusion.14
  52.6 0.5 collective-permute-start.8
  53.1 0.7 collective-permute-start.11
  53.8 1.3 multiply_convert_fusion.7.refs_8_
  55.2 1.3 collective-permute-start.19
  56.5 1.3 constant_dynamic-slice_fusion.31
  57.9 1.0 collective-permute-start.10
  58.9 1.1 collective-permute-start.9
  60.0 0.7 fusion.29
  60.8 1.5 %collective-permute-start.18 = (bf16[128,4096]{1,0:T(8,128)(2,1)S(1)}, bf16[128,4096]{1,0:T(8,128)(2,1)S(1)}, u32[]{:S(2)}, u32[]{:S(2)}) collective-permute-start(bf16[128,4096]{1,0:T(8,128)(2,1)S(1)} %collective-permute-done.11), channel_id=1, source_target_pairs={{8,0},{12,4},{16,24},{20,28},{9,1},{13,5},{17,25},{21,29},{10,2},{... | collective-permute-start | bytes 3145736 | tf_op jit(solution)/shard_map/ppermute | solution.py:157
  62.2 0.1 constant_dynamic-slice_fusion.23
  62.4 2.8 %multiply_convert_fusion.4 = (bf16[128,4096]{1,0:T(8,128)(2,1)S(1)}, bf16[128,4096]{1,0:T(8,128)(2,1)S(1)}, bf16[128,4096]{1,0:T(8,128)(2,1)S(1)}) fusion(bf16[32,4096]{1,0:T(8,128)(2,1)S(1)} %get-tuple-element.103, bf16[32,4096]{1,0:T(8,128)(2,1)S(1)} %get-tuple-element.104, bf16[32,4096]{1,0:T(8,128)(2,1)S(1)} %get-tuple-element.105, ...), kind=kLoop, calls=%fused_computation.8 | loop fusion | flops 17301504 | bytes 6309376 | tf_op jit(solution)/shard_map/convert_element_type | solution.py:180
  65.1 18.0 %collective-permute-done.10.refs_2_.refs_6_ = bf16[2,4,32,2048]{3,2,1,0:T(8,128)(2,1)S(1)} collective-permute-done((bf16[2,4,32,2048]{3,2,1,0:T(8,128)(2,1)S(1)}, bf16[2,4,32,2048]{3,2,1,0:T(8,128)(2,1)S(1)}, u32[]{:S(2)}, u32[]{:S(2)}) %collective-permute-start.10) | collective-permute-done | bytes 1048608 | tf_op jit(solution)/shard_map/ppermute | solution.py:157
  83.1 0.7 collective-permute-done.9.refs_1_.refs_5_
  83.8 3.1 %collective-permute-done.19 = bf16[128,4096]{1,0:T(8,128)(2,1)S(1)} collective-permute-done((bf16[128,4096]{1,0:T(8,128)(2,1)}, bf16[128,4096]{1,0:T(8,128)(2,1)S(1)}, u32[]{:S(2)}, u32[]{:S(2)}) %collective-permute-start.19) | collective-permute-done | bytes 1048608 | tf_op jit(solution)/shard_map/ppermute | solution.py:157
  86.9 0.1 broadcast_select_fusion.1
  87.2 0.7 fusion.31
  87.9 1.0 collective-permute-start.16
  89.0 0.7 fusion.30
  89.7 1.1 collective-permute-start.15
  90.9 11.5 %collective-permute-done.16 = bf16[4,32,2048]{2,1,0:T(8,128)(2,1)S(1)} collective-permute-done((bf16[4,32,2048]{2,1,0:T(8,128)(2,1)S(1)}, bf16[4,32,2048]{2,1,0:T(8,128)(2,1)S(1)}, u32[]{:S(2)}, u32[]{:S(2)}) %collective-permute-start.16) | collective-permute-done | bytes 524320 | tf_op jit(solution)/shard_map/ppermute | solution.py:157
  102.3 0.4 fusion.7
  103.1 0.7 collective-permute-done.15
  103.8 0.4 fusion.4
  104.3 0.6 multiply_convert_fusion.2
  104.9 4.9 %collective-permute-done.18 = bf16[128,4096]{1,0:T(8,128)(2,1)S(1)} collective-permute-done((bf16[128,4096]{1,0:T(8,128)(2,1)S(1)}, bf16[128,4096]{1,0:T(8,128)(2,1)S(1)}, u32[]{:S(2)}, u32[]{:S(2)}) %collective-permute-start.18) | collective-permute-done | bytes 1048608 | tf_op jit(solution)/shard_map/ppermute | solution.py:157
  109.8 0.1 broadcast_select_fusion
  110.3 0.2 bitcast_add_fusion
  110.6 2.3 %collective-permute-start.24 = (f32[128,512]{1,0:T(8,128)S(1)}, f32[128,512]{1,0:T(8,128)S(1)}, u32[]{:S(2)}, u32[]{:S(2)}) collective-permute-start(f32[128,512]{1,0:T(8,128)S(1)} %get-tuple-element.83), channel_id=1, source_target_pairs={{0,24},{4,28},{8,16},{12,20},{16,8},{20,12},{24,0},{28,4},{1,25},{... | collective-permute-start | bytes 786440 | tf_op jit(solution)/shard_map/ppermute | solution.py:157
  112.9 2.2 %collective-permute-start.22 = (f32[128,512]{1,0:T(8,128)S(1)}, f32[128,512]{1,0:T(8,128)S(1)}, u32[]{:S(2)}, u32[]{:S(2)}) collective-permute-start(f32[128,512]{1,0:T(8,128)S(1)} %get-tuple-element.85), channel_id=1, source_target_pairs={{0,8},{4,12},{8,0},{12,4},{16,24},{20,28},{24,16},{28,20},{1,9},{5... | collective-permute-start | bytes 786440 | tf_op jit(solution)/shard_map/ppermute | solution.py:157
  115.1 0.6 multiply_convert_fusion
  115.7 21.9 %shard_map.70 = f32[2048,4096]{1,0:T(8,128)} custom-call(bf16[2,4,32,2048]{3,2,1,0:T(8,128)(2,1)S(1)} %pad_maximum_fusion.refs_0_.refs_4_, bf16[2,4,32,2048]{3,2,1,0:T(8,128)(2,1)S(1)} %collective-permute-done.9.refs_1_.refs_5_, bf16[2,4,32,2048]{3,2,1,0:T(8,128)(2,1)S(1)} %collective-permute-done.10.refs_2_.refs_6_, bf16[1,4,32,2048]{3,2,1,0:T(8,128)(2,1)S(1)} %bitcast.97, ...), custom_call_target="tpu_custom_call" | custom-call | flops 17179869184 | bytes 33554432 | tf_op jit(solution)/shard_map/pallas_call | solution.py:45
  137.8 0.7 fusion.27
  (73 shorter events, 2.4 us)
Async XLA Ops:
  0.6 12.0 %copy-start.2 = (bf16[4096]{0:T(1024)(128)(2,1)S(1)}, bf16[4096]{0:T(1024)(128)(2,1)}, u32[]{:S(2)}) copy-start(bf16[4096]{0:T(1024)(128)(2,1)} %param.5) | copy-start | bytes 24580
  0.6 29.8 %collective-permute-start.6 = (bf16[128,4096]{1,0:T(8,128)(2,1)}, bf16[128,4096]{1,0:T(8,128)(2,1)}, u32[]{:S(2)}, u32[]{:S(2)}) collective-permute-start(bf16[128,4096]{1,0:T(8,128)(2,1)} %param.4), channel_id=1, source_target_pairs={{0,8},{4,12},{8,0},{12,4},{16,24},{20,28},{24,16},{28,20},{1,9},{5... | collective-permute-start | bytes 3145736 | tf_op jit(solution)/shard_map/ppermute | solution.py:157
  3.7 29.1 %collective-permute-start.7 = (bf16[128,4096]{1,0:T(8,128)(2,1)}, bf16[128,4096]{1,0:T(8,128)(2,1)}, u32[]{:S(2)}, u32[]{:S(2)}) collective-permute-start(bf16[128,4096]{1,0:T(8,128)(2,1)} %param.4), channel_id=1, source_target_pairs={{8,16},{12,20},{16,8},{20,12},{9,17},{13,21},{17,9},{21,13},{10,18... | collective-permute-start | bytes 3145736 | tf_op jit(solution)/shard_map/ppermute | solution.py:157
  5.4 27.5 %copy-start = (bf16[2048,256]{1,0:T(8,128)(2,1)S(1)}, bf16[2048,256]{1,0:T(8,128)(2,1)}, u32[]{:S(2)}) copy-start(bf16[2048,256]{1,0:T(8,128)(2,1)} %left) | copy-start | bytes 3145732
  5.4 27.5 %copy-start.1 = (bf16[2048,256]{1,0:T(8,128)(2,1)S(1)}, bf16[2048,256]{1,0:T(8,128)(2,1)}, u32[]{:S(2)}) copy-start(bf16[2048,256]{1,0:T(8,128)(2,1)} %right) | copy-start | bytes 3145732
  7.6 17.9 %collective-permute-start.2 = (bf16[32,4096]{1,0:T(8,128)(2,1)S(1)}, bf16[32,4096]{1,0:T(8,128)(2,1)S(1)}, u32[]{:S(2)}, u32[]{:S(2)}) collective-permute-start(bf16[32,4096]{1,0:T(8,128)(2,1)S(1)} %get-tuple-element.114), channel_id=1, source_target_pairs={{0,3},{1,2},{2,1},{3,0},{4,7},{5,6},{6,5},{7,4},{8,11},{9,10},{10,... | collective-permute-start | bytes 786440 | tf_op jit(solution)/shard_map/ppermute | solution.py:157
  10.0 15.5 %collective-permute-start.1 = (bf16[32,4096]{1,0:T(8,128)(2,1)}, bf16[32,4096]{1,0:T(8,128)(2,1)S(1)}, u32[]{:S(2)}, u32[]{:S(2)}) collective-permute-start(bf16[32,4096]{1,0:T(8,128)(2,1)} %get-tuple-element.115), channel_id=1, source_target_pairs={{0,2},{1,3},{2,0},{3,1},{4,6},{5,7},{6,4},{7,5},{8,10},{9,11},{10,... | collective-permute-start | bytes 786440 | tf_op jit(solution)/shard_map/ppermute | solution.py:157
  10.5 15.0 %collective-permute-start = (bf16[32,4096]{1,0:T(8,128)(2,1)}, bf16[32,4096]{1,0:T(8,128)(2,1)S(1)}, u32[]{:S(2)}, u32[]{:S(2)}) collective-permute-start(bf16[32,4096]{1,0:T(8,128)(2,1)} %get-tuple-element.116), channel_id=1, source_target_pairs={{0,1},{1,0},{2,3},{3,2},{4,5},{5,4},{6,7},{7,6},{8,9},{9,8},{10,11... | collective-permute-start | bytes 786440 | tf_op jit(solution)/shard_map/ppermute | solution.py:157
  25.5 29.7 %collective-permute-start.12 = (bf16[128,4096]{1,0:T(8,128)(2,1)}, bf16[128,4096]{1,0:T(8,128)(2,1)}, u32[]{:S(2)}, u32[]{:S(2)}) collective-permute-start(bf16[128,4096]{1,0:T(8,128)(2,1)} %param.4), channel_id=1, source_target_pairs={{0,4},{4,0},{8,12},{12,8},{16,20},{20,16},{24,28},{28,24},{1,5},{5... | collective-permute-start | bytes 3145736 | tf_op jit(solution)/shard_map/ppermute | solution.py:157
  27.1 14.8 %collective-permute-start.3 = (bf16[32,4224]{1,0:T(8,128)(2,1)S(1)}, bf16[32,4224]{1,0:T(8,128)(2,1)S(1)}, u32[]{:S(2)}, u32[]{:S(2)}) collective-permute-start(bf16[32,4224]{1,0:T(8,128)(2,1)S(1)} %get-tuple-element.47), channel_id=1, source_target_pairs={{0,8},{4,12},{8,0},{12,4},{16,24},{20,28},{24,16},{28,20},{1,9},{5... | collective-permute-start | bytes 811016 | tf_op jit(solution)/shard_map/ppermute | solution.py:157
  30.4 21.9 %collective-permute-start.4 = (bf16[32,4224]{1,0:T(8,128)(2,1)S(1)}, bf16[32,4224]{1,0:T(8,128)(2,1)S(1)}, u32[]{:S(2)}, u32[]{:S(2)}) collective-permute-start(bf16[32,4224]{1,0:T(8,128)(2,1)S(1)} %get-tuple-element.48), channel_id=1, source_target_pairs={{0,16},{4,20},{8,24},{12,28},{16,0},{20,4},{24,8},{28,12},{1,17},{... | collective-permute-start | bytes 811016 | tf_op jit(solution)/shard_map/ppermute | solution.py:157
  30.4 21.9 %collective-permute-start.5 = (bf16[32,4224]{1,0:T(8,128)(2,1)S(1)}, bf16[32,4224]{1,0:T(8,128)(2,1)S(1)}, u32[]{:S(2)}, u32[]{:S(2)}) collective-permute-start(bf16[32,4224]{1,0:T(8,128)(2,1)S(1)} %get-tuple-element.49), channel_id=1, source_target_pairs={{0,24},{4,28},{8,16},{12,20},{16,8},{20,12},{24,0},{28,4},{1,25},{... | collective-permute-start | bytes 811016 | tf_op jit(solution)/shard_map/ppermute | solution.py:157
  32.8 29.4 %collective-permute-start.14 = (bf16[128,4096]{1,0:T(8,128)(2,1)}, bf16[128,4096]{1,0:T(8,128)(2,1)S(1)}, u32[]{:S(2)}, u32[]{:S(2)}) collective-permute-start(bf16[128,4096]{1,0:T(8,128)(2,1)} %collective-permute-done.6), channel_id=1, source_target_pairs={{0,4},{4,0},{8,12},{12,8},{16,20},{20,16},{24,28},{28,24},{1,5},{5... | collective-permute-start | bytes 3145736 | tf_op jit(solution)/shard_map/ppermute | solution.py:157
  52.6 5.2 %collective-permute-start.13 = (f32[4,128]{1,0:T(4,128)S(1)}, f32[4,128]{1,0:T(4,128)S(1)}, u32[]{:S(2)}, u32[]{:S(2)}) collective-permute-start(f32[4,128]{1,0:T(4,128)S(1)} %pad_maximum_fusion.6), channel_id=1, source_target_pairs={{0,4},{4,0},{8,12},{12,8},{16,20},{20,16},{24,28},{28,24},{1,5},{5... | collective-permute-start | bytes 6152 | tf_op jit(solution)/shard_map/ppermute | solution.py:157
  52.6 5.2 %collective-permute-start.8 = (bf16[4,32,2048]{2,1,0:T(8,128)(2,1)S(1)}, bf16[4,32,2048]{2,1,0:T(8,128)(2,1)S(1)}, u32[]{:S(2)}, u32[]{:S(2)}) collective-permute-start(bf16[4,32,2048]{2,1,0:T(8,128)(2,1)S(1)} %get-tuple-element.57), channel_id=1, source_target_pairs={{0,4},{4,0},{8,12},{12,8},{16,20},{20,16},{24,28},{28,24},{1,5},{5... | collective-permute-start | bytes 1572872 | tf_op jit(solution)/shard_map/ppermute | solution.py:157
  53.1 7.6 %collective-permute-start.11 = (bf16[128,4096]{1,0:T(8,128)(2,1)}, bf16[128,4096]{1,0:T(8,128)(2,1)S(1)}, u32[]{:S(2)}, u32[]{:S(2)}) collective-permute-start(bf16[128,4096]{1,0:T(8,128)(2,1)} %collective-permute-done.6), channel_id=1, source_target_pairs={{8,16},{12,20},{16,8},{20,12},{9,17},{13,21},{17,9},{21,13},{10,18... | collective-permute-start | bytes 3145736 | tf_op jit(solution)/shard_map/ppermute | solution.py:157
  55.2 31.7 %collective-permute-start.19 = (bf16[128,4096]{1,0:T(8,128)(2,1)}, bf16[128,4096]{1,0:T(8,128)(2,1)S(1)}, u32[]{:S(2)}, u32[]{:S(2)}) collective-permute-start(bf16[128,4096]{1,0:T(8,128)(2,1)} %collective-permute-done.7), channel_id=1, source_target_pairs={{8,0},{12,4},{16,24},{20,28},{9,1},{13,5},{17,25},{21,29},{10,2},{... | collective-permute-start | bytes 3145736 | tf_op jit(solution)/shard_map/ppermute | solution.py:157
  57.9 25.2 %collective-permute-start.10 = (bf16[2,4,32,2048]{3,2,1,0:T(8,128)(2,1)S(1)}, bf16[2,4,32,2048]{3,2,1,0:T(8,128)(2,1)S(1)}, u32[]{:S(2)}, u32[]{:S(2)}) collective-permute-start(bf16[2,4,32,2048]{3,2,1,0:T(8,128)(2,1)S(1)} %pad_maximum_fusion.refs_0_.refs_4_), channel_id=1, source_target_pairs={{0,2},{1,3},{2,0},{3,1},{4,6},{5,7},{6,4},{7,5},{8,10},{9,11},{10,... | collective-permute-start | bytes 3145736 | tf_op jit(solution)/shard_map/ppermute | solution.py:157
  58.9 24.9 %collective-permute-start.9 = (bf16[2,4,32,2048]{3,2,1,0:T(8,128)(2,1)S(1)}, bf16[2,4,32,2048]{3,2,1,0:T(8,128)(2,1)S(1)}, u32[]{:S(2)}, u32[]{:S(2)}) collective-permute-start(bf16[2,4,32,2048]{3,2,1,0:T(8,128)(2,1)S(1)} %pad_maximum_fusion.refs_0_.refs_4_), channel_id=1, source_target_pairs={{0,1},{1,0},{2,3},{3,2},{4,5},{5,4},{6,7},{7,6},{8,9},{9,8},{10,11... | collective-permute-start | bytes 3145736 | tf_op jit(solution)/shard_map/ppermute | solution.py:157
  60.8 49.0 %collective-permute-start.18 = (bf16[128,4096]{1,0:T(8,128)(2,1)S(1)}, bf16[128,4096]{1,0:T(8,128)(2,1)S(1)}, u32[]{:S(2)}, u32[]{:S(2)}) collective-permute-start(bf16[128,4096]{1,0:T(8,128)(2,1)S(1)} %collective-permute-done.11), channel_id=1, source_target_pairs={{8,0},{12,4},{16,24},{20,28},{9,1},{13,5},{17,25},{21,29},{10,2},{... | collective-permute-start | bytes 3145736 | tf_op jit(solution)/shard_map/ppermute | solution.py:157
  87.1 17.1 %collective-permute-start.20 = (bf16[128,4096]{1,0:T(8,128)(2,1)S(1)}, bf16[128,4096]{1,0:T(8,128)(2,1)S(1)}, u32[]{:S(2)}, u32[]{:S(2)}) collective-permute-start(bf16[128,4096]{1,0:T(8,128)(2,1)S(1)} %broadcast_select_fusion.1), channel_id=1, source_target_pairs={{0,4},{4,0},{8,12},{12,8},{16,20},{20,16},{24,28},{28,24},{1,5},{5... | collective-permute-start | bytes 3145736 | tf_op jit(solution)/shard_map/ppermute | solution.py:157
  87.9 14.4 %collective-permute-start.16 = (bf16[4,32,2048]{2,1,0:T(8,128)(2,1)S(1)}, bf16[4,32,2048]{2,1,0:T(8,128)(2,1)S(1)}, u32[]{:S(2)}, u32[]{:S(2)}) collective-permute-start(bf16[4,32,2048]{2,1,0:T(8,128)(2,1)S(1)} %slice_bitcast_fusion), channel_id=1, source_target_pairs={{0,2},{1,3},{2,0},{3,1},{4,6},{5,7},{6,4},{7,5},{8,10},{9,11},{10,... | collective-permute-start | bytes 1572872 | tf_op jit(solution)/shard_map/ppermute | solution.py:157
  89.7 14.1 %collective-permute-start.15 = (bf16[4,32,2048]{2,1,0:T(8,128)(2,1)S(1)}, bf16[4,32,2048]{2,1,0:T(8,128)(2,1)S(1)}, u32[]{:S(2)}, u32[]{:S(2)}) collective-permute-start(bf16[4,32,2048]{2,1,0:T(8,128)(2,1)S(1)} %slice_bitcast_fusion.1), channel_id=1, source_target_pairs={{0,1},{1,0},{2,3},{3,2},{4,5},{5,4},{6,7},{7,6},{8,9},{9,8},{10,11... | collective-permute-start | bytes 1572872 | tf_op jit(solution)/shard_map/ppermute | solution.py:157
  103.0 7.3 %collective-permute-start.17 = (f32[4,128,512]{2,1,0:T(8,128)S(1)}, f32[4,128,512]{2,1,0:T(8,128)S(1)}, u32[]{:S(2)}, u32[]{:S(2)}) collective-permute-start(f32[4,128,512]{2,1,0:T(8,128)S(1)} %bitcast.103), channel_id=1, source_target_pairs={{0,4},{4,0},{8,12},{12,8},{16,20},{20,16},{24,28},{28,24},{1,5},{5... | collective-permute-start | bytes 3145736 | tf_op jit(solution)/shard_map/ppermute | solution.py:157
  109.9 5.1 %collective-permute-start.21 = (bf16[128,4096]{1,0:T(8,128)(2,1)S(1)}, bf16[128,4096]{1,0:T(8,128)(2,1)S(1)}, u32[]{:S(2)}, u32[]{:S(2)}) collective-permute-start(bf16[128,4096]{1,0:T(8,128)(2,1)S(1)} %broadcast_select_fusion), channel_id=1, source_target_pairs={{0,4},{4,0},{8,12},{12,8},{16,20},{20,16},{24,28},{28,24},{1,5},{5... | collective-permute-start | bytes 3145736 | tf_op jit(solution)/shard_map/ppermute | solution.py:157
  110.6 27.0 %collective-permute-start.24 = (f32[128,512]{1,0:T(8,128)S(1)}, f32[128,512]{1,0:T(8,128)S(1)}, u32[]{:S(2)}, u32[]{:S(2)}) collective-permute-start(f32[128,512]{1,0:T(8,128)S(1)} %get-tuple-element.83), channel_id=1, source_target_pairs={{0,24},{4,28},{8,16},{12,20},{16,8},{20,12},{24,0},{28,4},{1,25},{... | collective-permute-start | bytes 786440 | tf_op jit(solution)/shard_map/ppermute | solution.py:157
  112.8 24.8 %collective-permute-start.23 = (f32[128,512]{1,0:T(8,128)S(1)}, f32[128,512]{1,0:T(8,128)S(1)}, u32[]{:S(2)}, u32[]{:S(2)}) collective-permute-start(f32[128,512]{1,0:T(8,128)S(1)} %get-tuple-element.84), channel_id=1, source_target_pairs={{0,16},{4,20},{8,24},{12,28},{16,0},{20,4},{24,8},{28,12},{1,17},{... | collective-permute-start | bytes 786440 | tf_op jit(solution)/shard_map/ppermute | solution.py:157
  112.9 24.8 %collective-permute-start.22 = (f32[128,512]{1,0:T(8,128)S(1)}, f32[128,512]{1,0:T(8,128)S(1)}, u32[]{:S(2)}, u32[]{:S(2)}) collective-permute-start(f32[128,512]{1,0:T(8,128)S(1)} %get-tuple-element.85), channel_id=1, source_target_pairs={{0,8},{4,12},{8,0},{12,4},{16,24},{20,28},{24,16},{28,20},{1,9},{5... | collective-permute-start | bytes 786440 | tf_op jit(solution)/shard_map/ppermute | solution.py:157
